TPU v7x, 32 devices: a whole 2x2x4 slice. The times are simulated.
32 devices in a mesh: ctx: 8 (over z, y), head: 4 (over x, core).
Axes of the slice: x: 2, y: 2, z: 4, core: 2. Of those that a mesh axis runs over, the one named last changes fastest.
Arguments:
- queries: bfloat16 [2048, 2048], P('ctx', 'head'), may hold values from -32 to 32
- keys: bfloat16 [2048, 1024], P('ctx', 'head'), may hold values from -32 to 32
- values: bfloat16 [2048, 1024], P('ctx', 'head'), may hold values from -6 to 6
- doc_ids: int32 [16], replicated, may hold values from 0 to 2, as said below
- out_weight: bfloat16 [2048, 5376], P('head'), may hold values from -1 to 1
Outputs:
- projected: bfloat16 [2048, 5376], P(('ctx', 'head'))
Inputs may be any that keep to these rules, and one draw needn't show every extreme that they name: doc_ids is non-decreasing along the sequence and starts at 0; the first document spans exactly 12 blocks, every other one 1 or more blocks.
All inputs are finite; a program needn't handle non-finite values.
Results may differ from a plain program's by a relative error of at most 0.015.
Values may be sent and summed in bfloat16 or wider, within the bound.
No kernel may reach another device: no remote copies, remote signals or barrier semaphores. Data moves between devices by JAX's collectives and lax.ppermute only.
A program may use at most 64 MiB of HBM per device.

v0:
```python
import functools

import jax
import jax.numpy as jnp
from jax import lax
from jax.experimental import pallas as pl
from jax.experimental.pallas import tpu as pltpu
from jax.sharding import PartitionSpec as P

HEAD_SIZE = 128
BLOCK = 128
SCALE = 168.0 ** (-0.5)
LOG2E = 1.4426950408889634
NEG = -1e30
VMEM = pl.BlockSpec(memory_space=pltpu.VMEM)
SMEM = pl.BlockSpec(memory_space=pltpu.SMEM)
HBM = pl.BlockSpec(memory_space=pltpu.HBM)
LIMIT = pltpu.CompilerParams(vmem_limit_bytes=32 * 1024 * 1024)


def hop(block, axis, pairs):
    return lax.ppermute(block, axis, pairs)


def in_place(number, position, n_ctx):
    away = {2: 2, 3: 4, 4: 2, 5: 4}[number]
    return (position < n_ctx * 3 // 4) & (position >= away)


BESIDE = ((0, 1), (2, 3), (4, 5), (6, 7))
BY_TWO = ((0, 2, 4), (1, 3, 5))
AGAIN = ((2, 4), (3, 5))


def move(block, rings):
    n_ctx, heads = lax.axis_size("ctx"), lax.axis_size("head")
    target = {ring[i]: ring[(i + 1) % len(ring)] for ring in rings for i in range(len(ring))}
    pairs = [
        (i * heads + h, target[i] * heads + h if i in target else i * heads + (h ^ 1))
        for i in range(n_ctx)
        for h in range(heads)
    ]
    return lax.ppermute(block, ("ctx", "head"), pairs)


def after(x, event):
    return lax.optimization_barrier((x, event))[0]


def score_blocks(doors, q, a, h, chunks, numbers):
    position = lax.axis_index("ctx")
    n_ctx = lax.axis_size("ctx")
    n_query = chunks[0][0].shape[0]
    scores = []
    for (keys, _), c in zip(chunks, numbers):
        count = (a + 1) * BLOCK if c == 0 else n_query
        k = keys[:count, h * HEAD_SIZE : (h + 1) * HEAD_SIZE]
        s = lax.dot_general(q, k, (((1,), (1,)), ((), ())), preferred_element_type=jnp.float32)
        for b in range(count // BLOCK):
            part = s[:, b * BLOCK : (b + 1) * BLOCK]
            if c == 0 and b == a:
                row = lax.broadcasted_iota(jnp.int32, part.shape, 0) % BLOCK
                col = lax.broadcasted_iota(jnp.int32, part.shape, 1)
                part = jnp.where(row >= col, part, NEG)
            elif c < 2:
                part = part + doors(c, a, b)
            else:
                part = part + jnp.where(in_place(c, position, n_ctx), 0.0, NEG)
            scores.append(part)
    return scores


def weigh(scores, peak, factor, a, h, chunks, numbers):
    n_query = chunks[0][0].shape[0]
    total = added = None
    scores = list(scores)
    for (_, values), c in zip(chunks, numbers):
        count = (a + 1) * BLOCK if c == 0 else n_query
        parts = []
        for b in range(count // BLOCK):
            w = jnp.exp2(scores.pop(0) * factor - peak)
            total = w if total is None else total + w
            parts.append(w.astype(jnp.bfloat16))
        w = jnp.concatenate(parts, axis=1) if len(parts) > 1 else parts[0]
        v = values[:count, h * HEAD_SIZE : (h + 1) * HEAD_SIZE]
        term = jnp.dot(w, v, preferred_element_type=jnp.float32)
        added = term if added is None else added + term
    return total, added


def head_slices(queries, keys, h):
    group = queries.shape[1] // keys.shape[1]
    return [slice((h * group + g) * HEAD_SIZE, (h * group + g + 1) * HEAD_SIZE) for g in range(group)]


def absorb(numbers, doors, queries, chunks, before, after):
    n_query = queries.shape[0]
    factor = SCALE * LOG2E
    parts = []
    for a in range(n_query // BLOCK):
        for h in range(chunks[0][0].shape[1] // HEAD_SIZE):
            heads = head_slices(queries, chunks[0][0], h)
            size = len(heads) * BLOCK
            parts.append((a, h, heads, slice(len(parts) * size, (len(parts) + 1) * size)))
    scores = []
    for a, h, heads, _ in parts:
        q = jnp.concatenate([queries[a * BLOCK : (a + 1) * BLOCK, s] for s in heads], axis=0)
        scores.append(score_blocks(doors, q, a, h, chunks, numbers))
    peaks = [functools.reduce(jnp.maximum, s) for s in scores]
    peaks = [jnp.max(peak, axis=1, keepdims=True) * factor for peak in peaks]
    shrinks = None
    if before is None:
        peaks = [jnp.broadcast_to(peak, (peak.shape[0], HEAD_SIZE)) for peak in peaks]
    else:
        lasts = [before[0][rows, :] for _, _, _, rows in parts]
        peaks = [jnp.maximum(last, peak) for last, peak in zip(lasts, peaks)]
        shrinks = [jnp.exp2(last - peak) for last, peak in zip(lasts, peaks)]
    sums = [
        weigh(s, peak, factor, a, h, chunks, numbers)
        for s, peak, (a, h, _, _) in zip(scores, peaks, parts)
    ]
    for i, (a, h, heads, rows) in enumerate(parts):
        total, added = sums[i]
        if before is not None:
            total = total + before[1][rows, :] * shrinks[i]
            added = added + before[2][rows, :] * shrinks[i]
        sums[i] = (total, added)
    after(parts, peaks, sums)


def store_state(state):
    def after(parts, peaks, sums):
        for (_, _, _, rows), peak, (total, added) in zip(parts, peaks, sums):
            for ref, part in zip(state, (peak, total, added)):
                ref[rows, :] = part

    return after


def pairs_of(refs):
    return list(zip(refs[0::2], refs[1::2]))


def first_kernel(docs_in, queries_in, keys_in, values_in, *refs):
    *state, queries, open_beside, docs, keys, values, sems = refs
    places = ((docs_in, docs), (queries_in, queries), (keys_in, keys), (values_in, values))
    fetches = [pltpu.make_async_copy(a, b, sems.at[i]) for i, (a, b) in enumerate(places)]
    for fetch in fetches:
        fetch.start()
    for fetch in fetches:
        fetch.wait()
    position = lax.axis_index("ctx")
    q_blocks = queries.shape[0] // BLOCK

    def doors(number, a, b):
        source = position if number == 0 else jnp.maximum(position - 1, 0)
        seen = docs[source * q_blocks + b] == docs[position * q_blocks + a]
        if number == 1:
            seen = seen & (position % 2 == 1)
        return jnp.where(seen, 0.0, NEG)

    for a in range(q_blocks):
        for b in range(q_blocks):
            part = open_beside.at[a * 8 : (a + 1) * 8, b * BLOCK : (b + 1) * BLOCK]
            part[...] = jnp.full(part.shape, doors(1, a, b), jnp.float32)
    absorb((0,), doors, queries, [(keys, values)], None, store_state(state))


def next_kernel(numbers, queries, open_beside, weight_in, *refs):
    *refs, weight, sem = refs
    fetch = pltpu.make_async_copy(weight_in, weight, sem)
    fetch.start()
    pairs = 2 * len(numbers)

    def doors(number, a, b):
        return open_beside[a * 8 : a * 8 + 1, b * BLOCK : (b + 1) * BLOCK]

    absorb(numbers, doors, queries, pairs_of(refs[3 : 3 + pairs]), refs[:3], store_state(refs[3 + pairs :]))
    fetch.wait()


def attend_cost(queries, numbers, fetched=0):
    n_query, width = queries.shape
    count = len(numbers) * n_query
    return pl.CostEstimate(
        flops=4 * n_query * width * count,
        bytes_accessed=fetched,
        transcendentals=n_query * count * width // HEAD_SIZE,
    )


def state_shapes(queries):
    rows = queries.size // HEAD_SIZE
    return (pltpu.VMEM((rows, HEAD_SIZE), jnp.float32),) * 3


def attend_first(docs, queries, keys, values):
    n_query = queries.shape[0]
    return pl.pallas_call(
        first_kernel,
        out_shape=state_shapes(queries)
        + (
            pltpu.VMEM(queries.shape, queries.dtype),
            pltpu.VMEM((8 * n_query // BLOCK, n_query), jnp.float32),
        ),
        in_specs=[HBM] * 4,
        out_specs=(VMEM,) * 5,
        scratch_shapes=[
            pltpu.SMEM(docs.shape, docs.dtype),
            pltpu.VMEM(keys.shape, keys.dtype),
            pltpu.VMEM(values.shape, values.dtype),
            pltpu.SemaphoreType.DMA((4,)),
        ],
        compiler_params=LIMIT,
        cost_estimate=attend_cost(queries, (0,)),
        name="attend_first",
    )(*[pltpu.with_memory_space_constraint(x, pltpu.HBM) for x in (docs, queries, keys, values)])


def attend_next(queries, open_beside, weight, state, chunks, numbers):
    return pl.pallas_call(
        functools.partial(next_kernel, numbers),
        out_shape=state_shapes(queries) + (pltpu.VMEM(weight.shape, weight.dtype),),
        in_specs=[VMEM, VMEM, HBM] + [VMEM] * (3 + 2 * len(chunks)),
        out_specs=(VMEM,) * 4,
        scratch_shapes=[pltpu.SemaphoreType.DMA],
        compiler_params=LIMIT,
        cost_estimate=attend_cost(queries, numbers, 2 * weight.size),
        name="attend_next",
    )(
        queries,
        open_beside,
        pltpu.with_memory_space_constraint(weight, pltpu.HBM),
        *state,
        *[x for pair in chunks for x in pair],
    )


def last_kernel(numbers, columns, queries, weight, *refs):
    pairs = 2 * len(numbers)
    chunks = pairs_of(refs[3 : 3 + pairs])
    far, near, mine, send, attended = refs[3 + pairs :]

    def after(parts, peaks, sums):
        inverses = [1.0 / jnp.sum(total, axis=1, keepdims=True) for total, _ in sums]
        for (a, _, heads, _), inverse, (_, added) in zip(parts, inverses, sums):
            result = (added * inverse).astype(jnp.bfloat16)
            for g, head in enumerate(heads):
                attended[a * BLOCK : (a + 1) * BLOCK, head] = result[g * BLOCK : (g + 1) * BLOCK]

    absorb(numbers, None, queries, chunks, refs[:3], after)
    place = lax.axis_index("head")
    share = queries.shape[0] // 4
    for half, owners in ((far, (place ^ 2, place ^ 3)), (near, (place, place ^ 1))):
        for i, owner in enumerate(owners):
            source = pl.ds(pl.multiple_of(owner * share, share), share)
            half[i * share : (i + 1) * share, :] = attended[source, :]
    project_columns(far, weight, mine, (send,), *columns)


def attend_last(queries, weight, state, chunks, numbers, columns):
    n_query, width = queries.shape
    half = jax.ShapeDtypeStruct((n_query // 2, width), jnp.bfloat16)
    return pl.pallas_call(
        functools.partial(last_kernel, numbers, columns),
        out_shape=(half, half) + project_shapes(n_query // 4, columns[1] - columns[0]),
        in_specs=[VMEM] * (5 + 2 * len(numbers)),
        out_specs=(VMEM,) * 4,
        scratch_shapes=[pltpu.VMEM(queries.shape, jnp.bfloat16)],
        compiler_params=LIMIT,
        cost_estimate=attend_cost(queries, numbers),
        name="attend_last",
    )(queries, weight, *state, *[x for pair in chunks for x in pair])


def project_shapes(rows, count, sends=1):
    send = jax.ShapeDtypeStruct((rows, count // sends), jnp.bfloat16)
    return (jax.ShapeDtypeStruct((rows, count), jnp.float32),) + (send,) * sends


def project_columns(rows, weight, mine, sends, start, end):
    share = rows.shape[0] // 2
    width = sends[0].shape[1]
    for i, send in enumerate(sends):
        for at in range(0, width, 768):
            stop = min(at + 768, width)
            columns = weight[:, start + i * width + at : start + i * width + stop]
            product = jnp.dot(rows[...], columns, preferred_element_type=jnp.float32)
            mine[:, i * width + at : i * width + stop] = product[:share]
            send[:, at:stop] = product[share:].astype(send.dtype)


def project_kernel(columns, rows, weight, mine, *sends):
    project_columns(rows, weight, mine, sends, *columns)


def project(rows, weight, columns, sends=1):
    count = columns[1] - columns[0]
    return pl.pallas_call(
        functools.partial(project_kernel, columns),
        out_shape=project_shapes(rows.shape[0] // 2, count, sends),
        in_specs=[VMEM, VMEM],
        out_specs=(VMEM,) * (1 + sends),
        compiler_params=LIMIT,
        cost_estimate=pl.CostEstimate(
            flops=2 * rows.shape[0] * rows.shape[1] * count, bytes_accessed=0, transcendentals=0
        ),
        name="project",
    )(rows, weight)


def add_kernel(mine, theirs, out):
    out[...] = (mine[...] + theirs[...].astype(jnp.float32)).astype(out.dtype)


def add_up(mine, theirs):
    return pl.pallas_call(
        add_kernel,
        out_shape=jax.ShapeDtypeStruct(theirs.shape, theirs.dtype),
        in_specs=[VMEM, VMEM],
        out_specs=VMEM,
        compiler_params=LIMIT,
        cost_estimate=pl.CostEstimate(flops=theirs.size, bytes_accessed=0, transcendentals=0),
        name="add_up",
    )(mine, theirs)


def combine_kernel(at, mine, across, *refs):
    *beside, out, total, sem = refs
    width = across.shape[1]
    left = 0
    for part in beside[: len(beside) - (at > 0)]:
        low, high = max(left, at), min(left + part.shape[1], at + width)
        if low < high:
            piece = mine[:, low:high] + part[:, low - left : high - left].astype(jnp.float32)
            piece += across[:, low - at : high - at].astype(jnp.float32)
            total[:, low - at : high - at] = piece.astype(total.dtype)
        left += part.shape[1]
    copy = pltpu.make_async_copy(total, out.at[:, at : at + width], sem)
    copy.start()
    copy.wait()


def combine(mine, beside, across, at=0, out=None):
    outs = [] if out is None else [out]
    return pl.pallas_call(
        functools.partial(combine_kernel, at),
        out_shape=jax.ShapeDtypeStruct(mine.shape, across.dtype),
        in_specs=[VMEM] * (2 + len(beside)) + [HBM] * len(outs),
        out_specs=HBM,
        scratch_shapes=[pltpu.VMEM(across.shape, across.dtype), pltpu.SemaphoreType.DMA],
        input_output_aliases={2 + len(beside): 0} if outs else {},
        compiler_params=LIMIT,
        name="combine",
    )(mine, across, *beside, *outs)


def from_behind(block, axis, distance):
    devices = range(lax.axis_size(axis))
    route = [(i - distance, i) for i in devices if i - distance in devices]
    return lax.ppermute(block, axis, route)


def token_docs(doc_ids, start, count):
    blocks = (start + jnp.arange(count, dtype=jnp.int32)) // BLOCK
    table = blocks[:, None] == jnp.arange(doc_ids.shape[0], dtype=jnp.int32)[None, :]
    return jnp.sum(jnp.where(table, doc_ids[None, :], 0), axis=1)


def attend(carry, queries, q_docs, q_start, k_piece, v_piece, k_docs, k_start):
    peak, totals, accum = carry
    n_query = queries.shape[0]
    n_key = k_piece.shape[0]
    kv_heads = k_piece.shape[1] // HEAD_SIZE
    query_group = queries.shape[1] // k_piece.shape[1]
    q_heads = queries.reshape(n_query, kv_heads, query_group, HEAD_SIZE)
    k_heads = k_piece.reshape(n_key, kv_heads, HEAD_SIZE)
    v_heads = v_piece.reshape(n_key, kv_heads, HEAD_SIZE)
    scores = (
        jnp.einsum("qkgd,skd->kgqs", q_heads, k_heads, preferred_element_type=jnp.float32) * SCALE
    )
    q_pos = q_start + jnp.arange(n_query, dtype=jnp.int32)
    k_pos = k_start + jnp.arange(n_key, dtype=jnp.int32)
    allowed = (q_docs[:, None] == k_docs[None, :]) & (q_pos[:, None] >= k_pos[None, :])
    scores = jnp.where(allowed, scores, NEG)
    new_peak = jnp.maximum(peak, jnp.max(scores, axis=-1))
    shrink = jnp.exp(peak - new_peak)
    weights = jnp.exp(scores - new_peak[..., None])
    totals = totals * shrink + jnp.sum(weights, axis=-1)
    rounded = weights.astype(jnp.bfloat16)
    added = jnp.einsum("kgqs,skd->kgqd", rounded, v_heads, preferred_element_type=jnp.float32)
    accum = accum * shrink[..., None] + added
    return (new_peak, totals, accum)


def absorb_block(carry, queries, q_docs, q_start, k_piece, v_piece, k_start, doc_ids, flag):
    n_key = k_piece.shape[0]
    k_docs = token_docs(doc_ids, k_start, n_key)
    fresh = attend(carry, queries, q_docs, q_start, k_piece, v_piece, k_docs, k_start)
    return jax.tree.map(lambda new, old: jnp.where(flag, new, old), fresh, carry)


def ring_attention(queries, keys, values, doc_ids, n_ctx, position):
    n_query = queries.shape[0]
    q_start = position * n_query
    q_docs = token_docs(doc_ids, q_start, n_query)
    kv_heads = keys.shape[1] // HEAD_SIZE
    query_group = queries.shape[1] // keys.shape[1]
    carry = (
        jnp.full((kv_heads, query_group, n_query), NEG, jnp.float32),
        jnp.zeros((kv_heads, query_group, n_query), jnp.float32),
        jnp.zeros((kv_heads, query_group, n_query, HEAD_SIZE), jnp.float32),
    )
    always = jnp.array(True)
    carry = absorb_block(carry, queries, q_docs, q_start, keys, values, q_start, doc_ids, always)

    def turn_one(step, state):
        inner_state, moving = state
        moving = from_behind(moving, "ctx", 1)
        start = ((position - step) % n_ctx) * n_query
        inner_state = absorb_block(
            inner_state, queries, q_docs, q_start, moving[0], moving[1], start, doc_ids, always
        )
        return (inner_state, moving)

    _, totals, accum = lax.fori_loop(1, n_ctx, turn_one, (carry, jnp.stack((keys, values))))[0]
    result = accum / totals[..., None]
    return jnp.transpose(result, (2, 0, 1, 3)).reshape(queries.shape).astype(jnp.bfloat16)


def part_rows(attended, place):
    share = attended.shape[0] // 4
    rows = [lax.dynamic_slice_in_dim(attended, (place ^ flip) * share, share, 0) for flip in (2, 3, 0, 1)]
    return jnp.concatenate(rows[:2], axis=0), jnp.concatenate(rows[2:], axis=0)


def per_device(queries, keys, values, doc_ids, out_weight):
    n_ctx = lax.axis_size("ctx")
    heads = lax.axis_size("head")
    position = lax.axis_index("ctx")
    place = lax.axis_index("head")
    other_core = [(i, i ^ 1) for i in range(heads)]
    other_chip = [(i, i ^ 2) for i in range(heads)]
    columns = out_weight.shape[1]
    cut = columns * 4 // 7 // BLOCK * BLOCK

    if n_ctx == 8:
        by_two = [move(x, BY_TWO) for x in (keys, values)]
        beside = [move(x, BESIDE) for x in (keys, values)]
        *state, fetched, open_beside = attend_first(doc_ids, queries, keys, values)
        by_four = [move(after(x, state[0]), AGAIN) for x in by_two]
        swap_two = [move(after(after(x, beside[0]), state[0]), BESIDE) for x in by_two]
        swap_four = [move(after(x, by_four[0]), AGAIN) for x in swap_two]
        chunks = [beside, by_two, by_four]
        *state, weight = attend_next(fetched, open_beside, out_weight, state, chunks, (1, 2, 3))
        chunks = [swap_two, swap_four]
        far, near, mine, send = attend_last(fetched, weight, state, chunks, (4, 5), (0, cut))
    else:
        weight = out_weight
        attended = ring_attention(queries, keys, values, doc_ids, n_ctx, position)
        far, near = part_rows(attended, place)
        mine, send = project(far, weight, (0, cut))
    theirs = hop(send, "head", other_core)
    later_mine, later_send = project(far, weight, (cut, columns))
    mine, later_mine = lax.optimization_barrier((mine, later_mine))
    first_sum = add_up(mine, theirs)
    first_part = hop(first_sum, "head", other_chip)
    later_theirs = hop(later_send, "head", other_core)
    later_mine, first_sum = lax.optimization_barrier((later_mine, first_sum))
    later_sum = add_up(later_mine, later_theirs)
    second_part = hop(later_sum, "head", other_chip)
    near, later_sum = lax.optimization_barrier((near, later_sum))
    mine, *sends = project(near, weight, (0, columns), 3)
    theirs = [hop(send, "head", other_core) for send in sends]
    out = combine(mine, theirs, first_part)
    return combine(mine, theirs, second_part, cut, out)


def solution(mesh):
    placed = (P("ctx", "head"), P("ctx", "head"), P("ctx", "head"), P(), P("head", None))
    return jax.shard_map(
        per_device, mesh=mesh, in_specs=placed, out_specs=P(("ctx", "head"), None), check_vma=False
    )
```

profile of v0, /device:TPU:0, one launch (start us, length us, event | category | flops | bytes accessed | tf_op | source)
XLA Modules:
  0.0 44.7 jit_solution(14680644454711363150)
XLA Ops:
  0.0 3.0 %collective-permute-start.2 = (bf16[256,256]{1,0:T(8,128)(2,1)}, bf16[256,256]{1,0:T(8,128)(2,1)S(1)}, u32[]{:S(2)}, u32[]{:S(2)}) collective-permute-start(bf16[256,256]{1,0:T(8,128)(2,1)} %keys_in.1), channel_id=1, source_target_pairs={{0,8},{1,9},{2,10},{3,11},{4,12},{5,13},{6,14},{7,15},{8,16},{9,17... | collective-permute-start | bytes 393224 | tf_op jit(solution)/shard_map/ppermute | solution.py:43
  3.0 1.5 %collective-permute-start = (bf16[256,256]{1,0:T(8,128)(2,1)}, bf16[256,256]{1,0:T(8,128)(2,1)S(1)}, u32[]{:S(2)}, u32[]{:S(2)}) collective-permute-start(bf16[256,256]{1,0:T(8,128)(2,1)} %keys_in.1), channel_id=1, source_target_pairs={{0,4},{1,5},{2,6},{3,7},{4,0},{5,1},{6,2},{7,3},{8,12},{9,13},{10,... | collective-permute-start | bytes 393224 | tf_op jit(solution)/shard_map/ppermute | solution.py:43
  4.5 1.6 %collective-permute-start.3 = (bf16[256,256]{1,0:T(8,128)(2,1)}, bf16[256,256]{1,0:T(8,128)(2,1)S(1)}, u32[]{:S(2)}, u32[]{:S(2)}) collective-permute-start(bf16[256,256]{1,0:T(8,128)(2,1)} %values_in.1), channel_id=1, source_target_pairs={{0,8},{1,9},{2,10},{3,11},{4,12},{5,13},{6,14},{7,15},{8,16},{9,17... | collective-permute-start | bytes 393224 | tf_op jit(solution)/shard_map/ppermute | solution.py:43
  6.1 1.6 %attend_first.1 = (f32[1024,128]{1,0:T(8,128)S(1)}, f32[1024,128]{1,0:T(8,128)S(1)}, f32[1024,128]{1,0:T(8,128)S(1)}, bf16[256,512]{1,0:T(8,128)(2,1)S(1)}, f32[16,256]{1,0:T(8,128)S(1)}) custom-call(s32[16]{0:T(128)} %docs_in.1, bf16[256,512]{1,0:T(8,128)(2,1)} %queries_in.1, bf16[256,256]{1,0:T(8,128)(2,1)} %keys_in.1, bf16[256,256]{1,0:T(8,128)(2,1)} %values_in.1), custom_call_target="tpu_custom_call" | custom-call | flops 134217728 | tf_op jit(solution)/shard_map/attend_first/pallas_call | solution.py:199
  7.7 0.2 collective-permute-done.2.refs_5_
  7.9 0.3 collective-permute-done.refs_3_
  8.2 2.3 %collective-permute-start.6 = (bf16[256,256]{1,0:T(8,128)(2,1)S(1)}, bf16[256,256]{1,0:T(8,128)(2,1)S(1)}, u32[]{:S(2)}, u32[]{:S(2)}) collective-permute-start(bf16[256,256]{1,0:T(8,128)(2,1)S(1)} %collective-permute-done.2.refs_5_), channel_id=1, source_target_pairs={{0,4},{1,5},{2,6},{3,7},{4,0},{5,1},{6,2},{7,3},{8,12},{9,13},{10,... | collective-permute-start | bytes 393224 | tf_op jit(solution)/shard_map/ppermute | solution.py:43
  10.5 1.3 %collective-permute-done.3.refs_6_ = bf16[256,256]{1,0:T(8,128)(2,1)S(1)} collective-permute-done((bf16[256,256]{1,0:T(8,128)(2,1)}, bf16[256,256]{1,0:T(8,128)(2,1)S(1)}, u32[]{:S(2)}, u32[]{:S(2)}) %collective-permute-start.3) | collective-permute-done | bytes 131104 | tf_op jit(solution)/shard_map/ppermute | solution.py:43
  11.8 1.4 %collective-permute-start.7 = (bf16[256,256]{1,0:T(8,128)(2,1)S(1)}, bf16[256,256]{1,0:T(8,128)(2,1)S(1)}, u32[]{:S(2)}, u32[]{:S(2)}) collective-permute-start(bf16[256,256]{1,0:T(8,128)(2,1)S(1)} %collective-permute-done.3.refs_6_), channel_id=1, source_target_pairs={{0,4},{1,5},{2,6},{3,7},{4,0},{5,1},{6,2},{7,3},{8,12},{9,13},{10,... | collective-permute-start | bytes 393224 | tf_op jit(solution)/shard_map/ppermute | solution.py:43
  13.2 0.6 %collective-permute-start.1 = (bf16[256,256]{1,0:T(8,128)(2,1)}, bf16[256,256]{1,0:T(8,128)(2,1)S(1)}, u32[]{:S(2)}, u32[]{:S(2)}) collective-permute-start(bf16[256,256]{1,0:T(8,128)(2,1)} %values_in.1), channel_id=1, source_target_pairs={{0,4},{1,5},{2,6},{3,7},{4,0},{5,1},{6,2},{7,3},{8,12},{9,13},{10,... | collective-permute-start | bytes 393224 | tf_op jit(solution)/shard_map/ppermute | solution.py:43
  13.8 1.0 %collective-permute-done.6.refs_3_ = bf16[256,256]{1,0:T(8,128)(2,1)S(1)} collective-permute-done((bf16[256,256]{1,0:T(8,128)(2,1)S(1)}, bf16[256,256]{1,0:T(8,128)(2,1)S(1)}, u32[]{:S(2)}, u32[]{:S(2)}) %collective-permute-start.6) | collective-permute-done | bytes 131104 | tf_op jit(solution)/shard_map/ppermute | solution.py:43
  14.8 3.4 %collective-permute-done.7.refs_4_ = bf16[256,256]{1,0:T(8,128)(2,1)S(1)} collective-permute-done((bf16[256,256]{1,0:T(8,128)(2,1)S(1)}, bf16[256,256]{1,0:T(8,128)(2,1)S(1)}, u32[]{:S(2)}, u32[]{:S(2)}) %collective-permute-start.7) | collective-permute-done | bytes 131104 | tf_op jit(solution)/shard_map/ppermute | solution.py:43
  18.2 2.0 %collective-permute-done.1.refs_4_ = bf16[256,256]{1,0:T(8,128)(2,1)S(1)} collective-permute-done((bf16[256,256]{1,0:T(8,128)(2,1)}, bf16[256,256]{1,0:T(8,128)(2,1)S(1)}, u32[]{:S(2)}, u32[]{:S(2)}) %collective-permute-start.1) | collective-permute-done | bytes 131104 | tf_op jit(solution)/shard_map/ppermute | solution.py:43
  20.3 2.6 %attend_next.1 = (f32[1024,128]{1,0:T(8,128)S(1)}, f32[1024,128]{1,0:T(8,128)S(1)}, f32[1024,128]{1,0:T(8,128)S(1)}, bf16[512,5376]{1,0:T(8,128)(2,1)S(1)}) custom-call(bf16[256,512]{1,0:T(8,128)(2,1)S(1)} %get-tuple-element.36.queries, f32[16,256]{1,0:T(8,128)S(1)} %get-tuple-element.37.open_beside, bf16[512,5376]{1,0:T(8,128)(2,1)} %weight_in.1, ...), custom_call_target="tpu_custom_call" | custom-call | flops 402653184 | bytes 5505024 | tf_op jit(solution)/shard_map/attend_next/pallas_call | solution.py:221
  22.9 1.6 %attend_last.1 = (bf16[128,512]{1,0:T(8,128)(2,1)S(1)}, bf16[128,512]{1,0:T(8,128)(2,1)S(1)}, f32[64,3072]{1,0:T(8,128)S(1)}, bf16[64,3072]{1,0:T(8,128)(2,1)S(1)}) custom-call(bf16[256,512]{1,0:T(8,128)(2,1)S(1)} %get-tuple-element.36.queries, bf16[512,5376]{1,0:T(8,128)(2,1)S(1)} %get-tuple-element.43.weight, f32[1024,128]{1,0:T(8,128)S(1)} %get-tuple-element.44.refs_0_, ...), custom_call_target="tpu_custom_call" | custom-call | flops 268435456 | tf_op jit(solution)/shard_map/attend_last/pallas_call | solution.py:264
  24.5 0.1 collective-permute-start.10
  24.6 0.5 %project.2 = (f32[64,2304]{1,0:T(8,128)S(1)}, bf16[64,2304]{1,0:T(8,128)(2,1)S(1)}) custom-call(bf16[128,512]{1,0:T(8,128)(2,1)S(1)} %get-tuple-element.55.rows, bf16[512,5376]{1,0:T(8,128)(2,1)S(1)} %get-tuple-element.43.weight), custom_call_target="tpu_custom_call" | custom-call | flops 301989888 | tf_op jit(solution)/shard_map/project/pallas_call | solution.py:299
  25.1 0.6 %collective-permute-start.11 = (bf16[64,2304]{1,0:T(8,128)(2,1)S(1)}, bf16[64,2304]{1,0:T(8,128)(2,1)S(1)}, u32[]{:S(2)}, u32[]{:S(2)}) collective-permute-start(bf16[64,2304]{1,0:T(8,128)(2,1)S(1)} %get-tuple-element.61), channel_id=1, source_target_pairs={{0,1},{1,0},{2,3},{3,2},{4,5},{5,4},{6,7},{7,6},{8,9},{9,8},{10,11... | collective-permute-start | bytes 884744 | tf_op jit(solution)/shard_map/ppermute | solution.py:22
  25.6 0.7 %collective-permute-done.10.theirs = bf16[64,3072]{1,0:T(8,128)(2,1)S(1)} collective-permute-done((bf16[64,3072]{1,0:T(8,128)(2,1)S(1)}, bf16[64,3072]{1,0:T(8,128)(2,1)S(1)}, u32[]{:S(2)}, u32[]{:S(2)}) %collective-permute-start.10) | collective-permute-done | bytes 393248 | tf_op jit(solution)/shard_map/ppermute | solution.py:22
  26.4 1.6 %collective-permute-start.16 = (bf16[64,3072]{1,0:T(8,128)(2,1)S(1)}, bf16[64,3072]{1,0:T(8,128)(2,1)S(1)}, u32[]{:S(2)}, u32[]{:S(2)}) collective-permute-start(bf16[64,3072]{1,0:T(8,128)(2,1)S(1)} %add_up.2), channel_id=1, source_target_pairs={{0,2},{1,3},{2,0},{3,1},{4,6},{5,7},{6,4},{7,5},{8,10},{9,11},{10,... | collective-permute-start | bytes 1179656 | tf_op jit(solution)/shard_map/ppermute | solution.py:22
  28.0 0.6 %collective-permute-start.12 = (bf16[64,2304]{1,0:T(8,128)(2,1)S(1)}, bf16[64,2304]{1,0:T(8,128)(2,1)S(1)}, u32[]{:S(2)}, u32[]{:S(2)}) collective-permute-start(bf16[64,2304]{1,0:T(8,128)(2,1)S(1)} %add_up.3), channel_id=1, source_target_pairs={{0,2},{1,3},{2,0},{3,1},{4,6},{5,7},{6,4},{7,5},{8,10},{9,11},{10,... | collective-permute-start | bytes 884744 | tf_op jit(solution)/shard_map/ppermute | solution.py:22
  28.6 0.9 %project.3 = (f32[64,5376]{1,0:T(8,128)S(1)}, bf16[64,1792]{1,0:T(8,128)(2,1)S(1)}, bf16[64,1792]{1,0:T(8,128)(2,1)S(1)}, bf16[64,1792]{1,0:T(8,128)(2,1)S(1)}) custom-call(bf16[128,512]{1,0:T(8,128)(2,1)S(1)} %get-tuple-element.62.rows, bf16[512,5376]{1,0:T(8,128)(2,1)S(1)} %get-tuple-element.43.weight), custom_call_target="tpu_custom_call" | custom-call | flops 704643072 | tf_op jit(solution)/shard_map/project/pallas_call | solution.py:299
  29.5 0.1 collective-permute-start.13
  29.5 0.5 %collective-permute-start.14 = (bf16[64,1792]{1,0:T(8,128)(2,1)S(1)}, bf16[64,1792]{1,0:T(8,128)(2,1)S(1)}, u32[]{:S(2)}, u32[]{:S(2)}) collective-permute-start(bf16[64,1792]{1,0:T(8,128)(2,1)S(1)} %get-tuple-element.65), channel_id=1, source_target_pairs={{0,1},{1,0},{2,3},{3,2},{4,5},{5,4},{6,7},{7,6},{8,9},{9,8},{10,11... | collective-permute-start | bytes 688136 | tf_op jit(solution)/shard_map/ppermute | solution.py:22
  30.0 0.1 collective-permute-start.15
  30.1 0.9 %collective-permute-done.13.refs_0_ = bf16[64,1792]{1,0:T(8,128)(2,1)S(1)} collective-permute-done((bf16[64,1792]{1,0:T(8,128)(2,1)S(1)}, bf16[64,1792]{1,0:T(8,128)(2,1)S(1)}, u32[]{:S(2)}, u32[]{:S(2)}) %collective-permute-start.13) | collective-permute-done | bytes 229408 | tf_op jit(solution)/shard_map/ppermute | solution.py:22
  31.0 0.3 collective-permute-done.14.refs_1_
  31.3 0.3 collective-permute-done.15.refs_2_
  31.7 6.7 %collective-permute-done.16.across = bf16[64,3072]{1,0:T(8,128)(2,1)S(1)} collective-permute-done((bf16[64,3072]{1,0:T(8,128)(2,1)S(1)}, bf16[64,3072]{1,0:T(8,128)(2,1)S(1)}, u32[]{:S(2)}, u32[]{:S(2)}) %collective-permute-start.16) | collective-permute-done | bytes 393248 | tf_op jit(solution)/shard_map/ppermute | solution.py:22
  38.4 0.9 %combine.2.refs_3_ = bf16[64,5376]{1,0:T(8,128)(2,1)} custom-call(f32[64,5376]{1,0:T(8,128)S(1)} %get-tuple-element.63.mine, bf16[64,3072]{1,0:T(8,128)(2,1)S(1)} %collective-permute-done.16.across, bf16[64,1792]{1,0:T(8,128)(2,1)S(1)} %collective-permute-done.13.refs_0_, bf16[64,1792]{1,0:T(8,128)(2,1)S(1)} %collective-permute-done.14.refs_1_, ...), custom_call_target="tpu_custom_call" | custom-call | tf_op jit(solution)/shard_map/combine/pallas_call | solution.py:346
  39.3 4.6 %collective-permute-done.12.across = bf16[64,2304]{1,0:T(8,128)(2,1)S(1)} collective-permute-done((bf16[64,2304]{1,0:T(8,128)(2,1)S(1)}, bf16[64,2304]{1,0:T(8,128)(2,1)S(1)}, u32[]{:S(2)}, u32[]{:S(2)}) %collective-permute-start.12) | collective-permute-done | bytes 294944 | tf_op jit(solution)/shard_map/ppermute | solution.py:22
  43.9 0.8 %combine.3 = bf16[64,5376]{1,0:T(8,128)(2,1)} custom-call(f32[64,5376]{1,0:T(8,128)S(1)} %get-tuple-element.63.mine, bf16[64,2304]{1,0:T(8,128)(2,1)S(1)} %collective-permute-done.12.across, bf16[64,1792]{1,0:T(8,128)(2,1)S(1)} %collective-permute-done.13.refs_0_, ...), custom_call_target="tpu_custom_call", output_to_operand_aliasing={{}: (5, {})} | custom-call | tf_op jit(solution)/shard_map/combine/pallas_call | solution.py:346
  (11 shorter events, 0.1 us)
Async XLA Ops:
  0.0 7.9 %collective-permute-start.2 = (bf16[256,256]{1,0:T(8,128)(2,1)}, bf16[256,256]{1,0:T(8,128)(2,1)S(1)}, u32[]{:S(2)}, u32[]{:S(2)}) collective-permute-start(bf16[256,256]{1,0:T(8,128)(2,1)} %keys_in.1), channel_id=1, source_target_pairs={{0,8},{1,9},{2,10},{3,11},{4,12},{5,13},{6,14},{7,15},{8,16},{9,17... | collective-permute-start | bytes 393224 | tf_op jit(solution)/shard_map/ppermute | solution.py:43
  3.0 5.2 %collective-permute-start = (bf16[256,256]{1,0:T(8,128)(2,1)}, bf16[256,256]{1,0:T(8,128)(2,1)S(1)}, u32[]{:S(2)}, u32[]{:S(2)}) collective-permute-start(bf16[256,256]{1,0:T(8,128)(2,1)} %keys_in.1), channel_id=1, source_target_pairs={{0,4},{1,5},{2,6},{3,7},{4,0},{5,1},{6,2},{7,3},{8,12},{9,13},{10,... | collective-permute-start | bytes 393224 | tf_op jit(solution)/shard_map/ppermute | solution.py:43
  4.5 7.2 %collective-permute-start.3 = (bf16[256,256]{1,0:T(8,128)(2,1)}, bf16[256,256]{1,0:T(8,128)(2,1)S(1)}, u32[]{:S(2)}, u32[]{:S(2)}) collective-permute-start(bf16[256,256]{1,0:T(8,128)(2,1)} %values_in.1), channel_id=1, source_target_pairs={{0,8},{1,9},{2,10},{3,11},{4,12},{5,13},{6,14},{7,15},{8,16},{9,17... | collective-permute-start | bytes 393224 | tf_op jit(solution)/shard_map/ppermute | solution.py:43
  7.9 5.9 %collective-permute-start.4 = (bf16[256,256]{1,0:T(8,128)(2,1)S(1)}, bf16[256,256]{1,0:T(8,128)(2,1)S(1)}, u32[]{:S(2)}, u32[]{:S(2)}) collective-permute-start(bf16[256,256]{1,0:T(8,128)(2,1)S(1)} %collective-permute-done.2.refs_5_), channel_id=1, source_target_pairs={{0,1},{1,0},{2,3},{3,2},{4,5},{5,4},{6,7},{7,6},{8,16},{9,17},{10,... | collective-permute-start | bytes 393224 | tf_op jit(solution)/shard_map/ppermute | solution.py:43
  8.2 6.6 %collective-permute-start.6 = (bf16[256,256]{1,0:T(8,128)(2,1)S(1)}, bf16[256,256]{1,0:T(8,128)(2,1)S(1)}, u32[]{:S(2)}, u32[]{:S(2)}) collective-permute-start(bf16[256,256]{1,0:T(8,128)(2,1)S(1)} %collective-permute-done.2.refs_5_), channel_id=1, source_target_pairs={{0,4},{1,5},{2,6},{3,7},{4,0},{5,1},{6,2},{7,3},{8,12},{9,13},{10,... | collective-permute-start | bytes 393224 | tf_op jit(solution)/shard_map/ppermute | solution.py:43
  11.8 6.4 %collective-permute-start.7 = (bf16[256,256]{1,0:T(8,128)(2,1)S(1)}, bf16[256,256]{1,0:T(8,128)(2,1)S(1)}, u32[]{:S(2)}, u32[]{:S(2)}) collective-permute-start(bf16[256,256]{1,0:T(8,128)(2,1)S(1)} %collective-permute-done.3.refs_6_), channel_id=1, source_target_pairs={{0,4},{1,5},{2,6},{3,7},{4,0},{5,1},{6,2},{7,3},{8,12},{9,13},{10,... | collective-permute-start | bytes 393224 | tf_op jit(solution)/shard_map/ppermute | solution.py:43
  13.2 7.1 %collective-permute-start.1 = (bf16[256,256]{1,0:T(8,128)(2,1)}, bf16[256,256]{1,0:T(8,128)(2,1)S(1)}, u32[]{:S(2)}, u32[]{:S(2)}) collective-permute-start(bf16[256,256]{1,0:T(8,128)(2,1)} %values_in.1), channel_id=1, source_target_pairs={{0,4},{1,5},{2,6},{3,7},{4,0},{5,1},{6,2},{7,3},{8,12},{9,13},{10,... | collective-permute-start | bytes 393224 | tf_op jit(solution)/shard_map/ppermute | solution.py:43
  13.8 6.5 %collective-permute-start.5 = (bf16[256,256]{1,0:T(8,128)(2,1)S(1)}, bf16[256,256]{1,0:T(8,128)(2,1)S(1)}, u32[]{:S(2)}, u32[]{:S(2)}) collective-permute-start(bf16[256,256]{1,0:T(8,128)(2,1)S(1)} %collective-permute-done.3.refs_6_), channel_id=1, source_target_pairs={{0,1},{1,0},{2,3},{3,2},{4,5},{5,4},{6,7},{7,6},{8,16},{9,17},{10,... | collective-permute-start | bytes 393224 | tf_op jit(solution)/shard_map/ppermute | solution.py:43
  14.8 8.0 %collective-permute-start.8 = (bf16[256,256]{1,0:T(8,128)(2,1)S(1)}, bf16[256,256]{1,0:T(8,128)(2,1)S(1)}, u32[]{:S(2)}, u32[]{:S(2)}) collective-permute-start(bf16[256,256]{1,0:T(8,128)(2,1)S(1)} %collective-permute-done.6.refs_3_), channel_id=1, source_target_pairs={{0,1},{1,0},{2,3},{3,2},{4,5},{5,4},{6,7},{7,6},{8,16},{9,17},{10,... | collective-permute-start | bytes 393224 | tf_op jit(solution)/shard_map/ppermute | solution.py:43
  18.2 4.7 %collective-permute-start.9 = (bf16[256,256]{1,0:T(8,128)(2,1)S(1)}, bf16[256,256]{1,0:T(8,128)(2,1)S(1)}, u32[]{:S(2)}, u32[]{:S(2)}) collective-permute-start(bf16[256,256]{1,0:T(8,128)(2,1)S(1)} %collective-permute-done.7.refs_4_), channel_id=1, source_target_pairs={{0,1},{1,0},{2,3},{3,2},{4,5},{5,4},{6,7},{7,6},{8,16},{9,17},{10,... | collective-permute-start | bytes 393224 | tf_op jit(solution)/shard_map/ppermute | solution.py:43
  24.5 1.8 %collective-permute-start.10 = (bf16[64,3072]{1,0:T(8,128)(2,1)S(1)}, bf16[64,3072]{1,0:T(8,128)(2,1)S(1)}, u32[]{:S(2)}, u32[]{:S(2)}) collective-permute-start(bf16[64,3072]{1,0:T(8,128)(2,1)S(1)} %get-tuple-element.59), channel_id=1, source_target_pairs={{0,1},{1,0},{2,3},{3,2},{4,5},{5,4},{6,7},{7,6},{8,9},{9,8},{10,11... | collective-permute-start | bytes 1179656 | tf_op jit(solution)/shard_map/ppermute | solution.py:22
  25.1 2.9 %collective-permute-start.11 = (bf16[64,2304]{1,0:T(8,128)(2,1)S(1)}, bf16[64,2304]{1,0:T(8,128)(2,1)S(1)}, u32[]{:S(2)}, u32[]{:S(2)}) collective-permute-start(bf16[64,2304]{1,0:T(8,128)(2,1)S(1)} %get-tuple-element.61), channel_id=1, source_target_pairs={{0,1},{1,0},{2,3},{3,2},{4,5},{5,4},{6,7},{7,6},{8,9},{9,8},{10,11... | collective-permute-start | bytes 884744 | tf_op jit(solution)/shard_map/ppermute | solution.py:22
  26.4 12.0 %collective-permute-start.16 = (bf16[64,3072]{1,0:T(8,128)(2,1)S(1)}, bf16[64,3072]{1,0:T(8,128)(2,1)S(1)}, u32[]{:S(2)}, u32[]{:S(2)}) collective-permute-start(bf16[64,3072]{1,0:T(8,128)(2,1)S(1)} %add_up.2), channel_id=1, source_target_pairs={{0,2},{1,3},{2,0},{3,1},{4,6},{5,7},{6,4},{7,5},{8,10},{9,11},{10,... | collective-permute-start | bytes 1179656 | tf_op jit(solution)/shard_map/ppermute | solution.py:22
  28.0 15.9 %collective-permute-start.12 = (bf16[64,2304]{1,0:T(8,128)(2,1)S(1)}, bf16[64,2304]{1,0:T(8,128)(2,1)S(1)}, u32[]{:S(2)}, u32[]{:S(2)}) collective-permute-start(bf16[64,2304]{1,0:T(8,128)(2,1)S(1)} %add_up.3), channel_id=1, source_target_pairs={{0,2},{1,3},{2,0},{3,1},{4,6},{5,7},{6,4},{7,5},{8,10},{9,11},{10,... | collective-permute-start | bytes 884744 | tf_op jit(solution)/shard_map/ppermute | solution.py:22
  29.5 1.6 %collective-permute-start.13 = (bf16[64,1792]{1,0:T(8,128)(2,1)S(1)}, bf16[64,1792]{1,0:T(8,128)(2,1)S(1)}, u32[]{:S(2)}, u32[]{:S(2)}) collective-permute-start(bf16[64,1792]{1,0:T(8,128)(2,1)S(1)} %get-tuple-element.64), channel_id=1, source_target_pairs={{0,1},{1,0},{2,3},{3,2},{4,5},{5,4},{6,7},{7,6},{8,9},{9,8},{10,11... | collective-permute-start | bytes 688136 | tf_op jit(solution)/shard_map/ppermute | solution.py:22
  29.5 1.8 %collective-permute-start.14 = (bf16[64,1792]{1,0:T(8,128)(2,1)S(1)}, bf16[64,1792]{1,0:T(8,128)(2,1)S(1)}, u32[]{:S(2)}, u32[]{:S(2)}) collective-permute-start(bf16[64,1792]{1,0:T(8,128)(2,1)S(1)} %get-tuple-element.65), channel_id=1, source_target_pairs={{0,1},{1,0},{2,3},{3,2},{4,5},{5,4},{6,7},{7,6},{8,9},{9,8},{10,11... | collective-permute-start | bytes 688136 | tf_op jit(solution)/shard_map/ppermute | solution.py:22
  30.0 1.6 %collective-permute-start.15 = (bf16[64,1792]{1,0:T(8,128)(2,1)S(1)}, bf16[64,1792]{1,0:T(8,128)(2,1)S(1)}, u32[]{:S(2)}, u32[]{:S(2)}) collective-permute-start(bf16[64,1792]{1,0:T(8,128)(2,1)S(1)} %get-tuple-element.66), channel_id=1, source_target_pairs={{0,1},{1,0},{2,3},{3,2},{4,5},{5,4},{6,7},{7,6},{8,9},{9,8},{10,11... | collective-permute-start | bytes 688136 | tf_op jit(solution)/shard_map/ppermute | solution.py:22
where the time goes:
time: 44.9 us; the launch traced here: 44.7 us
  waiting for transfers between devices  21.8 us (49%)
  starting transfers between devices  13.9 us (31%)
  Pallas kernels  8.97 us (20%)
    ppermute x7, waiting for transfers between devices, hop(): return lax.ppermute(block, axis, pairs)  13.6 us
    ppermute x10, starting transfers between devices, move(): return lax.ppermute(block, ('ctx', 'head'), pairs)  10.4 us
    ppermute x10, waiting for transfers between devices, move(): return lax.ppermute(block, ('ctx', 'head'), pairs)  8.22 us
    ppermute x7, starting transfers between devices, hop(): return lax.ppermute(block, axis, pairs)  3.43 us
    pallas_call x1, Pallas kernels, attend_next(): pl.pallas_call(functools.partial(next_kernel, numbers), out_shape=state_s...  2.59 us
    pallas_call x2, Pallas kernels, combine(): pl.pallas_call(functools.partial(combine_kernel, at), out_shape=jax.Shape...  1.68 us
    pallas_call x1, Pallas kernels, attend_last(): pl.pallas_call(functools.partial(last_kernel, numbers, columns), out_shap...  1.61 us
    pallas_call x1, Pallas kernels, attend_first(): pl.pallas_call(first_kernel, out_shape=state_shapes(queries) + (pltpu.VME...  1.6 us
  transfers between devices with their start and end apart: 17, of which 12 were waited for; matrix products, arithmetic and copies ran while one was open for 0% of the time, Pallas kernels for 15%

commit v1 on v0

--- a/solution.py
+++ b/solution.py
@@ -30,6 +30,7 @@
 BESIDE = ((0, 1), (2, 3), (4, 5), (6, 7))
 BY_TWO = ((0, 2, 4), (1, 3, 5))
 AGAIN = ((2, 4), (3, 5))
+ACROSS = ((2, 3), (4, 5))
 
 
 def move(block, rings):
@@ -449,8 +450,11 @@
         beside = [move(x, BESIDE) for x in (keys, values)]
         *state, fetched, open_beside = attend_first(doc_ids, queries, keys, values)
         by_four = [move(after(x, state[0]), AGAIN) for x in by_two]
-        swap_two = [move(after(after(x, beside[0]), state[0]), BESIDE) for x in by_two]
-        swap_four = [move(after(x, by_four[0]), AGAIN) for x in swap_two]
+        swap_two = [
+            move(after(after(by_two[0], beside[0]), state[0]), ACROSS),
+            move(after(by_two[1], beside[1]), ACROSS),
+        ]
+        swap_four = [move(by_four[0], ACROSS), move(after(swap_two[1], by_four[0]), AGAIN)]
         chunks = [beside, by_two, by_four]
         *state, weight = attend_next(fetched, open_beside, out_weight, state, chunks, (1, 2, 3))
         chunks = [swap_two, swap_four]

time: 44.9 us -> 43.2 us (0.962)
  the two profiles are of different devices: /device:TPU:0 before, /device:TPU:8 now
where the time goes in v1:
time: 43.2 us; the launch traced here: 43 us
  waiting for transfers between devices  17.9 us (41%)
  starting transfers between devices  16 us (37%)
  Pallas kernels  8.98 us (21%)
    ppermute x7, waiting for transfers between devices, hop(): return lax.ppermute(block, axis, pairs)  13.6 us
    ppermute x10, starting transfers between devices, move(): return lax.ppermute(block, ('ctx', 'head'), pairs)  12.6 us
    ppermute x10, waiting for transfers between devices, move(): return lax.ppermute(block, ('ctx', 'head'), pairs)  4.38 us
    ppermute x7, starting transfers between devices, hop(): return lax.ppermute(block, axis, pairs)  3.43 us
    pallas_call x1, Pallas kernels, attend_next(): pl.pallas_call(functools.partial(next_kernel, numbers), out_shape=state_s...  2.59 us
    pallas_call x2, Pallas kernels, combine(): pl.pallas_call(functools.partial(combine_kernel, at), out_shape=jax.Shape...  1.68 us
    pallas_call x1, Pallas kernels, attend_first(): pl.pallas_call(first_kernel, out_shape=state_shapes(queries) + (pltpu.VME...  1.62 us
    pallas_call x1, Pallas kernels, attend_last(): pl.pallas_call(functools.partial(last_kernel, numbers, columns), out_shap...  1.61 us
  transfers between devices with their start and end apart: 17, of which 10 were waited for; matrix products, arithmetic and copies ran while one was open for 0% of the time, Pallas kernels for 15%

profile of v1, /device:TPU:8, one launch (start us, length us, event | category | flops | bytes accessed | tf_op | source)
XLA Modules:
  0.0 43.0 jit_solution(505931637499038653)
XLA Ops:
  0.0 1.6 %collective-permute-start.2 = (bf16[256,256]{1,0:T(8,128)(2,1)}, bf16[256,256]{1,0:T(8,128)(2,1)S(1)}, u32[]{:S(2)}, u32[]{:S(2)}) collective-permute-start(bf16[256,256]{1,0:T(8,128)(2,1)} %keys_in.1), channel_id=1, source_target_pairs={{0,8},{1,9},{2,10},{3,11},{4,12},{5,13},{6,14},{7,15},{8,16},{9,17... | collective-permute-start | bytes 393224 | tf_op jit(solution)/shard_map/ppermute | solution.py:44
  1.6 1.8 %collective-permute-start.1 = (bf16[256,256]{1,0:T(8,128)(2,1)}, bf16[256,256]{1,0:T(8,128)(2,1)S(1)}, u32[]{:S(2)}, u32[]{:S(2)}) collective-permute-start(bf16[256,256]{1,0:T(8,128)(2,1)} %values_in.1), channel_id=1, source_target_pairs={{0,4},{1,5},{2,6},{3,7},{4,0},{5,1},{6,2},{7,3},{8,12},{9,13},{10,... | collective-permute-start | bytes 393224 | tf_op jit(solution)/shard_map/ppermute | solution.py:44
  3.4 0.2 collective-permute-start
  3.6 1.6 %attend_first.1 = (f32[1024,128]{1,0:T(8,128)S(1)}, f32[1024,128]{1,0:T(8,128)S(1)}, f32[1024,128]{1,0:T(8,128)S(1)}, bf16[256,512]{1,0:T(8,128)(2,1)S(1)}, f32[16,256]{1,0:T(8,128)S(1)}) custom-call(s32[16]{0:T(128)} %docs_in.1, bf16[256,512]{1,0:T(8,128)(2,1)} %queries_in.1, bf16[256,256]{1,0:T(8,128)(2,1)} %keys_in.1, bf16[256,256]{1,0:T(8,128)(2,1)} %values_in.1), custom_call_target="tpu_custom_call" | custom-call | flops 134217728 | tf_op jit(solution)/shard_map/attend_first/pallas_call | solution.py:200
  5.3 1.3 %collective-permute-done.2.refs_5_ = bf16[256,256]{1,0:T(8,128)(2,1)S(1)} collective-permute-done((bf16[256,256]{1,0:T(8,128)(2,1)}, bf16[256,256]{1,0:T(8,128)(2,1)S(1)}, u32[]{:S(2)}, u32[]{:S(2)}) %collective-permute-start.2) | collective-permute-done | bytes 131104 | tf_op jit(solution)/shard_map/ppermute | solution.py:44
  6.6 1.6 %collective-permute-start.4 = (bf16[256,256]{1,0:T(8,128)(2,1)S(1)}, bf16[256,256]{1,0:T(8,128)(2,1)S(1)}, u32[]{:S(2)}, u32[]{:S(2)}) collective-permute-start(bf16[256,256]{1,0:T(8,128)(2,1)S(1)} %collective-permute-done.2.refs_5_), channel_id=1, source_target_pairs={{0,1},{1,0},{2,3},{3,2},{4,5},{5,4},{6,7},{7,6},{8,16},{9,17},{10,... | collective-permute-start | bytes 393224 | tf_op jit(solution)/shard_map/ppermute | solution.py:44
  8.2 0.4 %collective-permute-done.3.refs_6_ = bf16[256,256]{1,0:T(8,128)(2,1)S(1)} collective-permute-done((bf16[256,256]{1,0:T(8,128)(2,1)}, bf16[256,256]{1,0:T(8,128)(2,1)S(1)}, u32[]{:S(2)}, u32[]{:S(2)}) %collective-permute-start.3) | collective-permute-done | bytes 131104 | tf_op jit(solution)/shard_map/ppermute | solution.py:44
  8.6 1.5 %collective-permute-start.7 = (bf16[256,256]{1,0:T(8,128)(2,1)S(1)}, bf16[256,256]{1,0:T(8,128)(2,1)S(1)}, u32[]{:S(2)}, u32[]{:S(2)}) collective-permute-start(bf16[256,256]{1,0:T(8,128)(2,1)S(1)} %collective-permute-done.3.refs_6_), channel_id=1, source_target_pairs={{0,1},{1,0},{2,3},{3,2},{4,5},{5,4},{6,7},{7,6},{8,12},{9,13},{10,... | collective-permute-start | bytes 393224 | tf_op jit(solution)/shard_map/ppermute | solution.py:44
  10.1 2.4 %collective-permute-start.5 = (bf16[256,256]{1,0:T(8,128)(2,1)S(1)}, bf16[256,256]{1,0:T(8,128)(2,1)S(1)}, u32[]{:S(2)}, u32[]{:S(2)}) collective-permute-start(bf16[256,256]{1,0:T(8,128)(2,1)S(1)} %collective-permute-done.3.refs_6_), channel_id=1, source_target_pairs={{0,1},{1,0},{2,3},{3,2},{4,5},{5,4},{6,7},{7,6},{8,16},{9,17},{10,... | collective-permute-start | bytes 393224 | tf_op jit(solution)/shard_map/ppermute | solution.py:44
  12.5 0.5 %collective-permute-start.6 = (bf16[256,256]{1,0:T(8,128)(2,1)S(1)}, bf16[256,256]{1,0:T(8,128)(2,1)S(1)}, u32[]{:S(2)}, u32[]{:S(2)}) collective-permute-start(bf16[256,256]{1,0:T(8,128)(2,1)S(1)} %collective-permute-done.2.refs_5_), channel_id=1, source_target_pairs={{0,1},{1,0},{2,3},{3,2},{4,5},{5,4},{6,7},{7,6},{8,12},{9,13},{10,... | collective-permute-start | bytes 393224 | tf_op jit(solution)/shard_map/ppermute | solution.py:44
  13.0 1.8 %collective-permute-done.7.refs_4_ = bf16[256,256]{1,0:T(8,128)(2,1)S(1)} collective-permute-done((bf16[256,256]{1,0:T(8,128)(2,1)S(1)}, bf16[256,256]{1,0:T(8,128)(2,1)S(1)}, u32[]{:S(2)}, u32[]{:S(2)}) %collective-permute-start.7) | collective-permute-done | bytes 131104 | tf_op jit(solution)/shard_map/ppermute | solution.py:44
  14.8 1.4 %collective-permute-start.9 = (bf16[256,256]{1,0:T(8,128)(2,1)S(1)}, bf16[256,256]{1,0:T(8,128)(2,1)S(1)}, u32[]{:S(2)}, u32[]{:S(2)}) collective-permute-start(bf16[256,256]{1,0:T(8,128)(2,1)S(1)} %collective-permute-done.7.refs_4_), channel_id=1, source_target_pairs={{0,1},{1,0},{2,3},{3,2},{4,5},{5,4},{6,7},{7,6},{8,16},{9,17},{10,... | collective-permute-start | bytes 393224 | tf_op jit(solution)/shard_map/ppermute | solution.py:44
  16.2 1.5 %collective-permute-start.8 = (bf16[256,256]{1,0:T(8,128)(2,1)S(1)}, bf16[256,256]{1,0:T(8,128)(2,1)S(1)}, u32[]{:S(2)}, u32[]{:S(2)}) collective-permute-start(bf16[256,256]{1,0:T(8,128)(2,1)S(1)} %collective-permute-done.4.refs_7_), channel_id=1, source_target_pairs={{0,1},{1,0},{2,3},{3,2},{4,5},{5,4},{6,7},{7,6},{8,12},{9,13},{10,... | collective-permute-start | bytes 393224 | tf_op jit(solution)/shard_map/ppermute | solution.py:44
  17.7 2.6 %attend_next.1 = (f32[1024,128]{1,0:T(8,128)S(1)}, f32[1024,128]{1,0:T(8,128)S(1)}, f32[1024,128]{1,0:T(8,128)S(1)}, bf16[512,5376]{1,0:T(8,128)(2,1)S(1)}) custom-call(bf16[256,512]{1,0:T(8,128)(2,1)S(1)} %get-tuple-element.34.queries, f32[16,256]{1,0:T(8,128)S(1)} %get-tuple-element.35.open_beside, bf16[512,5376]{1,0:T(8,128)(2,1)} %weight_in.1, ...), custom_call_target="tpu_custom_call" | custom-call | flops 402653184 | bytes 5505024 | tf_op jit(solution)/shard_map/attend_next/pallas_call | solution.py:222
  20.4 0.8 %collective-permute-done.8.refs_5_ = bf16[256,256]{1,0:T(8,128)(2,1)S(1)} collective-permute-done((bf16[256,256]{1,0:T(8,128)(2,1)S(1)}, bf16[256,256]{1,0:T(8,128)(2,1)S(1)}, u32[]{:S(2)}, u32[]{:S(2)}) %collective-permute-start.8) | collective-permute-done | bytes 131104 | tf_op jit(solution)/shard_map/ppermute | solution.py:44
  21.2 1.6 %attend_last.1 = (bf16[128,512]{1,0:T(8,128)(2,1)S(1)}, bf16[128,512]{1,0:T(8,128)(2,1)S(1)}, f32[64,3072]{1,0:T(8,128)S(1)}, bf16[64,3072]{1,0:T(8,128)(2,1)S(1)}) custom-call(bf16[256,512]{1,0:T(8,128)(2,1)S(1)} %get-tuple-element.34.queries, bf16[512,5376]{1,0:T(8,128)(2,1)S(1)} %get-tuple-element.41.weight, f32[1024,128]{1,0:T(8,128)S(1)} %get-tuple-element.42.refs_0_, ...), custom_call_target="tpu_custom_call" | custom-call | flops 268435456 | tf_op jit(solution)/shard_map/attend_last/pallas_call | solution.py:265
  22.8 0.1 collective-permute-start.10
  22.9 0.5 %project.2 = (f32[64,2304]{1,0:T(8,128)S(1)}, bf16[64,2304]{1,0:T(8,128)(2,1)S(1)}) custom-call(bf16[128,512]{1,0:T(8,128)(2,1)S(1)} %get-tuple-element.51.rows, bf16[512,5376]{1,0:T(8,128)(2,1)S(1)} %get-tuple-element.41.weight), custom_call_target="tpu_custom_call" | custom-call | flops 301989888 | tf_op jit(solution)/shard_map/project/pallas_call | solution.py:300
  23.4 0.6 %collective-permute-start.11 = (bf16[64,2304]{1,0:T(8,128)(2,1)S(1)}, bf16[64,2304]{1,0:T(8,128)(2,1)S(1)}, u32[]{:S(2)}, u32[]{:S(2)}) collective-permute-start(bf16[64,2304]{1,0:T(8,128)(2,1)S(1)} %get-tuple-element.57), channel_id=1, source_target_pairs={{0,1},{1,0},{2,3},{3,2},{4,5},{5,4},{6,7},{7,6},{8,9},{9,8},{10,11... | collective-permute-start | bytes 884744 | tf_op jit(solution)/shard_map/ppermute | solution.py:22
  23.9 0.7 %collective-permute-done.10.theirs = bf16[64,3072]{1,0:T(8,128)(2,1)S(1)} collective-permute-done((bf16[64,3072]{1,0:T(8,128)(2,1)S(1)}, bf16[64,3072]{1,0:T(8,128)(2,1)S(1)}, u32[]{:S(2)}, u32[]{:S(2)}) %collective-permute-start.10) | collective-permute-done | bytes 393248 | tf_op jit(solution)/shard_map/ppermute | solution.py:22
  24.7 1.6 %collective-permute-start.16 = (bf16[64,3072]{1,0:T(8,128)(2,1)S(1)}, bf16[64,3072]{1,0:T(8,128)(2,1)S(1)}, u32[]{:S(2)}, u32[]{:S(2)}) collective-permute-start(bf16[64,3072]{1,0:T(8,128)(2,1)S(1)} %add_up.2), channel_id=1, source_target_pairs={{0,2},{1,3},{2,0},{3,1},{4,6},{5,7},{6,4},{7,5},{8,10},{9,11},{10,... | collective-permute-start | bytes 1179656 | tf_op jit(solution)/shard_map/ppermute | solution.py:22
  26.3 0.6 %collective-permute-start.12 = (bf16[64,2304]{1,0:T(8,128)(2,1)S(1)}, bf16[64,2304]{1,0:T(8,128)(2,1)S(1)}, u32[]{:S(2)}, u32[]{:S(2)}) collective-permute-start(bf16[64,2304]{1,0:T(8,128)(2,1)S(1)} %add_up.3), channel_id=1, source_target_pairs={{0,2},{1,3},{2,0},{3,1},{4,6},{5,7},{6,4},{7,5},{8,10},{9,11},{10,... | collective-permute-start | bytes 884744 | tf_op jit(solution)/shard_map/ppermute | solution.py:22
  26.9 0.9 %project.3 = (f32[64,5376]{1,0:T(8,128)S(1)}, bf16[64,1792]{1,0:T(8,128)(2,1)S(1)}, bf16[64,1792]{1,0:T(8,128)(2,1)S(1)}, bf16[64,1792]{1,0:T(8,128)(2,1)S(1)}) custom-call(bf16[128,512]{1,0:T(8,128)(2,1)S(1)} %get-tuple-element.58.rows, bf16[512,5376]{1,0:T(8,128)(2,1)S(1)} %get-tuple-element.41.weight), custom_call_target="tpu_custom_call" | custom-call | flops 704643072 | tf_op jit(solution)/shard_map/project/pallas_call | solution.py:300
  27.8 0.5 %collective-permute-start.14 = (bf16[64,1792]{1,0:T(8,128)(2,1)S(1)}, bf16[64,1792]{1,0:T(8,128)(2,1)S(1)}, u32[]{:S(2)}, u32[]{:S(2)}) collective-permute-start(bf16[64,1792]{1,0:T(8,128)(2,1)S(1)} %get-tuple-element.61), channel_id=1, source_target_pairs={{0,1},{1,0},{2,3},{3,2},{4,5},{5,4},{6,7},{7,6},{8,9},{9,8},{10,11... | collective-permute-start | bytes 688136 | tf_op jit(solution)/shard_map/ppermute | solution.py:22
  28.3 0.1 collective-permute-start.15
  28.4 0.9 %collective-permute-done.13.refs_0_ = bf16[64,1792]{1,0:T(8,128)(2,1)S(1)} collective-permute-done((bf16[64,1792]{1,0:T(8,128)(2,1)S(1)}, bf16[64,1792]{1,0:T(8,128)(2,1)S(1)}, u32[]{:S(2)}, u32[]{:S(2)}) %collective-permute-start.13) | collective-permute-done | bytes 229408 | tf_op jit(solution)/shard_map/ppermute | solution.py:22
  29.3 0.3 collective-permute-done.14.refs_1_
  29.6 0.3 collective-permute-done.15.refs_2_
  30.0 6.7 %collective-permute-done.16.across = bf16[64,3072]{1,0:T(8,128)(2,1)S(1)} collective-permute-done((bf16[64,3072]{1,0:T(8,128)(2,1)S(1)}, bf16[64,3072]{1,0:T(8,128)(2,1)S(1)}, u32[]{:S(2)}, u32[]{:S(2)}) %collective-permute-start.16) | collective-permute-done | bytes 393248 | tf_op jit(solution)/shard_map/ppermute | solution.py:22
  36.7 0.9 %combine.2.refs_3_ = bf16[64,5376]{1,0:T(8,128)(2,1)} custom-call(f32[64,5376]{1,0:T(8,128)S(1)} %get-tuple-element.59.mine, bf16[64,3072]{1,0:T(8,128)(2,1)S(1)} %collective-permute-done.16.across, bf16[64,1792]{1,0:T(8,128)(2,1)S(1)} %collective-permute-done.13.refs_0_, bf16[64,1792]{1,0:T(8,128)(2,1)S(1)} %collective-permute-done.14.refs_1_, ...), custom_call_target="tpu_custom_call" | custom-call | tf_op jit(solution)/shard_map/combine/pallas_call | solution.py:347
  37.6 4.6 %collective-permute-done.12.across = bf16[64,2304]{1,0:T(8,128)(2,1)S(1)} collective-permute-done((bf16[64,2304]{1,0:T(8,128)(2,1)S(1)}, bf16[64,2304]{1,0:T(8,128)(2,1)S(1)}, u32[]{:S(2)}, u32[]{:S(2)}) %collective-permute-start.12) | collective-permute-done | bytes 294944 | tf_op jit(solution)/shard_map/ppermute | solution.py:22
  42.2 0.8 %combine.3 = bf16[64,5376]{1,0:T(8,128)(2,1)} custom-call(f32[64,5376]{1,0:T(8,128)S(1)} %get-tuple-element.59.mine, bf16[64,2304]{1,0:T(8,128)(2,1)S(1)} %collective-permute-done.12.across, bf16[64,1792]{1,0:T(8,128)(2,1)S(1)} %collective-permute-done.13.refs_0_, ...), custom_call_target="tpu_custom_call", output_to_operand_aliasing={{}: (5, {})} | custom-call | tf_op jit(solution)/shard_map/combine/pallas_call | solution.py:347
  (11 shorter events, 0.2 us)
Async XLA Ops:
  0.0 6.6 %collective-permute-start.2 = (bf16[256,256]{1,0:T(8,128)(2,1)}, bf16[256,256]{1,0:T(8,128)(2,1)S(1)}, u32[]{:S(2)}, u32[]{:S(2)}) collective-permute-start(bf16[256,256]{1,0:T(8,128)(2,1)} %keys_in.1), channel_id=1, source_target_pairs={{0,8},{1,9},{2,10},{3,11},{4,12},{5,13},{6,14},{7,15},{8,16},{9,17... | collective-permute-start | bytes 393224 | tf_op jit(solution)/shard_map/ppermute | solution.py:44
  1.6 7.0 %collective-permute-start.3 = (bf16[256,256]{1,0:T(8,128)(2,1)}, bf16[256,256]{1,0:T(8,128)(2,1)S(1)}, u32[]{:S(2)}, u32[]{:S(2)}) collective-permute-start(bf16[256,256]{1,0:T(8,128)(2,1)} %values_in.1), channel_id=1, source_target_pairs={{0,8},{1,9},{2,10},{3,11},{4,12},{5,13},{6,14},{7,15},{8,16},{9,17... | collective-permute-start | bytes 393224 | tf_op jit(solution)/shard_map/ppermute | solution.py:44
  1.6 7.0 %collective-permute-start.1 = (bf16[256,256]{1,0:T(8,128)(2,1)}, bf16[256,256]{1,0:T(8,128)(2,1)S(1)}, u32[]{:S(2)}, u32[]{:S(2)}) collective-permute-start(bf16[256,256]{1,0:T(8,128)(2,1)} %values_in.1), channel_id=1, source_target_pairs={{0,4},{1,5},{2,6},{3,7},{4,0},{5,1},{6,2},{7,3},{8,12},{9,13},{10,... | collective-permute-start | bytes 393224 | tf_op jit(solution)/shard_map/ppermute | solution.py:44
  3.4 9.1 %collective-permute-start = (bf16[256,256]{1,0:T(8,128)(2,1)}, bf16[256,256]{1,0:T(8,128)(2,1)S(1)}, u32[]{:S(2)}, u32[]{:S(2)}) collective-permute-start(bf16[256,256]{1,0:T(8,128)(2,1)} %keys_in.1), channel_id=1, source_target_pairs={{0,4},{1,5},{2,6},{3,7},{4,0},{5,1},{6,2},{7,3},{8,12},{9,13},{10,... | collective-permute-start | bytes 393224 | tf_op jit(solution)/shard_map/ppermute | solution.py:44
  6.6 6.4 %collective-permute-start.4 = (bf16[256,256]{1,0:T(8,128)(2,1)S(1)}, bf16[256,256]{1,0:T(8,128)(2,1)S(1)}, u32[]{:S(2)}, u32[]{:S(2)}) collective-permute-start(bf16[256,256]{1,0:T(8,128)(2,1)S(1)} %collective-permute-done.2.refs_5_), channel_id=1, source_target_pairs={{0,1},{1,0},{2,3},{3,2},{4,5},{5,4},{6,7},{7,6},{8,16},{9,17},{10,... | collective-permute-start | bytes 393224 | tf_op jit(solution)/shard_map/ppermute | solution.py:44
  8.6 6.2 %collective-permute-start.7 = (bf16[256,256]{1,0:T(8,128)(2,1)S(1)}, bf16[256,256]{1,0:T(8,128)(2,1)S(1)}, u32[]{:S(2)}, u32[]{:S(2)}) collective-permute-start(bf16[256,256]{1,0:T(8,128)(2,1)S(1)} %collective-permute-done.3.refs_6_), channel_id=1, source_target_pairs={{0,1},{1,0},{2,3},{3,2},{4,5},{5,4},{6,7},{7,6},{8,12},{9,13},{10,... | collective-permute-start | bytes 393224 | tf_op jit(solution)/shard_map/ppermute | solution.py:44
  10.1 7.6 %collective-permute-start.5 = (bf16[256,256]{1,0:T(8,128)(2,1)S(1)}, bf16[256,256]{1,0:T(8,128)(2,1)S(1)}, u32[]{:S(2)}, u32[]{:S(2)}) collective-permute-start(bf16[256,256]{1,0:T(8,128)(2,1)S(1)} %collective-permute-done.3.refs_6_), channel_id=1, source_target_pairs={{0,1},{1,0},{2,3},{3,2},{4,5},{5,4},{6,7},{7,6},{8,16},{9,17},{10,... | collective-permute-start | bytes 393224 | tf_op jit(solution)/shard_map/ppermute | solution.py:44
  12.5 7.8 %collective-permute-start.6 = (bf16[256,256]{1,0:T(8,128)(2,1)S(1)}, bf16[256,256]{1,0:T(8,128)(2,1)S(1)}, u32[]{:S(2)}, u32[]{:S(2)}) collective-permute-start(bf16[256,256]{1,0:T(8,128)(2,1)S(1)} %collective-permute-done.2.refs_5_), channel_id=1, source_target_pairs={{0,1},{1,0},{2,3},{3,2},{4,5},{5,4},{6,7},{7,6},{8,12},{9,13},{10,... | collective-permute-start | bytes 393224 | tf_op jit(solution)/shard_map/ppermute | solution.py:44
  14.8 5.6 %collective-permute-start.9 = (bf16[256,256]{1,0:T(8,128)(2,1)S(1)}, bf16[256,256]{1,0:T(8,128)(2,1)S(1)}, u32[]{:S(2)}, u32[]{:S(2)}) collective-permute-start(bf16[256,256]{1,0:T(8,128)(2,1)S(1)} %collective-permute-done.7.refs_4_), channel_id=1, source_target_pairs={{0,1},{1,0},{2,3},{3,2},{4,5},{5,4},{6,7},{7,6},{8,16},{9,17},{10,... | collective-permute-start | bytes 393224 | tf_op jit(solution)/shard_map/ppermute | solution.py:44
  16.2 5.0 %collective-permute-start.8 = (bf16[256,256]{1,0:T(8,128)(2,1)S(1)}, bf16[256,256]{1,0:T(8,128)(2,1)S(1)}, u32[]{:S(2)}, u32[]{:S(2)}) collective-permute-start(bf16[256,256]{1,0:T(8,128)(2,1)S(1)} %collective-permute-done.4.refs_7_), channel_id=1, source_target_pairs={{0,1},{1,0},{2,3},{3,2},{4,5},{5,4},{6,7},{7,6},{8,12},{9,13},{10,... | collective-permute-start | bytes 393224 | tf_op jit(solution)/shard_map/ppermute | solution.py:44
  22.8 1.8 %collective-permute-start.10 = (bf16[64,3072]{1,0:T(8,128)(2,1)S(1)}, bf16[64,3072]{1,0:T(8,128)(2,1)S(1)}, u32[]{:S(2)}, u32[]{:S(2)}) collective-permute-start(bf16[64,3072]{1,0:T(8,128)(2,1)S(1)} %get-tuple-element.55), channel_id=1, source_target_pairs={{0,1},{1,0},{2,3},{3,2},{4,5},{5,4},{6,7},{7,6},{8,9},{9,8},{10,11... | collective-permute-start | bytes 1179656 | tf_op jit(solution)/shard_map/ppermute | solution.py:22
  23.4 2.9 %collective-permute-start.11 = (bf16[64,2304]{1,0:T(8,128)(2,1)S(1)}, bf16[64,2304]{1,0:T(8,128)(2,1)S(1)}, u32[]{:S(2)}, u32[]{:S(2)}) collective-permute-start(bf16[64,2304]{1,0:T(8,128)(2,1)S(1)} %get-tuple-element.57), channel_id=1, source_target_pairs={{0,1},{1,0},{2,3},{3,2},{4,5},{5,4},{6,7},{7,6},{8,9},{9,8},{10,11... | collective-permute-start | bytes 884744 | tf_op jit(solution)/shard_map/ppermute | solution.py:22
  24.7 12.0 %collective-permute-start.16 = (bf16[64,3072]{1,0:T(8,128)(2,1)S(1)}, bf16[64,3072]{1,0:T(8,128)(2,1)S(1)}, u32[]{:S(2)}, u32[]{:S(2)}) collective-permute-start(bf16[64,3072]{1,0:T(8,128)(2,1)S(1)} %add_up.2), channel_id=1, source_target_pairs={{0,2},{1,3},{2,0},{3,1},{4,6},{5,7},{6,4},{7,5},{8,10},{9,11},{10,... | collective-permute-start | bytes 1179656 | tf_op jit(solution)/shard_map/ppermute | solution.py:22
  26.3 15.9 %collective-permute-start.12 = (bf16[64,2304]{1,0:T(8,128)(2,1)S(1)}, bf16[64,2304]{1,0:T(8,128)(2,1)S(1)}, u32[]{:S(2)}, u32[]{:S(2)}) collective-permute-start(bf16[64,2304]{1,0:T(8,128)(2,1)S(1)} %add_up.3), channel_id=1, source_target_pairs={{0,2},{1,3},{2,0},{3,1},{4,6},{5,7},{6,4},{7,5},{8,10},{9,11},{10,... | collective-permute-start | bytes 884744 | tf_op jit(solution)/shard_map/ppermute | solution.py:22
  27.8 1.6 %collective-permute-start.13 = (bf16[64,1792]{1,0:T(8,128)(2,1)S(1)}, bf16[64,1792]{1,0:T(8,128)(2,1)S(1)}, u32[]{:S(2)}, u32[]{:S(2)}) collective-permute-start(bf16[64,1792]{1,0:T(8,128)(2,1)S(1)} %get-tuple-element.60), channel_id=1, source_target_pairs={{0,1},{1,0},{2,3},{3,2},{4,5},{5,4},{6,7},{7,6},{8,9},{9,8},{10,11... | collective-permute-start | bytes 688136 | tf_op jit(solution)/shard_map/ppermute | solution.py:22
  27.8 1.8 %collective-permute-start.14 = (bf16[64,1792]{1,0:T(8,128)(2,1)S(1)}, bf16[64,1792]{1,0:T(8,128)(2,1)S(1)}, u32[]{:S(2)}, u32[]{:S(2)}) collective-permute-start(bf16[64,1792]{1,0:T(8,128)(2,1)S(1)} %get-tuple-element.61), channel_id=1, source_target_pairs={{0,1},{1,0},{2,3},{3,2},{4,5},{5,4},{6,7},{7,6},{8,9},{9,8},{10,11... | collective-permute-start | bytes 688136 | tf_op jit(solution)/shard_map/ppermute | solution.py:22
  28.3 1.6 %collective-permute-start.15 = (bf16[64,1792]{1,0:T(8,128)(2,1)S(1)}, bf16[64,1792]{1,0:T(8,128)(2,1)S(1)}, u32[]{:S(2)}, u32[]{:S(2)}) collective-permute-start(bf16[64,1792]{1,0:T(8,128)(2,1)S(1)} %get-tuple-element.62), channel_id=1, source_target_pairs={{0,1},{1,0},{2,3},{3,2},{4,5},{5,4},{6,7},{7,6},{8,9},{9,8},{10,11... | collective-permute-start | bytes 688136 | tf_op jit(solution)/shard_map/ppermute | solution.py:22

commit v2 on v1

--- a/solution.py
+++ b/solution.py
@@ -31,6 +31,7 @@
 BY_TWO = ((0, 2, 4), (1, 3, 5))
 AGAIN = ((2, 4), (3, 5))
 ACROSS = ((2, 3), (4, 5))
+LAST = ((4, 5),)
 
 
 def move(block, rings):
@@ -454,7 +455,7 @@
             move(after(after(by_two[0], beside[0]), state[0]), ACROSS),
             move(after(by_two[1], beside[1]), ACROSS),
         ]
-        swap_four = [move(by_four[0], ACROSS), move(after(swap_two[1], by_four[0]), AGAIN)]
+        swap_four = [move(after(swap_two[0], by_four[0]), AGAIN), move(by_four[1], LAST)]
         chunks = [beside, by_two, by_four]
         *state, weight = attend_next(fetched, open_beside, out_weight, state, chunks, (1, 2, 3))
         chunks = [swap_two, swap_four]

time: 43.2 us -> 42.4 us (0.981)
  the two profiles are of different devices: /device:TPU:8 before, /device:TPU:16 now
where the time goes in v2:
time: 42.4 us; the launch traced here: 42.3 us
  waiting for transfers between devices  19.3 us (46%)
  starting transfers between devices  13.9 us (33%)
  Pallas kernels  8.96 us (21%)
    ppermute x7, waiting for transfers between devices, hop(): return lax.ppermute(block, axis, pairs)  13.6 us
    ppermute x10, starting transfers between devices, move(): return lax.ppermute(block, ('ctx', 'head'), pairs)  10.5 us
    ppermute x10, waiting for transfers between devices, move(): return lax.ppermute(block, ('ctx', 'head'), pairs)  5.72 us
    ppermute x7, starting transfers between devices, hop(): return lax.ppermute(block, axis, pairs)  3.43 us
    pallas_call x1, Pallas kernels, attend_next(): pl.pallas_call(functools.partial(next_kernel, numbers), out_shape=state_s...  2.59 us
    pallas_call x2, Pallas kernels, combine(): pl.pallas_call(functools.partial(combine_kernel, at), out_shape=jax.Shape...  1.68 us
    pallas_call x1, Pallas kernels, attend_first(): pl.pallas_call(first_kernel, out_shape=state_shapes(queries) + (pltpu.VME...  1.61 us
    pallas_call x1, Pallas kernels, attend_last(): pl.pallas_call(functools.partial(last_kernel, numbers, columns), out_shap...  1.61 us
  transfers between devices with their start and end apart: 17, of which 12 were waited for; matrix products, arithmetic and copies ran while one was open for 0% of the time, Pallas kernels for 15%

profile of v2, /device:TPU:16, one launch (start us, length us, event | category | flops | bytes accessed | tf_op | source)
XLA Modules:
  0.0 42.3 jit_solution(1061407900151349876)
XLA Ops:
  0.0 1.9 %collective-permute-start = (bf16[256,256]{1,0:T(8,128)(2,1)}, bf16[256,256]{1,0:T(8,128)(2,1)S(1)}, u32[]{:S(2)}, u32[]{:S(2)}) collective-permute-start(bf16[256,256]{1,0:T(8,128)(2,1)} %keys_in.1), channel_id=1, source_target_pairs={{0,4},{1,5},{2,6},{3,7},{4,0},{5,1},{6,2},{7,3},{8,12},{9,13},{10,... | collective-permute-start | bytes 393224 | tf_op jit(solution)/shard_map/ppermute | solution.py:45
  1.9 1.6 %collective-permute-start.3 = (bf16[256,256]{1,0:T(8,128)(2,1)}, bf16[256,256]{1,0:T(8,128)(2,1)S(1)}, u32[]{:S(2)}, u32[]{:S(2)}) collective-permute-start(bf16[256,256]{1,0:T(8,128)(2,1)} %values_in.1), channel_id=1, source_target_pairs={{0,8},{1,9},{2,10},{3,11},{4,12},{5,13},{6,14},{7,15},{8,16},{9,17... | collective-permute-start | bytes 393224 | tf_op jit(solution)/shard_map/ppermute | solution.py:45
  3.4 0.5 %collective-permute-start.1 = (bf16[256,256]{1,0:T(8,128)(2,1)}, bf16[256,256]{1,0:T(8,128)(2,1)S(1)}, u32[]{:S(2)}, u32[]{:S(2)}) collective-permute-start(bf16[256,256]{1,0:T(8,128)(2,1)} %values_in.1), channel_id=1, source_target_pairs={{0,4},{1,5},{2,6},{3,7},{4,0},{5,1},{6,2},{7,3},{8,12},{9,13},{10,... | collective-permute-start | bytes 393224 | tf_op jit(solution)/shard_map/ppermute | solution.py:45
  3.9 1.6 %attend_first.1 = (f32[1024,128]{1,0:T(8,128)S(1)}, f32[1024,128]{1,0:T(8,128)S(1)}, f32[1024,128]{1,0:T(8,128)S(1)}, bf16[256,512]{1,0:T(8,128)(2,1)S(1)}, f32[16,256]{1,0:T(8,128)S(1)}) custom-call(s32[16]{0:T(128)} %docs_in.1, bf16[256,512]{1,0:T(8,128)(2,1)} %queries_in.1, bf16[256,256]{1,0:T(8,128)(2,1)} %keys_in.1, bf16[256,256]{1,0:T(8,128)(2,1)} %values_in.1), custom_call_target="tpu_custom_call" | custom-call | flops 134217728 | tf_op jit(solution)/shard_map/attend_first/pallas_call | solution.py:201
  5.6 1.0 %collective-permute-done.2.refs_5_ = bf16[256,256]{1,0:T(8,128)(2,1)S(1)} collective-permute-done((bf16[256,256]{1,0:T(8,128)(2,1)}, bf16[256,256]{1,0:T(8,128)(2,1)S(1)}, u32[]{:S(2)}, u32[]{:S(2)}) %collective-permute-start.2) | collective-permute-done | bytes 131104 | tf_op jit(solution)/shard_map/ppermute | solution.py:45
  6.6 2.0 %collective-permute-start.6 = (bf16[256,256]{1,0:T(8,128)(2,1)S(1)}, bf16[256,256]{1,0:T(8,128)(2,1)S(1)}, u32[]{:S(2)}, u32[]{:S(2)}) collective-permute-start(bf16[256,256]{1,0:T(8,128)(2,1)S(1)} %collective-permute-done.2.refs_5_), channel_id=1, source_target_pairs={{0,1},{1,0},{2,3},{3,2},{4,5},{5,4},{6,7},{7,6},{8,12},{9,13},{10,... | collective-permute-start | bytes 393224 | tf_op jit(solution)/shard_map/ppermute | solution.py:45
  8.6 0.8 %collective-permute-done.3.refs_6_ = bf16[256,256]{1,0:T(8,128)(2,1)S(1)} collective-permute-done((bf16[256,256]{1,0:T(8,128)(2,1)}, bf16[256,256]{1,0:T(8,128)(2,1)S(1)}, u32[]{:S(2)}, u32[]{:S(2)}) %collective-permute-start.3) | collective-permute-done | bytes 131104 | tf_op jit(solution)/shard_map/ppermute | solution.py:45
  9.4 0.7 %collective-permute-start.5 = (bf16[256,256]{1,0:T(8,128)(2,1)S(1)}, bf16[256,256]{1,0:T(8,128)(2,1)S(1)}, u32[]{:S(2)}, u32[]{:S(2)}) collective-permute-start(bf16[256,256]{1,0:T(8,128)(2,1)S(1)} %collective-permute-done.3.refs_6_), channel_id=1, source_target_pairs={{0,1},{1,0},{2,3},{3,2},{4,5},{5,4},{6,7},{7,6},{8,16},{9,17},{10,... | collective-permute-start | bytes 393224 | tf_op jit(solution)/shard_map/ppermute | solution.py:45
  10.2 0.8 %collective-permute-start.7 = (bf16[256,256]{1,0:T(8,128)(2,1)S(1)}, bf16[256,256]{1,0:T(8,128)(2,1)S(1)}, u32[]{:S(2)}, u32[]{:S(2)}) collective-permute-start(bf16[256,256]{1,0:T(8,128)(2,1)S(1)} %collective-permute-done.3.refs_6_), channel_id=1, source_target_pairs={{0,1},{1,0},{2,3},{3,2},{4,5},{5,4},{6,7},{7,6},{8,12},{9,13},{10,... | collective-permute-start | bytes 393224 | tf_op jit(solution)/shard_map/ppermute | solution.py:45
  10.9 1.7 %collective-permute-done.4.refs_7_ = bf16[256,256]{1,0:T(8,128)(2,1)S(1)} collective-permute-done((bf16[256,256]{1,0:T(8,128)(2,1)S(1)}, bf16[256,256]{1,0:T(8,128)(2,1)S(1)}, u32[]{:S(2)}, u32[]{:S(2)}) %collective-permute-start.4) | collective-permute-done | bytes 131104 | tf_op jit(solution)/shard_map/ppermute | solution.py:45
  12.6 0.2 collective-permute-done.6.refs_3_
  12.8 1.6 %collective-permute-start.8 = (bf16[256,256]{1,0:T(8,128)(2,1)S(1)}, bf16[256,256]{1,0:T(8,128)(2,1)S(1)}, u32[]{:S(2)}, u32[]{:S(2)}) collective-permute-start(bf16[256,256]{1,0:T(8,128)(2,1)S(1)} %collective-permute-done.6.refs_3_), channel_id=1, source_target_pairs={{0,1},{1,0},{2,3},{3,2},{4,5},{5,4},{6,7},{7,6},{8,16},{9,17},{10,... | collective-permute-start | bytes 393224 | tf_op jit(solution)/shard_map/ppermute | solution.py:45
  14.4 1.1 %collective-permute-done.5.refs_8_ = bf16[256,256]{1,0:T(8,128)(2,1)S(1)} collective-permute-done((bf16[256,256]{1,0:T(8,128)(2,1)S(1)}, bf16[256,256]{1,0:T(8,128)(2,1)S(1)}, u32[]{:S(2)}, u32[]{:S(2)}) %collective-permute-start.5) | collective-permute-done | bytes 131104 | tf_op jit(solution)/shard_map/ppermute | solution.py:45
  15.5 1.5 %collective-permute-start.9 = (bf16[256,256]{1,0:T(8,128)(2,1)S(1)}, bf16[256,256]{1,0:T(8,128)(2,1)S(1)}, u32[]{:S(2)}, u32[]{:S(2)}) collective-permute-start(bf16[256,256]{1,0:T(8,128)(2,1)S(1)} %collective-permute-done.5.refs_8_), channel_id=1, source_target_pairs={{0,1},{1,0},{2,3},{3,2},{4,5},{5,4},{6,7},{7,6},{8,9},{9,8},{10,11... | collective-permute-start | bytes 393224 | tf_op jit(solution)/shard_map/ppermute | solution.py:45
  17.0 2.6 %attend_next.1 = (f32[1024,128]{1,0:T(8,128)S(1)}, f32[1024,128]{1,0:T(8,128)S(1)}, f32[1024,128]{1,0:T(8,128)S(1)}, bf16[512,5376]{1,0:T(8,128)(2,1)S(1)}) custom-call(bf16[256,512]{1,0:T(8,128)(2,1)S(1)} %get-tuple-element.34.queries, f32[16,256]{1,0:T(8,128)S(1)} %get-tuple-element.35.open_beside, bf16[512,5376]{1,0:T(8,128)(2,1)} %weight_in.1, ...), custom_call_target="tpu_custom_call" | custom-call | flops 402653184 | bytes 5505024 | tf_op jit(solution)/shard_map/attend_next/pallas_call | solution.py:223
  19.6 0.9 %collective-permute-done.9.refs_6_ = bf16[256,256]{1,0:T(8,128)(2,1)S(1)} collective-permute-done((bf16[256,256]{1,0:T(8,128)(2,1)S(1)}, bf16[256,256]{1,0:T(8,128)(2,1)S(1)}, u32[]{:S(2)}, u32[]{:S(2)}) %collective-permute-start.9) | collective-permute-done | bytes 131104 | tf_op jit(solution)/shard_map/ppermute | solution.py:45
  20.4 1.6 %attend_last.1 = (bf16[128,512]{1,0:T(8,128)(2,1)S(1)}, bf16[128,512]{1,0:T(8,128)(2,1)S(1)}, f32[64,3072]{1,0:T(8,128)S(1)}, bf16[64,3072]{1,0:T(8,128)(2,1)S(1)}) custom-call(bf16[256,512]{1,0:T(8,128)(2,1)S(1)} %get-tuple-element.34.queries, bf16[512,5376]{1,0:T(8,128)(2,1)S(1)} %get-tuple-element.41.weight, f32[1024,128]{1,0:T(8,128)S(1)} %get-tuple-element.42.refs_0_, ...), custom_call_target="tpu_custom_call" | custom-call | flops 268435456 | tf_op jit(solution)/shard_map/attend_last/pallas_call | solution.py:266
  22.1 0.5 %project.2 = (f32[64,2304]{1,0:T(8,128)S(1)}, bf16[64,2304]{1,0:T(8,128)(2,1)S(1)}) custom-call(bf16[128,512]{1,0:T(8,128)(2,1)S(1)} %get-tuple-element.51.rows, bf16[512,5376]{1,0:T(8,128)(2,1)S(1)} %get-tuple-element.41.weight), custom_call_target="tpu_custom_call" | custom-call | flops 301989888 | tf_op jit(solution)/shard_map/project/pallas_call | solution.py:301
  22.6 0.6 %collective-permute-start.11 = (bf16[64,2304]{1,0:T(8,128)(2,1)S(1)}, bf16[64,2304]{1,0:T(8,128)(2,1)S(1)}, u32[]{:S(2)}, u32[]{:S(2)}) collective-permute-start(bf16[64,2304]{1,0:T(8,128)(2,1)S(1)} %get-tuple-element.57), channel_id=1, source_target_pairs={{0,1},{1,0},{2,3},{3,2},{4,5},{5,4},{6,7},{7,6},{8,9},{9,8},{10,11... | collective-permute-start | bytes 884744 | tf_op jit(solution)/shard_map/ppermute | solution.py:22
  23.2 0.7 %collective-permute-done.10.theirs = bf16[64,3072]{1,0:T(8,128)(2,1)S(1)} collective-permute-done((bf16[64,3072]{1,0:T(8,128)(2,1)S(1)}, bf16[64,3072]{1,0:T(8,128)(2,1)S(1)}, u32[]{:S(2)}, u32[]{:S(2)}) %collective-permute-start.10) | collective-permute-done | bytes 393248 | tf_op jit(solution)/shard_map/ppermute | solution.py:22
  23.9 1.6 %collective-permute-start.16 = (bf16[64,3072]{1,0:T(8,128)(2,1)S(1)}, bf16[64,3072]{1,0:T(8,128)(2,1)S(1)}, u32[]{:S(2)}, u32[]{:S(2)}) collective-permute-start(bf16[64,3072]{1,0:T(8,128)(2,1)S(1)} %add_up.2), channel_id=1, source_target_pairs={{0,2},{1,3},{2,0},{3,1},{4,6},{5,7},{6,4},{7,5},{8,10},{9,11},{10,... | collective-permute-start | bytes 1179656 | tf_op jit(solution)/shard_map/ppermute | solution.py:22
  25.5 0.6 %collective-permute-start.12 = (bf16[64,2304]{1,0:T(8,128)(2,1)S(1)}, bf16[64,2304]{1,0:T(8,128)(2,1)S(1)}, u32[]{:S(2)}, u32[]{:S(2)}) collective-permute-start(bf16[64,2304]{1,0:T(8,128)(2,1)S(1)} %add_up.3), channel_id=1, source_target_pairs={{0,2},{1,3},{2,0},{3,1},{4,6},{5,7},{6,4},{7,5},{8,10},{9,11},{10,... | collective-permute-start | bytes 884744 | tf_op jit(solution)/shard_map/ppermute | solution.py:22
  26.1 0.9 %project.3 = (f32[64,5376]{1,0:T(8,128)S(1)}, bf16[64,1792]{1,0:T(8,128)(2,1)S(1)}, bf16[64,1792]{1,0:T(8,128)(2,1)S(1)}, bf16[64,1792]{1,0:T(8,128)(2,1)S(1)}) custom-call(bf16[128,512]{1,0:T(8,128)(2,1)S(1)} %get-tuple-element.58.rows, bf16[512,5376]{1,0:T(8,128)(2,1)S(1)} %get-tuple-element.41.weight), custom_call_target="tpu_custom_call" | custom-call | flops 704643072 | tf_op jit(solution)/shard_map/project/pallas_call | solution.py:301
  27.1 0.5 %collective-permute-start.14 = (bf16[64,1792]{1,0:T(8,128)(2,1)S(1)}, bf16[64,1792]{1,0:T(8,128)(2,1)S(1)}, u32[]{:S(2)}, u32[]{:S(2)}) collective-permute-start(bf16[64,1792]{1,0:T(8,128)(2,1)S(1)} %get-tuple-element.61), channel_id=1, source_target_pairs={{0,1},{1,0},{2,3},{3,2},{4,5},{5,4},{6,7},{7,6},{8,9},{9,8},{10,11... | collective-permute-start | bytes 688136 | tf_op jit(solution)/shard_map/ppermute | solution.py:22
  27.6 0.1 collective-permute-start.15
  27.7 0.9 %collective-permute-done.13.refs_0_ = bf16[64,1792]{1,0:T(8,128)(2,1)S(1)} collective-permute-done((bf16[64,1792]{1,0:T(8,128)(2,1)S(1)}, bf16[64,1792]{1,0:T(8,128)(2,1)S(1)}, u32[]{:S(2)}, u32[]{:S(2)}) %collective-permute-start.13) | collective-permute-done | bytes 229408 | tf_op jit(solution)/shard_map/ppermute | solution.py:22
  28.6 0.3 collective-permute-done.14.refs_1_
  28.9 0.3 collective-permute-done.15.refs_2_
  29.2 6.7 %collective-permute-done.16.across = bf16[64,3072]{1,0:T(8,128)(2,1)S(1)} collective-permute-done((bf16[64,3072]{1,0:T(8,128)(2,1)S(1)}, bf16[64,3072]{1,0:T(8,128)(2,1)S(1)}, u32[]{:S(2)}, u32[]{:S(2)}) %collective-permute-start.16) | collective-permute-done | bytes 393248 | tf_op jit(solution)/shard_map/ppermute | solution.py:22
  35.9 0.9 %combine.2.refs_3_ = bf16[64,5376]{1,0:T(8,128)(2,1)} custom-call(f32[64,5376]{1,0:T(8,128)S(1)} %get-tuple-element.59.mine, bf16[64,3072]{1,0:T(8,128)(2,1)S(1)} %collective-permute-done.16.across, bf16[64,1792]{1,0:T(8,128)(2,1)S(1)} %collective-permute-done.13.refs_0_, bf16[64,1792]{1,0:T(8,128)(2,1)S(1)} %collective-permute-done.14.refs_1_, ...), custom_call_target="tpu_custom_call" | custom-call | tf_op jit(solution)/shard_map/combine/pallas_call | solution.py:348
  36.8 4.6 %collective-permute-done.12.across = bf16[64,2304]{1,0:T(8,128)(2,1)S(1)} collective-permute-done((bf16[64,2304]{1,0:T(8,128)(2,1)S(1)}, bf16[64,2304]{1,0:T(8,128)(2,1)S(1)}, u32[]{:S(2)}, u32[]{:S(2)}) %collective-permute-start.12) | collective-permute-done | bytes 294944 | tf_op jit(solution)/shard_map/ppermute | solution.py:22
  41.5 0.8 %combine.3 = bf16[64,5376]{1,0:T(8,128)(2,1)} custom-call(f32[64,5376]{1,0:T(8,128)S(1)} %get-tuple-element.59.mine, bf16[64,2304]{1,0:T(8,128)(2,1)S(1)} %collective-permute-done.12.across, bf16[64,1792]{1,0:T(8,128)(2,1)S(1)} %collective-permute-done.13.refs_0_, ...), custom_call_target="tpu_custom_call", output_to_operand_aliasing={{}: (5, {})} | custom-call | tf_op jit(solution)/shard_map/combine/pallas_call | solution.py:348
  (11 shorter events, 0.3 us)
Async XLA Ops:
  0.0 6.6 %collective-permute-start.2 = (bf16[256,256]{1,0:T(8,128)(2,1)}, bf16[256,256]{1,0:T(8,128)(2,1)S(1)}, u32[]{:S(2)}, u32[]{:S(2)}) collective-permute-start(bf16[256,256]{1,0:T(8,128)(2,1)} %keys_in.1), channel_id=1, source_target_pairs={{0,8},{1,9},{2,10},{3,11},{4,12},{5,13},{6,14},{7,15},{8,16},{9,17... | collective-permute-start | bytes 393224 | tf_op jit(solution)/shard_map/ppermute | solution.py:45
  0.0 6.6 %collective-permute-start = (bf16[256,256]{1,0:T(8,128)(2,1)}, bf16[256,256]{1,0:T(8,128)(2,1)S(1)}, u32[]{:S(2)}, u32[]{:S(2)}) collective-permute-start(bf16[256,256]{1,0:T(8,128)(2,1)} %keys_in.1), channel_id=1, source_target_pairs={{0,4},{1,5},{2,6},{3,7},{4,0},{5,1},{6,2},{7,3},{8,12},{9,13},{10,... | collective-permute-start | bytes 393224 | tf_op jit(solution)/shard_map/ppermute | solution.py:45
  1.9 7.5 %collective-permute-start.3 = (bf16[256,256]{1,0:T(8,128)(2,1)}, bf16[256,256]{1,0:T(8,128)(2,1)S(1)}, u32[]{:S(2)}, u32[]{:S(2)}) collective-permute-start(bf16[256,256]{1,0:T(8,128)(2,1)} %values_in.1), channel_id=1, source_target_pairs={{0,8},{1,9},{2,10},{3,11},{4,12},{5,13},{6,14},{7,15},{8,16},{9,17... | collective-permute-start | bytes 393224 | tf_op jit(solution)/shard_map/ppermute | solution.py:45
  3.4 6.7 %collective-permute-start.1 = (bf16[256,256]{1,0:T(8,128)(2,1)}, bf16[256,256]{1,0:T(8,128)(2,1)S(1)}, u32[]{:S(2)}, u32[]{:S(2)}) collective-permute-start(bf16[256,256]{1,0:T(8,128)(2,1)} %values_in.1), channel_id=1, source_target_pairs={{0,4},{1,5},{2,6},{3,7},{4,0},{5,1},{6,2},{7,3},{8,12},{9,13},{10,... | collective-permute-start | bytes 393224 | tf_op jit(solution)/shard_map/ppermute | solution.py:45
  6.6 6.0 %collective-permute-start.4 = (bf16[256,256]{1,0:T(8,128)(2,1)S(1)}, bf16[256,256]{1,0:T(8,128)(2,1)S(1)}, u32[]{:S(2)}, u32[]{:S(2)}) collective-permute-start(bf16[256,256]{1,0:T(8,128)(2,1)S(1)} %collective-permute-done.2.refs_5_), channel_id=1, source_target_pairs={{0,1},{1,0},{2,3},{3,2},{4,5},{5,4},{6,7},{7,6},{8,16},{9,17},{10,... | collective-permute-start | bytes 393224 | tf_op jit(solution)/shard_map/ppermute | solution.py:45
  6.6 6.2 %collective-permute-start.6 = (bf16[256,256]{1,0:T(8,128)(2,1)S(1)}, bf16[256,256]{1,0:T(8,128)(2,1)S(1)}, u32[]{:S(2)}, u32[]{:S(2)}) collective-permute-start(bf16[256,256]{1,0:T(8,128)(2,1)S(1)} %collective-permute-done.2.refs_5_), channel_id=1, source_target_pairs={{0,1},{1,0},{2,3},{3,2},{4,5},{5,4},{6,7},{7,6},{8,12},{9,13},{10,... | collective-permute-start | bytes 393224 | tf_op jit(solution)/shard_map/ppermute | solution.py:45
  9.4 6.1 %collective-permute-start.5 = (bf16[256,256]{1,0:T(8,128)(2,1)S(1)}, bf16[256,256]{1,0:T(8,128)(2,1)S(1)}, u32[]{:S(2)}, u32[]{:S(2)}) collective-permute-start(bf16[256,256]{1,0:T(8,128)(2,1)S(1)} %collective-permute-done.3.refs_6_), channel_id=1, source_target_pairs={{0,1},{1,0},{2,3},{3,2},{4,5},{5,4},{6,7},{7,6},{8,16},{9,17},{10,... | collective-permute-start | bytes 393224 | tf_op jit(solution)/shard_map/ppermute | solution.py:45
  10.2 9.4 %collective-permute-start.7 = (bf16[256,256]{1,0:T(8,128)(2,1)S(1)}, bf16[256,256]{1,0:T(8,128)(2,1)S(1)}, u32[]{:S(2)}, u32[]{:S(2)}) collective-permute-start(bf16[256,256]{1,0:T(8,128)(2,1)S(1)} %collective-permute-done.3.refs_6_), channel_id=1, source_target_pairs={{0,1},{1,0},{2,3},{3,2},{4,5},{5,4},{6,7},{7,6},{8,12},{9,13},{10,... | collective-permute-start | bytes 393224 | tf_op jit(solution)/shard_map/ppermute | solution.py:45
  12.8 6.8 %collective-permute-start.8 = (bf16[256,256]{1,0:T(8,128)(2,1)S(1)}, bf16[256,256]{1,0:T(8,128)(2,1)S(1)}, u32[]{:S(2)}, u32[]{:S(2)}) collective-permute-start(bf16[256,256]{1,0:T(8,128)(2,1)S(1)} %collective-permute-done.6.refs_3_), channel_id=1, source_target_pairs={{0,1},{1,0},{2,3},{3,2},{4,5},{5,4},{6,7},{7,6},{8,16},{9,17},{10,... | collective-permute-start | bytes 393224 | tf_op jit(solution)/shard_map/ppermute | solution.py:45
  15.5 5.0 %collective-permute-start.9 = (bf16[256,256]{1,0:T(8,128)(2,1)S(1)}, bf16[256,256]{1,0:T(8,128)(2,1)S(1)}, u32[]{:S(2)}, u32[]{:S(2)}) collective-permute-start(bf16[256,256]{1,0:T(8,128)(2,1)S(1)} %collective-permute-done.5.refs_8_), channel_id=1, source_target_pairs={{0,1},{1,0},{2,3},{3,2},{4,5},{5,4},{6,7},{7,6},{8,9},{9,8},{10,11... | collective-permute-start | bytes 393224 | tf_op jit(solution)/shard_map/ppermute | solution.py:45
  22.1 1.8 %collective-permute-start.10 = (bf16[64,3072]{1,0:T(8,128)(2,1)S(1)}, bf16[64,3072]{1,0:T(8,128)(2,1)S(1)}, u32[]{:S(2)}, u32[]{:S(2)}) collective-permute-start(bf16[64,3072]{1,0:T(8,128)(2,1)S(1)} %get-tuple-element.55), channel_id=1, source_target_pairs={{0,1},{1,0},{2,3},{3,2},{4,5},{5,4},{6,7},{7,6},{8,9},{9,8},{10,11... | collective-permute-start | bytes 1179656 | tf_op jit(solution)/shard_map/ppermute | solution.py:22
  22.6 2.8 %collective-permute-start.11 = (bf16[64,2304]{1,0:T(8,128)(2,1)S(1)}, bf16[64,2304]{1,0:T(8,128)(2,1)S(1)}, u32[]{:S(2)}, u32[]{:S(2)}) collective-permute-start(bf16[64,2304]{1,0:T(8,128)(2,1)S(1)} %get-tuple-element.57), channel_id=1, source_target_pairs={{0,1},{1,0},{2,3},{3,2},{4,5},{5,4},{6,7},{7,6},{8,9},{9,8},{10,11... | collective-permute-start | bytes 884744 | tf_op jit(solution)/shard_map/ppermute | solution.py:22
  23.9 12.0 %collective-permute-start.16 = (bf16[64,3072]{1,0:T(8,128)(2,1)S(1)}, bf16[64,3072]{1,0:T(8,128)(2,1)S(1)}, u32[]{:S(2)}, u32[]{:S(2)}) collective-permute-start(bf16[64,3072]{1,0:T(8,128)(2,1)S(1)} %add_up.2), channel_id=1, source_target_pairs={{0,2},{1,3},{2,0},{3,1},{4,6},{5,7},{6,4},{7,5},{8,10},{9,11},{10,... | collective-permute-start | bytes 1179656 | tf_op jit(solution)/shard_map/ppermute | solution.py:22
  25.5 15.9 %collective-permute-start.12 = (bf16[64,2304]{1,0:T(8,128)(2,1)S(1)}, bf16[64,2304]{1,0:T(8,128)(2,1)S(1)}, u32[]{:S(2)}, u32[]{:S(2)}) collective-permute-start(bf16[64,2304]{1,0:T(8,128)(2,1)S(1)} %add_up.3), channel_id=1, source_target_pairs={{0,2},{1,3},{2,0},{3,1},{4,6},{5,7},{6,4},{7,5},{8,10},{9,11},{10,... | collective-permute-start | bytes 884744 | tf_op jit(solution)/shard_map/ppermute | solution.py:22
  27.0 1.6 %collective-permute-start.13 = (bf16[64,1792]{1,0:T(8,128)(2,1)S(1)}, bf16[64,1792]{1,0:T(8,128)(2,1)S(1)}, u32[]{:S(2)}, u32[]{:S(2)}) collective-permute-start(bf16[64,1792]{1,0:T(8,128)(2,1)S(1)} %get-tuple-element.60), channel_id=1, source_target_pairs={{0,1},{1,0},{2,3},{3,2},{4,5},{5,4},{6,7},{7,6},{8,9},{9,8},{10,11... | collective-permute-start | bytes 688136 | tf_op jit(solution)/shard_map/ppermute | solution.py:22
  27.1 1.8 %collective-permute-start.14 = (bf16[64,1792]{1,0:T(8,128)(2,1)S(1)}, bf16[64,1792]{1,0:T(8,128)(2,1)S(1)}, u32[]{:S(2)}, u32[]{:S(2)}) collective-permute-start(bf16[64,1792]{1,0:T(8,128)(2,1)S(1)} %get-tuple-element.61), channel_id=1, source_target_pairs={{0,1},{1,0},{2,3},{3,2},{4,5},{5,4},{6,7},{7,6},{8,9},{9,8},{10,11... | collective-permute-start | bytes 688136 | tf_op jit(solution)/shard_map/ppermute | solution.py:22
  27.6 1.6 %collective-permute-start.15 = (bf16[64,1792]{1,0:T(8,128)(2,1)S(1)}, bf16[64,1792]{1,0:T(8,128)(2,1)S(1)}, u32[]{:S(2)}, u32[]{:S(2)}) collective-permute-start(bf16[64,1792]{1,0:T(8,128)(2,1)S(1)} %get-tuple-element.62), channel_id=1, source_target_pairs={{0,1},{1,0},{2,3},{3,2},{4,5},{5,4},{6,7},{7,6},{8,9},{9,8},{10,11... | collective-permute-start | bytes 688136 | tf_op jit(solution)/shard_map/ppermute | solution.py:22

commit v3 on v2

--- a/solution.py
+++ b/solution.py
@@ -32,16 +32,17 @@
 AGAIN = ((2, 4), (3, 5))
 ACROSS = ((2, 3), (4, 5))
 LAST = ((4, 5),)
-
-
-def move(block, rings):
+EARLY = (0, 1, 6, 7)
+RELAY = ((0, 2), (1, 3), (4, 6), (5, 7))
+
+
+def move(block, rings, crossing=()):
     n_ctx, heads = lax.axis_size("ctx"), lax.axis_size("head")
     target = {ring[i]: ring[(i + 1) % len(ring)] for ring in rings for i in range(len(ring))}
-    pairs = [
-        (i * heads + h, target[i] * heads + h if i in target else i * heads + (h ^ 1))
-        for i in range(n_ctx)
-        for h in range(heads)
-    ]
+    pairs = []
+    for i in range(n_ctx):
+        flip = 0 if i in target else 2 if i in crossing else 1
+        pairs += [(i * heads + h, target.get(i, i) * heads + (h ^ flip)) for h in range(heads)]
     return lax.ppermute(block, ("ctx", "head"), pairs)
 
 
@@ -311,50 +312,73 @@
     )(rows, weight)
 
 
-def add_kernel(mine, theirs, out):
-    out[...] = (mine[...] + theirs[...].astype(jnp.float32)).astype(out.dtype)
-
-
-def add_up(mine, theirs):
+def add_kernel(mine, theirs, *outs):
+    at = 0
+    for out in outs:
+        columns = slice(at, at + out.shape[1])
+        at += out.shape[1]
+        out[...] = (mine[:, columns] + theirs[:, columns].astype(jnp.float32)).astype(out.dtype)
+
+
+def add_up(mine, theirs, widths):
     return pl.pallas_call(
         add_kernel,
-        out_shape=jax.ShapeDtypeStruct(theirs.shape, theirs.dtype),
+        out_shape=[jax.ShapeDtypeStruct((mine.shape[0], width), theirs.dtype) for width in widths],
         in_specs=[VMEM, VMEM],
-        out_specs=VMEM,
+        out_specs=[VMEM] * len(widths),
         compiler_params=LIMIT,
         cost_estimate=pl.CostEstimate(flops=theirs.size, bytes_accessed=0, transcendentals=0),
         name="add_up",
     )(mine, theirs)
 
 
-def combine_kernel(at, mine, across, *refs):
-    *beside, out, total, sem = refs
-    width = across.shape[1]
-    left = 0
-    for part in beside[: len(beside) - (at > 0)]:
-        low, high = max(left, at), min(left + part.shape[1], at + width)
-        if low < high:
-            piece = mine[:, low:high] + part[:, low - left : high - left].astype(jnp.float32)
-            piece += across[:, low - at : high - at].astype(jnp.float32)
-            total[:, low - at : high - at] = piece.astype(total.dtype)
-        left += part.shape[1]
-    copy = pltpu.make_async_copy(total, out.at[:, at : at + width], sem)
-    copy.start()
-    copy.wait()
-
-
-def combine(mine, beside, across, at=0, out=None):
+def combine_kernel(cuts, counts, mine, *refs):
+    across, refs = refs[: sum(counts)], refs[sum(counts) :]
+    beside, (out, *totals, sems) = refs[: len(refs) - len(cuts) - 2], refs[len(refs) - len(cuts) - 2 :]
+    copies = []
+    for i, (at, total) in enumerate(zip(cuts, totals)):
+        options = across[sum(counts[:i]) : sum(counts[: i + 1])]
+        width = options[0].shape[1]
+        left = 0
+        for part in beside:
+            low, high = max(left, at), min(left + part.shape[1], at + width)
+            if low < high:
+                piece = mine[:, low:high] + part[:, low - left : high - left].astype(jnp.float32)
+                there = options[0][:, low - at : high - at].astype(jnp.float32)
+                if len(options) == 2:
+                    position = lax.axis_index("ctx")
+                    early = functools.reduce(jnp.logical_or, [position == i for i in EARLY])
+                    relayed = options[1][:, low - at : high - at].astype(jnp.float32)
+                    there = jnp.where(early, there, relayed)
+                total[:, low - at : high - at] = (piece + there).astype(total.dtype)
+            left += part.shape[1]
+        copies.append(pltpu.make_async_copy(total, out.at[:, at : at + width], sems.at[i]))
+        copies[-1].start()
+    for copy in copies:
+        copy.wait()
+
+
+def combine(mine, beside, across, cuts, out=None):
     outs = [] if out is None else [out]
+    across = [x if isinstance(x, tuple) else (x,) for x in across]
+    arrays = [x for options in across for x in options]
+    counts = [len(options) for options in across]
+    inputs = 1 + len(arrays) + len(beside)
+
+    def kernel(*refs):
+        combine_kernel(cuts, counts, *refs[:inputs], *refs[inputs + len(outs) :])
+
     return pl.pallas_call(
-        functools.partial(combine_kernel, at),
-        out_shape=jax.ShapeDtypeStruct(mine.shape, across.dtype),
-        in_specs=[VMEM] * (2 + len(beside)) + [HBM] * len(outs),
+        kernel,
+        out_shape=jax.ShapeDtypeStruct(mine.shape, jnp.bfloat16),
+        in_specs=[VMEM] * inputs + [HBM] * len(outs),
         out_specs=HBM,
-        scratch_shapes=[pltpu.VMEM(across.shape, across.dtype), pltpu.SemaphoreType.DMA],
-        input_output_aliases={2 + len(beside): 0} if outs else {},
+        scratch_shapes=[pltpu.VMEM(options[0].shape, jnp.bfloat16) for options in across]
+        + [pltpu.SemaphoreType.DMA((len(cuts),))],
+        input_output_aliases={inputs: 0} if outs else {},
         compiler_params=LIMIT,
         name="combine",
-    )(mine, across, *beside, *outs)
+    )(mine, *arrays, *beside, *outs)
 
 
 def from_behind(block, axis, distance):
@@ -444,7 +468,8 @@
     other_core = [(i, i ^ 1) for i in range(heads)]
     other_chip = [(i, i ^ 2) for i in range(heads)]
     columns = out_weight.shape[1]
-    cut = columns * 4 // 7 // BLOCK * BLOCK
+    relay = columns // 8 // BLOCK * BLOCK
+    cuts = [0, columns * 2 // 7 // BLOCK * BLOCK, columns * 2 // 7 // BLOCK * BLOCK + relay]
 
     if n_ctx == 8:
         by_two = [move(x, BY_TWO) for x in (keys, values)]
@@ -459,26 +484,30 @@
         chunks = [beside, by_two, by_four]
         *state, weight = attend_next(fetched, open_beside, out_weight, state, chunks, (1, 2, 3))
         chunks = [swap_two, swap_four]
-        far, near, mine, send = attend_last(fetched, weight, state, chunks, (4, 5), (0, cut))
+        far, near, mine, send = attend_last(fetched, weight, state, chunks, (4, 5), (0, cuts[2]))
     else:
         weight = out_weight
         attended = ring_attention(queries, keys, values, doc_ids, n_ctx, position)
         far, near = part_rows(attended, place)
-        mine, send = project(far, weight, (0, cut))
+        mine, send = project(far, weight, (0, cuts[2]))
     theirs = hop(send, "head", other_core)
-    later_mine, later_send = project(far, weight, (cut, columns))
-    mine, later_mine = lax.optimization_barrier((mine, later_mine))
-    first_sum = add_up(mine, theirs)
+    later_mine, later_send = project(far, weight, (cuts[2], columns))
+    first_sum, relay_sum = add_up(mine, theirs, [cuts[1], cuts[2] - cuts[1]])
     first_part = hop(first_sum, "head", other_chip)
-    later_theirs = hop(later_send, "head", other_core)
-    later_mine, first_sum = lax.optimization_barrier((later_mine, first_sum))
-    later_sum = add_up(later_mine, later_theirs)
-    second_part = hop(later_sum, "head", other_chip)
-    near, later_sum = lax.optimization_barrier((near, later_sum))
-    mine, *sends = project(near, weight, (0, columns), 3)
+    later_theirs = hop(after(later_send, relay_sum), "head", other_core)
+    later_mine = after(later_mine, first_sum)
+    (later_sum,) = add_up(later_mine, later_theirs, [columns - cuts[2]])
+    later_part = hop(later_sum, "head", other_chip)
+    mine, *sends = project(after(near, later_sum), weight, (0, columns), 4)
     theirs = [hop(send, "head", other_core) for send in sends]
-    out = combine(mine, theirs, first_part)
-    return combine(mine, theirs, second_part, cut, out)
+    if n_ctx == 8:
+        direct = move(relay_sum, (), EARLY)
+        arrived = move(after(relay_sum, mine), RELAY)
+        relay_part = (direct, move(move(after(after(arrived, first_part), direct), (), EARLY), RELAY))
+    else:
+        relay_part = hop(relay_sum, "head", other_chip)
+    out = combine(mine, theirs, [first_part], [0])
+    return combine(mine, theirs, [later_part, relay_part], [cuts[2], cuts[1]], out)
 
 
 def solution(mesh):

time: 42.4 us -> 47.5 us (1.12)
  the two profiles are of different devices: /device:TPU:16 before, /device:TPU:0 now
where the time goes in v3:
time: 47.5 us; the launch traced here: 47.4 us
  starting transfers between devices  20 us (42%)
  waiting for transfers between devices  17.4 us (37%)
  Pallas kernels  9.78 us (21%)
    ppermute x14, starting transfers between devices, move(): return lax.ppermute(block, ('ctx', 'head'), pairs)  15.7 us
    ppermute x14, waiting for transfers between devices, move(): return lax.ppermute(block, ('ctx', 'head'), pairs)  15.4 us
    ppermute x8, starting transfers between devices, hop(): return lax.ppermute(block, axis, pairs)  4.33 us
    pallas_call x1, Pallas kernels, attend_next(): pl.pallas_call(functools.partial(next_kernel, numbers), out_shape=state_s...  2.59 us
    pallas_call x2, Pallas kernels, project(): pl.pallas_call(functools.partial(project_kernel, columns), out_shape=proj...  2.14 us
    ppermute x8, waiting for transfers between devices, hop(): return lax.ppermute(block, axis, pairs)  1.97 us
    pallas_call x2, Pallas kernels, combine(): pl.pallas_call(kernel, out_shape=jax.ShapeDtypeStruct(mine.shape, jnp.bfl...  1.83 us
    pallas_call x1, Pallas kernels, attend_first(): pl.pallas_call(first_kernel, out_shape=state_shapes(queries) + (pltpu.VME...  1.6 us
  transfers between devices with their start and end apart: 22, of which 9 were waited for; matrix products, arithmetic and copies ran while one was open for 0% of the time, Pallas kernels for 15%

profile of v3, /device:TPU:0, one launch (start us, length us, event | category | flops | bytes accessed | tf_op | source)
XLA Modules:
  0.0 47.4 jit_solution(11154304659923156418)
XLA Ops:
  0.0 3.0 %collective-permute-start.2 = (bf16[256,256]{1,0:T(8,128)(2,1)}, bf16[256,256]{1,0:T(8,128)(2,1)S(1)}, u32[]{:S(2)}, u32[]{:S(2)}) collective-permute-start(bf16[256,256]{1,0:T(8,128)(2,1)} %keys_in.1), channel_id=1, source_target_pairs={{0,8},{1,9},{2,10},{3,11},{4,12},{5,13},{6,14},{7,15},{8,16},{9,17... | collective-permute-start | bytes 393224 | tf_op jit(solution)/shard_map/ppermute | solution.py:46
  3.0 1.5 %collective-permute-start = (bf16[256,256]{1,0:T(8,128)(2,1)}, bf16[256,256]{1,0:T(8,128)(2,1)S(1)}, u32[]{:S(2)}, u32[]{:S(2)}) collective-permute-start(bf16[256,256]{1,0:T(8,128)(2,1)} %keys_in.1), channel_id=1, source_target_pairs={{0,4},{1,5},{2,6},{3,7},{4,0},{5,1},{6,2},{7,3},{8,12},{9,13},{10,... | collective-permute-start | bytes 393224 | tf_op jit(solution)/shard_map/ppermute | solution.py:46
  4.5 1.6 %collective-permute-start.3 = (bf16[256,256]{1,0:T(8,128)(2,1)}, bf16[256,256]{1,0:T(8,128)(2,1)S(1)}, u32[]{:S(2)}, u32[]{:S(2)}) collective-permute-start(bf16[256,256]{1,0:T(8,128)(2,1)} %values_in.1), channel_id=1, source_target_pairs={{0,8},{1,9},{2,10},{3,11},{4,12},{5,13},{6,14},{7,15},{8,16},{9,17... | collective-permute-start | bytes 393224 | tf_op jit(solution)/shard_map/ppermute | solution.py:46
  6.1 0.5 %collective-permute-start.1 = (bf16[256,256]{1,0:T(8,128)(2,1)}, bf16[256,256]{1,0:T(8,128)(2,1)S(1)}, u32[]{:S(2)}, u32[]{:S(2)}) collective-permute-start(bf16[256,256]{1,0:T(8,128)(2,1)} %values_in.1), channel_id=1, source_target_pairs={{0,4},{1,5},{2,6},{3,7},{4,0},{5,1},{6,2},{7,3},{8,12},{9,13},{10,... | collective-permute-start | bytes 393224 | tf_op jit(solution)/shard_map/ppermute | solution.py:46
  6.6 1.6 %attend_first.1 = (f32[1024,128]{1,0:T(8,128)S(1)}, f32[1024,128]{1,0:T(8,128)S(1)}, f32[1024,128]{1,0:T(8,128)S(1)}, bf16[256,512]{1,0:T(8,128)(2,1)S(1)}, f32[16,256]{1,0:T(8,128)S(1)}) custom-call(s32[16]{0:T(128)} %docs_in.1, bf16[256,512]{1,0:T(8,128)(2,1)} %queries_in.1, bf16[256,256]{1,0:T(8,128)(2,1)} %keys_in.1, bf16[256,256]{1,0:T(8,128)(2,1)} %values_in.1), custom_call_target="tpu_custom_call" | custom-call | flops 134217728 | tf_op jit(solution)/shard_map/attend_first/pallas_call | solution.py:202
  8.3 0.3 collective-permute-done.refs_3_
  8.6 0.2 collective-permute-start.6
  8.8 2.9 %collective-permute-done.3.refs_6_ = bf16[256,256]{1,0:T(8,128)(2,1)S(1)} collective-permute-done((bf16[256,256]{1,0:T(8,128)(2,1)}, bf16[256,256]{1,0:T(8,128)(2,1)S(1)}, u32[]{:S(2)}, u32[]{:S(2)}) %collective-permute-start.3) | collective-permute-done | bytes 131104 | tf_op jit(solution)/shard_map/ppermute | solution.py:46
  11.8 0.5 %collective-permute-start.7 = (bf16[256,256]{1,0:T(8,128)(2,1)S(1)}, bf16[256,256]{1,0:T(8,128)(2,1)S(1)}, u32[]{:S(2)}, u32[]{:S(2)}) collective-permute-start(bf16[256,256]{1,0:T(8,128)(2,1)S(1)} %collective-permute-done.3.refs_6_), channel_id=1, source_target_pairs={{0,1},{1,0},{2,3},{3,2},{4,5},{5,4},{6,7},{7,6},{8,12},{9,13},{10,... | collective-permute-start | bytes 393224 | tf_op jit(solution)/shard_map/ppermute | solution.py:46
  12.3 0.1 collective-permute-start.8
  12.4 0.7 %collective-permute-done.5.refs_8_ = bf16[256,256]{1,0:T(8,128)(2,1)S(1)} collective-permute-done((bf16[256,256]{1,0:T(8,128)(2,1)S(1)}, bf16[256,256]{1,0:T(8,128)(2,1)S(1)}, u32[]{:S(2)}, u32[]{:S(2)}) %collective-permute-start.5) | collective-permute-done | bytes 131104 | tf_op jit(solution)/shard_map/ppermute | solution.py:46
  13.1 0.1 collective-permute-start.9
  13.3 2.6 %attend_next.1 = (f32[1024,128]{1,0:T(8,128)S(1)}, f32[1024,128]{1,0:T(8,128)S(1)}, f32[1024,128]{1,0:T(8,128)S(1)}, bf16[512,5376]{1,0:T(8,128)(2,1)S(1)}) custom-call(bf16[256,512]{1,0:T(8,128)(2,1)S(1)} %get-tuple-element.39.queries, f32[16,256]{1,0:T(8,128)S(1)} %get-tuple-element.40.open_beside, bf16[512,5376]{1,0:T(8,128)(2,1)} %weight_in.1, ...), custom_call_target="tpu_custom_call" | custom-call | flops 402653184 | bytes 5505024 | tf_op jit(solution)/shard_map/attend_next/pallas_call | solution.py:224
  15.9 1.5 %attend_last.1 = (bf16[128,512]{1,0:T(8,128)(2,1)S(1)}, bf16[128,512]{1,0:T(8,128)(2,1)S(1)}, f32[64,2176]{1,0:T(8,128)S(1)}, bf16[64,2176]{1,0:T(8,128)(2,1)S(1)}) custom-call(bf16[256,512]{1,0:T(8,128)(2,1)S(1)} %get-tuple-element.39.queries, bf16[512,5376]{1,0:T(8,128)(2,1)S(1)} %get-tuple-element.46.weight, f32[1024,128]{1,0:T(8,128)S(1)} %get-tuple-element.47.refs_0_, ...), custom_call_target="tpu_custom_call" | custom-call | flops 268435456 | tf_op jit(solution)/shard_map/attend_last/pallas_call | solution.py:267
  17.4 0.4 collective-permute-start.10
  17.8 0.6 %project.2 = (f32[64,3200]{1,0:T(8,128)S(1)}, bf16[64,3200]{1,0:T(8,128)(2,1)S(1)}) custom-call(bf16[128,512]{1,0:T(8,128)(2,1)S(1)} %get-tuple-element.55.rows, bf16[512,5376]{1,0:T(8,128)(2,1)S(1)} %get-tuple-element.46.weight), custom_call_target="tpu_custom_call" | custom-call | flops 419430400 | tf_op jit(solution)/shard_map/project/pallas_call | solution.py:302
  18.5 0.6 %collective-permute-done.10.theirs = bf16[64,2176]{1,0:T(8,128)(2,1)S(1)} collective-permute-done((bf16[64,2176]{1,0:T(8,128)(2,1)S(1)}, bf16[64,2176]{1,0:T(8,128)(2,1)S(1)}, u32[]{:S(2)}, u32[]{:S(2)}) %collective-permute-start.10) | collective-permute-done | bytes 278560 | tf_op jit(solution)/shard_map/ppermute | solution.py:22
  19.1 0.4 collective-permute-start.11
  19.5 1.5 %collective-permute-start.15 = (bf16[64,1536]{1,0:T(8,128)(2,1)S(1)}, bf16[64,1536]{1,0:T(8,128)(2,1)S(1)}, u32[]{:S(2)}, u32[]{:S(2)}) collective-permute-start(bf16[64,1536]{1,0:T(8,128)(2,1)S(1)} %get-tuple-element.59), channel_id=1, source_target_pairs={{0,2},{1,3},{2,0},{3,1},{4,6},{5,7},{6,4},{7,5},{8,10},{9,11},{10,... | collective-permute-start | bytes 589832 | tf_op jit(solution)/shard_map/ppermute | solution.py:22
  21.1 1.5 %collective-permute-start.12 = (bf16[64,3200]{1,0:T(8,128)(2,1)S(1)}, bf16[64,3200]{1,0:T(8,128)(2,1)S(1)}, u32[]{:S(2)}, u32[]{:S(2)}) collective-permute-start(bf16[64,3200]{1,0:T(8,128)(2,1)S(1)} %add_up.3), channel_id=1, source_target_pairs={{0,2},{1,3},{2,0},{3,1},{4,6},{5,7},{6,4},{7,5},{8,10},{9,11},{10,... | collective-permute-start | bytes 1228808 | tf_op jit(solution)/shard_map/ppermute | solution.py:22
  22.5 1.5 %project.3 = (f32[64,5376]{1,0:T(8,128)S(1)}, bf16[64,1344]{1,0:T(8,128)(2,1)S(1)}, bf16[64,1344]{1,0:T(8,128)(2,1)S(1)}, bf16[64,1344]{1,0:T(8,128)(2,1)S(1)}, bf16[64,1344]{1,0:T(8,128)(2,1)S(1)}) custom-call(bf16[128,512]{1,0:T(8,128)(2,1)S(1)} %get-tuple-element.64.rows, bf16[512,5376]{1,0:T(8,128)(2,1)S(1)} %get-tuple-element.46.weight), custom_call_target="tpu_custom_call" | custom-call | flops 704643072 | tf_op jit(solution)/shard_map/project/pallas_call | solution.py:302
  24.1 6.1 %collective-permute-start.14 = (bf16[64,640]{1,0:T(8,128)(2,1)S(1)}, bf16[64,640]{1,0:T(8,128)(2,1)S(1)}, u32[]{:S(2)}, u32[]{:S(2)}) collective-permute-start(bf16[64,640]{1,0:T(8,128)(2,1)S(1)} %get-tuple-element.66), channel_id=1, source_target_pairs={{0,8},{1,9},{2,10},{3,11},{4,12},{5,13},{6,14},{7,15},{8,0},{9,1},... | collective-permute-start | bytes 245768 | tf_op jit(solution)/shard_map/ppermute | solution.py:46
  30.1 0.5 %collective-permute-start.13 = (bf16[64,640]{1,0:T(8,128)(2,1)S(1)}, bf16[64,640]{1,0:T(8,128)(2,1)S(1)}, u32[]{:S(2)}, u32[]{:S(2)}) collective-permute-start(bf16[64,640]{1,0:T(8,128)(2,1)S(1)} %get-tuple-element.66), channel_id=1, source_target_pairs={{0,2},{1,3},{2,0},{3,1},{4,6},{5,7},{6,4},{7,5},{8,9},{9,8},{10,11... | collective-permute-start | bytes 245768 | tf_op jit(solution)/shard_map/ppermute | solution.py:46
  30.7 1.9 %collective-permute-done.14 = bf16[64,640]{1,0:T(8,128)(2,1)S(1)} collective-permute-done((bf16[64,640]{1,0:T(8,128)(2,1)S(1)}, bf16[64,640]{1,0:T(8,128)(2,1)S(1)}, u32[]{:S(2)}, u32[]{:S(2)}) %collective-permute-start.14) | collective-permute-done | bytes 81952 | tf_op jit(solution)/shard_map/ppermute | solution.py:46
  32.6 4.4 %collective-permute-done.13.refs_2_ = bf16[64,640]{1,0:T(8,128)(2,1)S(1)} collective-permute-done((bf16[64,640]{1,0:T(8,128)(2,1)S(1)}, bf16[64,640]{1,0:T(8,128)(2,1)S(1)}, u32[]{:S(2)}, u32[]{:S(2)}) %collective-permute-start.13) | collective-permute-done | bytes 81952 | tf_op jit(solution)/shard_map/ppermute | solution.py:46
  37.0 1.5 %collective-permute-start.16 = (bf16[64,640]{1,0:T(8,128)(2,1)S(1)}, bf16[64,640]{1,0:T(8,128)(2,1)S(1)}, u32[]{:S(2)}, u32[]{:S(2)}) collective-permute-start(bf16[64,640]{1,0:T(8,128)(2,1)S(1)} %collective-permute-done.14), channel_id=1, source_target_pairs={{0,2},{1,3},{2,0},{3,1},{4,6},{5,7},{6,4},{7,5},{8,9},{9,8},{10,11... | collective-permute-start | bytes 245768 | tf_op jit(solution)/shard_map/ppermute | solution.py:46
  38.5 0.5 %collective-permute-start.19 = (bf16[64,1344]{1,0:T(8,128)(2,1)S(1)}, bf16[64,1344]{1,0:T(8,128)(2,1)S(1)}, u32[]{:S(2)}, u32[]{:S(2)}) collective-permute-start(bf16[64,1344]{1,0:T(8,128)(2,1)S(1)} %get-tuple-element.70), channel_id=1, source_target_pairs={{0,1},{1,0},{2,3},{3,2},{4,5},{5,4},{6,7},{7,6},{8,9},{9,8},{10,11... | collective-permute-start | bytes 516104 | tf_op jit(solution)/shard_map/ppermute | solution.py:22
  39.0 2.4 %collective-permute-done.16 = bf16[64,640]{1,0:T(8,128)(2,1)S(1)} collective-permute-done((bf16[64,640]{1,0:T(8,128)(2,1)S(1)}, bf16[64,640]{1,0:T(8,128)(2,1)S(1)}, u32[]{:S(2)}, u32[]{:S(2)}) %collective-permute-start.16) | collective-permute-done | bytes 81952 | tf_op jit(solution)/shard_map/ppermute | solution.py:46
  41.5 1.4 %collective-permute-done.21.refs_5_.refs_7_ = bf16[64,1344]{1,0:T(8,128)(2,1)S(1)} collective-permute-done((bf16[64,1344]{1,0:T(8,128)(2,1)S(1)}, bf16[64,1344]{1,0:T(8,128)(2,1)S(1)}, u32[]{:S(2)}, u32[]{:S(2)}) %collective-permute-start.21) | collective-permute-done | bytes 172064 | tf_op jit(solution)/shard_map/ppermute | solution.py:22
  42.9 0.8 %combine.2.refs_8_ = bf16[64,5376]{1,0:T(8,128)(2,1)} custom-call(f32[64,5376]{1,0:T(8,128)S(1)} %get-tuple-element.65.refs_0_, bf16[64,1536]{1,0:T(8,128)(2,1)S(1)} %collective-permute-done.15.refs_1_, bf16[64,1344]{1,0:T(8,128)(2,1)S(1)} %collective-permute-done.18.refs_2_.refs_4_, bf16[64,1344]{1,0:T(8,128)(2,1)S(1)} %collective-permute-done.19.refs_3_.refs_5_, ...), custom_call_target="tpu_custom_call" | custom-call | tf_op jit(solution)/shard_map/combine/pallas_call | solution.py:371
  43.6 2.7 %collective-permute-done.17.refs_3_ = bf16[64,640]{1,0:T(8,128)(2,1)S(1)} collective-permute-done((bf16[64,640]{1,0:T(8,128)(2,1)S(1)}, bf16[64,640]{1,0:T(8,128)(2,1)S(1)}, u32[]{:S(2)}, u32[]{:S(2)}) %collective-permute-start.17) | collective-permute-done | bytes 81952 | tf_op jit(solution)/shard_map/ppermute | solution.py:46
  46.3 1.1 %combine.3 = bf16[64,5376]{1,0:T(8,128)(2,1)} custom-call(f32[64,5376]{1,0:T(8,128)S(1)} %get-tuple-element.65.refs_0_, bf16[64,3200]{1,0:T(8,128)(2,1)S(1)} %collective-permute-done.12.refs_1_, bf16[64,640]{1,0:T(8,128)(2,1)S(1)} %collective-permute-done.13.refs_2_, ...), custom_call_target="tpu_custom_call", output_to_operand_aliasing={{}: (8, {})} | custom-call | tf_op jit(solution)/shard_map/combine/pallas_call | solution.py:371
  (21 shorter events, 0.2 us)
Async XLA Ops:
  0.0 8.2 %collective-permute-start.2 = (bf16[256,256]{1,0:T(8,128)(2,1)}, bf16[256,256]{1,0:T(8,128)(2,1)S(1)}, u32[]{:S(2)}, u32[]{:S(2)}) collective-permute-start(bf16[256,256]{1,0:T(8,128)(2,1)} %keys_in.1), channel_id=1, source_target_pairs={{0,8},{1,9},{2,10},{3,11},{4,12},{5,13},{6,14},{7,15},{8,16},{9,17... | collective-permute-start | bytes 393224 | tf_op jit(solution)/shard_map/ppermute | solution.py:46
  3.0 5.6 %collective-permute-start = (bf16[256,256]{1,0:T(8,128)(2,1)}, bf16[256,256]{1,0:T(8,128)(2,1)S(1)}, u32[]{:S(2)}, u32[]{:S(2)}) collective-permute-start(bf16[256,256]{1,0:T(8,128)(2,1)} %keys_in.1), channel_id=1, source_target_pairs={{0,4},{1,5},{2,6},{3,7},{4,0},{5,1},{6,2},{7,3},{8,12},{9,13},{10,... | collective-permute-start | bytes 393224 | tf_op jit(solution)/shard_map/ppermute | solution.py:46
  4.5 7.2 %collective-permute-start.3 = (bf16[256,256]{1,0:T(8,128)(2,1)}, bf16[256,256]{1,0:T(8,128)(2,1)S(1)}, u32[]{:S(2)}, u32[]{:S(2)}) collective-permute-start(bf16[256,256]{1,0:T(8,128)(2,1)} %values_in.1), channel_id=1, source_target_pairs={{0,8},{1,9},{2,10},{3,11},{4,12},{5,13},{6,14},{7,15},{8,16},{9,17... | collective-permute-start | bytes 393224 | tf_op jit(solution)/shard_map/ppermute | solution.py:46
  6.1 5.7 %collective-permute-start.1 = (bf16[256,256]{1,0:T(8,128)(2,1)}, bf16[256,256]{1,0:T(8,128)(2,1)S(1)}, u32[]{:S(2)}, u32[]{:S(2)}) collective-permute-start(bf16[256,256]{1,0:T(8,128)(2,1)} %values_in.1), channel_id=1, source_target_pairs={{0,4},{1,5},{2,6},{3,7},{4,0},{5,1},{6,2},{7,3},{8,12},{9,13},{10,... | collective-permute-start | bytes 393224 | tf_op jit(solution)/shard_map/ppermute | solution.py:46
  8.2 4.0 %collective-permute-start.4 = (bf16[256,256]{1,0:T(8,128)(2,1)S(1)}, bf16[256,256]{1,0:T(8,128)(2,1)S(1)}, u32[]{:S(2)}, u32[]{:S(2)}) collective-permute-start(bf16[256,256]{1,0:T(8,128)(2,1)S(1)} %collective-permute-done.2.refs_5_), channel_id=1, source_target_pairs={{0,1},{1,0},{2,3},{3,2},{4,5},{5,4},{6,7},{7,6},{8,16},{9,17},{10,... | collective-permute-start | bytes 393224 | tf_op jit(solution)/shard_map/ppermute | solution.py:46
  8.6 3.7 %collective-permute-start.6 = (bf16[256,256]{1,0:T(8,128)(2,1)S(1)}, bf16[256,256]{1,0:T(8,128)(2,1)S(1)}, u32[]{:S(2)}, u32[]{:S(2)}) collective-permute-start(bf16[256,256]{1,0:T(8,128)(2,1)S(1)} %collective-permute-done.2.refs_5_), channel_id=1, source_target_pairs={{0,1},{1,0},{2,3},{3,2},{4,5},{5,4},{6,7},{7,6},{8,12},{9,13},{10,... | collective-permute-start | bytes 393224 | tf_op jit(solution)/shard_map/ppermute | solution.py:46
  11.8 1.3 %collective-permute-start.5 = (bf16[256,256]{1,0:T(8,128)(2,1)S(1)}, bf16[256,256]{1,0:T(8,128)(2,1)S(1)}, u32[]{:S(2)}, u32[]{:S(2)}) collective-permute-start(bf16[256,256]{1,0:T(8,128)(2,1)S(1)} %collective-permute-done.3.refs_6_), channel_id=1, source_target_pairs={{0,1},{1,0},{2,3},{3,2},{4,5},{5,4},{6,7},{7,6},{8,16},{9,17},{10,... | collective-permute-start | bytes 393224 | tf_op jit(solution)/shard_map/ppermute | solution.py:46
  11.8 4.1 %collective-permute-start.7 = (bf16[256,256]{1,0:T(8,128)(2,1)S(1)}, bf16[256,256]{1,0:T(8,128)(2,1)S(1)}, u32[]{:S(2)}, u32[]{:S(2)}) collective-permute-start(bf16[256,256]{1,0:T(8,128)(2,1)S(1)} %collective-permute-done.3.refs_6_), channel_id=1, source_target_pairs={{0,1},{1,0},{2,3},{3,2},{4,5},{5,4},{6,7},{7,6},{8,12},{9,13},{10,... | collective-permute-start | bytes 393224 | tf_op jit(solution)/shard_map/ppermute | solution.py:46
  12.3 3.6 %collective-permute-start.8 = (bf16[256,256]{1,0:T(8,128)(2,1)S(1)}, bf16[256,256]{1,0:T(8,128)(2,1)S(1)}, u32[]{:S(2)}, u32[]{:S(2)}) collective-permute-start(bf16[256,256]{1,0:T(8,128)(2,1)S(1)} %collective-permute-done.6.refs_3_), channel_id=1, source_target_pairs={{0,1},{1,0},{2,3},{3,2},{4,5},{5,4},{6,7},{7,6},{8,16},{9,17},{10,... | collective-permute-start | bytes 393224 | tf_op jit(solution)/shard_map/ppermute | solution.py:46
  13.1 2.8 %collective-permute-start.9 = (bf16[256,256]{1,0:T(8,128)(2,1)S(1)}, bf16[256,256]{1,0:T(8,128)(2,1)S(1)}, u32[]{:S(2)}, u32[]{:S(2)}) collective-permute-start(bf16[256,256]{1,0:T(8,128)(2,1)S(1)} %collective-permute-done.5.refs_8_), channel_id=1, source_target_pairs={{0,1},{1,0},{2,3},{3,2},{4,5},{5,4},{6,7},{7,6},{8,9},{9,8},{10,11... | collective-permute-start | bytes 393224 | tf_op jit(solution)/shard_map/ppermute | solution.py:46
  17.4 1.6 %collective-permute-start.10 = (bf16[64,2176]{1,0:T(8,128)(2,1)S(1)}, bf16[64,2176]{1,0:T(8,128)(2,1)S(1)}, u32[]{:S(2)}, u32[]{:S(2)}) collective-permute-start(bf16[64,2176]{1,0:T(8,128)(2,1)S(1)} %get-tuple-element.58), channel_id=1, source_target_pairs={{0,1},{1,0},{2,3},{3,2},{4,5},{5,4},{6,7},{7,6},{8,9},{9,8},{10,11... | collective-permute-start | bytes 835592 | tf_op jit(solution)/shard_map/ppermute | solution.py:22
  19.1 1.9 %collective-permute-start.11 = (bf16[64,3200]{1,0:T(8,128)(2,1)S(1)}, bf16[64,3200]{1,0:T(8,128)(2,1)S(1)}, u32[]{:S(2)}, u32[]{:S(2)}) collective-permute-start(bf16[64,3200]{1,0:T(8,128)(2,1)S(1)} %get-tuple-element.63), channel_id=1, source_target_pairs={{0,1},{1,0},{2,3},{3,2},{4,5},{5,4},{6,7},{7,6},{8,9},{9,8},{10,11... | collective-permute-start | bytes 1228808 | tf_op jit(solution)/shard_map/ppermute | solution.py:22
  19.5 11.2 %collective-permute-start.15 = (bf16[64,1536]{1,0:T(8,128)(2,1)S(1)}, bf16[64,1536]{1,0:T(8,128)(2,1)S(1)}, u32[]{:S(2)}, u32[]{:S(2)}) collective-permute-start(bf16[64,1536]{1,0:T(8,128)(2,1)S(1)} %get-tuple-element.59), channel_id=1, source_target_pairs={{0,2},{1,3},{2,0},{3,1},{4,6},{5,7},{6,4},{7,5},{8,10},{9,11},{10,... | collective-permute-start | bytes 589832 | tf_op jit(solution)/shard_map/ppermute | solution.py:22
  21.1 25.2 %collective-permute-start.12 = (bf16[64,3200]{1,0:T(8,128)(2,1)S(1)}, bf16[64,3200]{1,0:T(8,128)(2,1)S(1)}, u32[]{:S(2)}, u32[]{:S(2)}) collective-permute-start(bf16[64,3200]{1,0:T(8,128)(2,1)S(1)} %add_up.3), channel_id=1, source_target_pairs={{0,2},{1,3},{2,0},{3,1},{4,6},{5,7},{6,4},{7,5},{8,10},{9,11},{10,... | collective-permute-start | bytes 1228808 | tf_op jit(solution)/shard_map/ppermute | solution.py:22
  24.1 8.5 %collective-permute-start.14 = (bf16[64,640]{1,0:T(8,128)(2,1)S(1)}, bf16[64,640]{1,0:T(8,128)(2,1)S(1)}, u32[]{:S(2)}, u32[]{:S(2)}) collective-permute-start(bf16[64,640]{1,0:T(8,128)(2,1)S(1)} %get-tuple-element.66), channel_id=1, source_target_pairs={{0,8},{1,9},{2,10},{3,11},{4,12},{5,13},{6,14},{7,15},{8,0},{9,1},... | collective-permute-start | bytes 245768 | tf_op jit(solution)/shard_map/ppermute | solution.py:46
  30.1 6.9 %collective-permute-start.13 = (bf16[64,640]{1,0:T(8,128)(2,1)S(1)}, bf16[64,640]{1,0:T(8,128)(2,1)S(1)}, u32[]{:S(2)}, u32[]{:S(2)}) collective-permute-start(bf16[64,640]{1,0:T(8,128)(2,1)S(1)} %get-tuple-element.66), channel_id=1, source_target_pairs={{0,2},{1,3},{2,0},{3,1},{4,6},{5,7},{6,4},{7,5},{8,9},{9,8},{10,11... | collective-permute-start | bytes 245768 | tf_op jit(solution)/shard_map/ppermute | solution.py:46
  37.0 4.4 %collective-permute-start.16 = (bf16[64,640]{1,0:T(8,128)(2,1)S(1)}, bf16[64,640]{1,0:T(8,128)(2,1)S(1)}, u32[]{:S(2)}, u32[]{:S(2)}) collective-permute-start(bf16[64,640]{1,0:T(8,128)(2,1)S(1)} %collective-permute-done.14), channel_id=1, source_target_pairs={{0,2},{1,3},{2,0},{3,1},{4,6},{5,7},{6,4},{7,5},{8,9},{9,8},{10,11... | collective-permute-start | bytes 245768 | tf_op jit(solution)/shard_map/ppermute | solution.py:46
  38.5 3.0 %collective-permute-start.18 = (bf16[64,1344]{1,0:T(8,128)(2,1)S(1)}, bf16[64,1344]{1,0:T(8,128)(2,1)S(1)}, u32[]{:S(2)}, u32[]{:S(2)}) collective-permute-start(bf16[64,1344]{1,0:T(8,128)(2,1)S(1)} %get-tuple-element.69), channel_id=1, source_target_pairs={{0,1},{1,0},{2,3},{3,2},{4,5},{5,4},{6,7},{7,6},{8,9},{9,8},{10,11... | collective-permute-start | bytes 516104 | tf_op jit(solution)/shard_map/ppermute | solution.py:22
  38.5 3.0 %collective-permute-start.19 = (bf16[64,1344]{1,0:T(8,128)(2,1)S(1)}, bf16[64,1344]{1,0:T(8,128)(2,1)S(1)}, u32[]{:S(2)}, u32[]{:S(2)}) collective-permute-start(bf16[64,1344]{1,0:T(8,128)(2,1)S(1)} %get-tuple-element.70), channel_id=1, source_target_pairs={{0,1},{1,0},{2,3},{3,2},{4,5},{5,4},{6,7},{7,6},{8,9},{9,8},{10,11... | collective-permute-start | bytes 516104 | tf_op jit(solution)/shard_map/ppermute | solution.py:22
  39.0 2.5 %collective-permute-start.20 = (bf16[64,1344]{1,0:T(8,128)(2,1)S(1)}, bf16[64,1344]{1,0:T(8,128)(2,1)S(1)}, u32[]{:S(2)}, u32[]{:S(2)}) collective-permute-start(bf16[64,1344]{1,0:T(8,128)(2,1)S(1)} %get-tuple-element.71), channel_id=1, source_target_pairs={{0,1},{1,0},{2,3},{3,2},{4,5},{5,4},{6,7},{7,6},{8,9},{9,8},{10,11... | collective-permute-start | bytes 516104 | tf_op jit(solution)/shard_map/ppermute | solution.py:22
  41.4 1.4 %collective-permute-start.21 = (bf16[64,1344]{1,0:T(8,128)(2,1)S(1)}, bf16[64,1344]{1,0:T(8,128)(2,1)S(1)}, u32[]{:S(2)}, u32[]{:S(2)}) collective-permute-start(bf16[64,1344]{1,0:T(8,128)(2,1)S(1)} %get-tuple-element.72), channel_id=1, source_target_pairs={{0,1},{1,0},{2,3},{3,2},{4,5},{5,4},{6,7},{7,6},{8,9},{9,8},{10,11... | collective-permute-start | bytes 516104 | tf_op jit(solution)/shard_map/ppermute | solution.py:22
  41.5 4.9 %collective-permute-start.17 = (bf16[64,640]{1,0:T(8,128)(2,1)S(1)}, bf16[64,640]{1,0:T(8,128)(2,1)S(1)}, u32[]{:S(2)}, u32[]{:S(2)}) collective-permute-start(bf16[64,640]{1,0:T(8,128)(2,1)S(1)} %collective-permute-done.16), channel_id=1, source_target_pairs={{0,8},{1,9},{2,10},{3,11},{4,12},{5,13},{6,14},{7,15},{8,0},{9,1},... | collective-permute-start | bytes 245768 | tf_op jit(solution)/shard_map/ppermute | solution.py:46

commit v4 on v3

--- a/solution.py
+++ b/solution.py
@@ -32,8 +32,8 @@
 AGAIN = ((2, 4), (3, 5))
 ACROSS = ((2, 3), (4, 5))
 LAST = ((4, 5),)
-EARLY = (0, 1, 6, 7)
-RELAY = ((0, 2), (1, 3), (4, 6), (5, 7))
+LATE = (4, 5)
+RELAY = ((4, 6), (5, 7))
 
 
 def move(block, rings, crossing=()):
@@ -347,9 +347,9 @@
                 there = options[0][:, low - at : high - at].astype(jnp.float32)
                 if len(options) == 2:
                     position = lax.axis_index("ctx")
-                    early = functools.reduce(jnp.logical_or, [position == i for i in EARLY])
+                    late = functools.reduce(jnp.logical_or, [position == i for i in LATE])
                     relayed = options[1][:, low - at : high - at].astype(jnp.float32)
-                    there = jnp.where(early, there, relayed)
+                    there = jnp.where(late, relayed, there)
                 total[:, low - at : high - at] = (piece + there).astype(total.dtype)
             left += part.shape[1]
         copies.append(pltpu.make_async_copy(total, out.at[:, at : at + width], sems.at[i]))
@@ -498,12 +498,12 @@
     later_mine = after(later_mine, first_sum)
     (later_sum,) = add_up(later_mine, later_theirs, [columns - cuts[2]])
     later_part = hop(later_sum, "head", other_chip)
-    mine, *sends = project(after(near, later_sum), weight, (0, columns), 4)
+    mine, *sends = project(after(near, later_sum), weight, (0, columns), 3)
     theirs = [hop(send, "head", other_core) for send in sends]
     if n_ctx == 8:
-        direct = move(relay_sum, (), EARLY)
+        direct = move(relay_sum, (), [i for i in range(n_ctx) if i not in LATE])
         arrived = move(after(relay_sum, mine), RELAY)
-        relay_part = (direct, move(move(after(after(arrived, first_part), direct), (), EARLY), RELAY))
+        relay_part = (direct, move(move(after(arrived, first_part), (), [ring[1] for ring in RELAY]), RELAY))
     else:
         relay_part = hop(relay_sum, "head", other_chip)
     out = combine(mine, theirs, [first_part], [0])

time: 47.5 us -> 42.1 us (0.89)
  the two profiles are of different devices: /device:TPU:0 before, /device:TPU:24 now
where the time goes in v4:
time: 42.1 us; the launch traced here: 41.9 us
  starting transfers between devices  17.7 us (42%)
  waiting for transfers between devices  15.1 us (36%)
  Pallas kernels  8.97 us (21%)
    ppermute x14, waiting for transfers between devices, move(): return lax.ppermute(block, ('ctx', 'head'), pairs)  14.6 us
    ppermute x14, starting transfers between devices, move(): return lax.ppermute(block, ('ctx', 'head'), pairs)  13.1 us
    ppermute x7, starting transfers between devices, hop(): return lax.ppermute(block, axis, pairs)  4.54 us
    pallas_call x1, Pallas kernels, attend_next(): pl.pallas_call(functools.partial(next_kernel, numbers), out_shape=state_s...  2.59 us
    pallas_call x2, Pallas kernels, combine(): pl.pallas_call(kernel, out_shape=jax.ShapeDtypeStruct(mine.shape, jnp.bfl...  1.66 us
    pallas_call x1, Pallas kernels, attend_first(): pl.pallas_call(first_kernel, out_shape=state_shapes(queries) + (pltpu.VME...  1.61 us
    pallas_call x1, Pallas kernels, attend_last(): pl.pallas_call(functools.partial(last_kernel, numbers, columns), out_shap...  1.5 us
    pallas_call x2, Pallas kernels, project(): pl.pallas_call(functools.partial(project_kernel, columns), out_shape=proj...  1.5 us
  transfers between devices with their start and end apart: 21, of which 7 were waited for; matrix products, arithmetic and copies ran while one was open for 0% of the time, Pallas kernels for 16%

profile of v4, /device:TPU:24, one launch (start us, length us, event | category | flops | bytes accessed | tf_op | source)
XLA Modules:
  0.0 41.9 jit_solution(12070244009909374516)
XLA Ops:
  0.0 1.5 %collective-permute-start = (bf16[256,256]{1,0:T(8,128)(2,1)}, bf16[256,256]{1,0:T(8,128)(2,1)S(1)}, u32[]{:S(2)}, u32[]{:S(2)}) collective-permute-start(bf16[256,256]{1,0:T(8,128)(2,1)} %keys_in.1), channel_id=1, source_target_pairs={{0,4},{1,5},{2,6},{3,7},{4,0},{5,1},{6,2},{7,3},{8,12},{9,13},{10,... | collective-permute-start | bytes 393224 | tf_op jit(solution)/shard_map/ppermute | solution.py:46
  1.5 0.2 collective-permute-start.3
  1.8 0.5 %collective-permute-start.1 = (bf16[256,256]{1,0:T(8,128)(2,1)}, bf16[256,256]{1,0:T(8,128)(2,1)S(1)}, u32[]{:S(2)}, u32[]{:S(2)}) collective-permute-start(bf16[256,256]{1,0:T(8,128)(2,1)} %values_in.1), channel_id=1, source_target_pairs={{0,4},{1,5},{2,6},{3,7},{4,0},{5,1},{6,2},{7,3},{8,12},{9,13},{10,... | collective-permute-start | bytes 393224 | tf_op jit(solution)/shard_map/ppermute | solution.py:46
  2.3 1.6 %attend_first.1 = (f32[1024,128]{1,0:T(8,128)S(1)}, f32[1024,128]{1,0:T(8,128)S(1)}, f32[1024,128]{1,0:T(8,128)S(1)}, bf16[256,512]{1,0:T(8,128)(2,1)S(1)}, f32[16,256]{1,0:T(8,128)S(1)}) custom-call(s32[16]{0:T(128)} %docs_in.1, bf16[256,512]{1,0:T(8,128)(2,1)} %queries_in.1, bf16[256,256]{1,0:T(8,128)(2,1)} %keys_in.1, bf16[256,256]{1,0:T(8,128)(2,1)} %values_in.1), custom_call_target="tpu_custom_call" | custom-call | flops 134217728 | tf_op jit(solution)/shard_map/attend_first/pallas_call | solution.py:202
  3.9 0.1 collective-permute-start.4
  4.0 2.5 %collective-permute-done.refs_3_ = bf16[256,256]{1,0:T(8,128)(2,1)S(1)} collective-permute-done((bf16[256,256]{1,0:T(8,128)(2,1)}, bf16[256,256]{1,0:T(8,128)(2,1)S(1)}, u32[]{:S(2)}, u32[]{:S(2)}) %collective-permute-start) | collective-permute-done | bytes 131104 | tf_op jit(solution)/shard_map/ppermute | solution.py:46
  6.5 0.5 %collective-permute-start.5 = (bf16[256,256]{1,0:T(8,128)(2,1)S(1)}, bf16[256,256]{1,0:T(8,128)(2,1)S(1)}, u32[]{:S(2)}, u32[]{:S(2)}) collective-permute-start(bf16[256,256]{1,0:T(8,128)(2,1)S(1)} %collective-permute-done.3.refs_6_), channel_id=1, source_target_pairs={{0,1},{1,0},{2,3},{3,2},{4,5},{5,4},{6,7},{7,6},{8,16},{9,17},{10,... | collective-permute-start | bytes 393224 | tf_op jit(solution)/shard_map/ppermute | solution.py:46
  7.0 1.9 %collective-permute-done.1.refs_4_ = bf16[256,256]{1,0:T(8,128)(2,1)S(1)} collective-permute-done((bf16[256,256]{1,0:T(8,128)(2,1)}, bf16[256,256]{1,0:T(8,128)(2,1)S(1)}, u32[]{:S(2)}, u32[]{:S(2)}) %collective-permute-start.1) | collective-permute-done | bytes 131104 | tf_op jit(solution)/shard_map/ppermute | solution.py:46
  8.9 0.5 %collective-permute-start.8 = (bf16[256,256]{1,0:T(8,128)(2,1)S(1)}, bf16[256,256]{1,0:T(8,128)(2,1)S(1)}, u32[]{:S(2)}, u32[]{:S(2)}) collective-permute-start(bf16[256,256]{1,0:T(8,128)(2,1)S(1)} %collective-permute-done.6.refs_3_), channel_id=1, source_target_pairs={{0,1},{1,0},{2,3},{3,2},{4,5},{5,4},{6,7},{7,6},{8,16},{9,17},{10,... | collective-permute-start | bytes 393224 | tf_op jit(solution)/shard_map/ppermute | solution.py:46
  9.5 0.1 collective-permute-start.9
  9.5 2.6 %attend_next.1 = (f32[1024,128]{1,0:T(8,128)S(1)}, f32[1024,128]{1,0:T(8,128)S(1)}, f32[1024,128]{1,0:T(8,128)S(1)}, bf16[512,5376]{1,0:T(8,128)(2,1)S(1)}) custom-call(bf16[256,512]{1,0:T(8,128)(2,1)S(1)} %get-tuple-element.37.queries, f32[16,256]{1,0:T(8,128)S(1)} %get-tuple-element.38.open_beside, bf16[512,5376]{1,0:T(8,128)(2,1)} %weight_in.1, ...), custom_call_target="tpu_custom_call" | custom-call | flops 402653184 | bytes 5505024 | tf_op jit(solution)/shard_map/attend_next/pallas_call | solution.py:224
  12.2 1.5 %attend_last.1 = (bf16[128,512]{1,0:T(8,128)(2,1)S(1)}, bf16[128,512]{1,0:T(8,128)(2,1)S(1)}, f32[64,2176]{1,0:T(8,128)S(1)}, bf16[64,2176]{1,0:T(8,128)(2,1)S(1)}) custom-call(bf16[256,512]{1,0:T(8,128)(2,1)S(1)} %get-tuple-element.37.queries, bf16[512,5376]{1,0:T(8,128)(2,1)S(1)} %get-tuple-element.44.weight, f32[1024,128]{1,0:T(8,128)S(1)} %get-tuple-element.45.refs_0_, ...), custom_call_target="tpu_custom_call" | custom-call | flops 268435456 | tf_op jit(solution)/shard_map/attend_last/pallas_call | solution.py:267
  13.7 0.5 %collective-permute-start.10 = (bf16[64,2176]{1,0:T(8,128)(2,1)S(1)}, bf16[64,2176]{1,0:T(8,128)(2,1)S(1)}, u32[]{:S(2)}, u32[]{:S(2)}) collective-permute-start(bf16[64,2176]{1,0:T(8,128)(2,1)S(1)} %get-tuple-element.56), channel_id=1, source_target_pairs={{0,1},{1,0},{2,3},{3,2},{4,5},{5,4},{6,7},{7,6},{8,9},{9,8},{10,11... | collective-permute-start | bytes 835592 | tf_op jit(solution)/shard_map/ppermute | solution.py:22
  14.2 0.6 %project.2 = (f32[64,3200]{1,0:T(8,128)S(1)}, bf16[64,3200]{1,0:T(8,128)(2,1)S(1)}) custom-call(bf16[128,512]{1,0:T(8,128)(2,1)S(1)} %get-tuple-element.53.rows, bf16[512,5376]{1,0:T(8,128)(2,1)S(1)} %get-tuple-element.44.weight), custom_call_target="tpu_custom_call" | custom-call | flops 419430400 | tf_op jit(solution)/shard_map/project/pallas_call | solution.py:302
  14.8 0.6 %collective-permute-done.10.theirs = bf16[64,2176]{1,0:T(8,128)(2,1)S(1)} collective-permute-done((bf16[64,2176]{1,0:T(8,128)(2,1)S(1)}, bf16[64,2176]{1,0:T(8,128)(2,1)S(1)}, u32[]{:S(2)}, u32[]{:S(2)}) %collective-permute-start.10) | collective-permute-done | bytes 278560 | tf_op jit(solution)/shard_map/ppermute | solution.py:22
  15.4 0.4 %collective-permute-start.11 = (bf16[64,3200]{1,0:T(8,128)(2,1)S(1)}, bf16[64,3200]{1,0:T(8,128)(2,1)S(1)}, u32[]{:S(2)}, u32[]{:S(2)}) collective-permute-start(bf16[64,3200]{1,0:T(8,128)(2,1)S(1)} %get-tuple-element.61), channel_id=1, source_target_pairs={{0,1},{1,0},{2,3},{3,2},{4,5},{5,4},{6,7},{7,6},{8,9},{9,8},{10,11... | collective-permute-start | bytes 1228808 | tf_op jit(solution)/shard_map/ppermute | solution.py:22
  15.8 1.5 %collective-permute-start.15 = (bf16[64,1536]{1,0:T(8,128)(2,1)S(1)}, bf16[64,1536]{1,0:T(8,128)(2,1)S(1)}, u32[]{:S(2)}, u32[]{:S(2)}) collective-permute-start(bf16[64,1536]{1,0:T(8,128)(2,1)S(1)} %get-tuple-element.57), channel_id=1, source_target_pairs={{0,2},{1,3},{2,0},{3,1},{4,6},{5,7},{6,4},{7,5},{8,10},{9,11},{10,... | collective-permute-start | bytes 589832 | tf_op jit(solution)/shard_map/ppermute | solution.py:22
  17.4 0.1 add_up.3
  17.4 1.4 %collective-permute-start.12 = (bf16[64,3200]{1,0:T(8,128)(2,1)S(1)}, bf16[64,3200]{1,0:T(8,128)(2,1)S(1)}, u32[]{:S(2)}, u32[]{:S(2)}) collective-permute-start(bf16[64,3200]{1,0:T(8,128)(2,1)S(1)} %add_up.3), channel_id=1, source_target_pairs={{0,2},{1,3},{2,0},{3,1},{4,6},{5,7},{6,4},{7,5},{8,10},{9,11},{10,... | collective-permute-start | bytes 1228808 | tf_op jit(solution)/shard_map/ppermute | solution.py:22
  18.9 0.9 %project.3 = (f32[64,5376]{1,0:T(8,128)S(1)}, bf16[64,1792]{1,0:T(8,128)(2,1)S(1)}, bf16[64,1792]{1,0:T(8,128)(2,1)S(1)}, bf16[64,1792]{1,0:T(8,128)(2,1)S(1)}) custom-call(bf16[128,512]{1,0:T(8,128)(2,1)S(1)} %get-tuple-element.62.rows, bf16[512,5376]{1,0:T(8,128)(2,1)S(1)} %get-tuple-element.44.weight), custom_call_target="tpu_custom_call" | custom-call | flops 704643072 | tf_op jit(solution)/shard_map/project/pallas_call | solution.py:302
  19.8 0.1 collective-permute-start.18
  19.9 8.6 %collective-permute-start.14 = (bf16[64,640]{1,0:T(8,128)(2,1)S(1)}, bf16[64,640]{1,0:T(8,128)(2,1)S(1)}, u32[]{:S(2)}, u32[]{:S(2)}) collective-permute-start(bf16[64,640]{1,0:T(8,128)(2,1)S(1)} %get-tuple-element.64), channel_id=1, source_target_pairs={{0,1},{1,0},{2,3},{3,2},{4,5},{5,4},{6,7},{7,6},{8,9},{9,8},{10,11... | collective-permute-start | bytes 245768 | tf_op jit(solution)/shard_map/ppermute | solution.py:46
  28.6 0.2 collective-permute-start.19
  28.7 0.3 collective-permute-start.20
  29.1 2.5 %collective-permute-done.14 = bf16[64,640]{1,0:T(8,128)(2,1)S(1)} collective-permute-done((bf16[64,640]{1,0:T(8,128)(2,1)S(1)}, bf16[64,640]{1,0:T(8,128)(2,1)S(1)}, u32[]{:S(2)}, u32[]{:S(2)}) %collective-permute-start.14) | collective-permute-done | bytes 81952 | tf_op jit(solution)/shard_map/ppermute | solution.py:46
  31.6 0.5 %collective-permute-start.16 = (bf16[64,640]{1,0:T(8,128)(2,1)S(1)}, bf16[64,640]{1,0:T(8,128)(2,1)S(1)}, u32[]{:S(2)}, u32[]{:S(2)}) collective-permute-start(bf16[64,640]{1,0:T(8,128)(2,1)S(1)} %collective-permute-done.14), channel_id=1, source_target_pairs={{0,1},{1,0},{2,3},{3,2},{4,5},{5,4},{6,7},{7,6},{8,9},{9,8},{10,11... | collective-permute-start | bytes 245768 | tf_op jit(solution)/shard_map/ppermute | solution.py:46
  32.1 3.9 %collective-permute-done.16 = bf16[64,640]{1,0:T(8,128)(2,1)S(1)} collective-permute-done((bf16[64,640]{1,0:T(8,128)(2,1)S(1)}, bf16[64,640]{1,0:T(8,128)(2,1)S(1)}, u32[]{:S(2)}, u32[]{:S(2)}) %collective-permute-start.16) | collective-permute-done | bytes 81952 | tf_op jit(solution)/shard_map/ppermute | solution.py:46
  36.0 0.5 %collective-permute-start.13 = (bf16[64,640]{1,0:T(8,128)(2,1)S(1)}, bf16[64,640]{1,0:T(8,128)(2,1)S(1)}, u32[]{:S(2)}, u32[]{:S(2)}) collective-permute-start(bf16[64,640]{1,0:T(8,128)(2,1)S(1)} %get-tuple-element.64), channel_id=1, source_target_pairs={{0,2},{1,3},{2,0},{3,1},{4,6},{5,7},{6,4},{7,5},{8,10},{9,11},{10,... | collective-permute-start | bytes 245768 | tf_op jit(solution)/shard_map/ppermute | solution.py:46
  36.6 0.7 %combine.2.refs_7_ = bf16[64,5376]{1,0:T(8,128)(2,1)} custom-call(f32[64,5376]{1,0:T(8,128)S(1)} %get-tuple-element.63.refs_0_, bf16[64,1536]{1,0:T(8,128)(2,1)S(1)} %collective-permute-done.15.refs_1_, bf16[64,1792]{1,0:T(8,128)(2,1)S(1)} %collective-permute-done.18.refs_2_.refs_4_, bf16[64,1792]{1,0:T(8,128)(2,1)S(1)} %collective-permute-done.19.refs_3_.refs_5_, ...), custom_call_target="tpu_custom_call" | custom-call | tf_op jit(solution)/shard_map/combine/pallas_call | solution.py:371
  37.4 3.1 %collective-permute-done.13.refs_2_ = bf16[64,640]{1,0:T(8,128)(2,1)S(1)} collective-permute-done((bf16[64,640]{1,0:T(8,128)(2,1)S(1)}, bf16[64,640]{1,0:T(8,128)(2,1)S(1)}, u32[]{:S(2)}, u32[]{:S(2)}) %collective-permute-start.13) | collective-permute-done | bytes 81952 | tf_op jit(solution)/shard_map/ppermute | solution.py:46
  40.5 0.5 %collective-permute-done.17.refs_3_ = bf16[64,640]{1,0:T(8,128)(2,1)S(1)} collective-permute-done((bf16[64,640]{1,0:T(8,128)(2,1)S(1)}, bf16[64,640]{1,0:T(8,128)(2,1)S(1)}, u32[]{:S(2)}, u32[]{:S(2)}) %collective-permute-start.17) | collective-permute-done | bytes 81952 | tf_op jit(solution)/shard_map/ppermute | solution.py:46
  41.0 0.9 %combine.3 = bf16[64,5376]{1,0:T(8,128)(2,1)} custom-call(f32[64,5376]{1,0:T(8,128)S(1)} %get-tuple-element.63.refs_0_, bf16[64,3200]{1,0:T(8,128)(2,1)S(1)} %collective-permute-done.12.refs_1_, bf16[64,640]{1,0:T(8,128)(2,1)S(1)} %collective-permute-done.13.refs_2_, ...), custom_call_target="tpu_custom_call", output_to_operand_aliasing={{}: (7, {})} | custom-call | tf_op jit(solution)/shard_map/combine/pallas_call | solution.py:371
  (19 shorter events, 0.1 us)
Async XLA Ops:
  0.0 3.9 %collective-permute-start.2 = (bf16[256,256]{1,0:T(8,128)(2,1)}, bf16[256,256]{1,0:T(8,128)(2,1)S(1)}, u32[]{:S(2)}, u32[]{:S(2)}) collective-permute-start(bf16[256,256]{1,0:T(8,128)(2,1)} %keys_in.1), channel_id=1, source_target_pairs={{0,8},{1,9},{2,10},{3,11},{4,12},{5,13},{6,14},{7,15},{8,16},{9,17... | collective-permute-start | bytes 393224 | tf_op jit(solution)/shard_map/ppermute | solution.py:46
  0.0 6.5 %collective-permute-start = (bf16[256,256]{1,0:T(8,128)(2,1)}, bf16[256,256]{1,0:T(8,128)(2,1)S(1)}, u32[]{:S(2)}, u32[]{:S(2)}) collective-permute-start(bf16[256,256]{1,0:T(8,128)(2,1)} %keys_in.1), channel_id=1, source_target_pairs={{0,4},{1,5},{2,6},{3,7},{4,0},{5,1},{6,2},{7,3},{8,12},{9,13},{10,... | collective-permute-start | bytes 393224 | tf_op jit(solution)/shard_map/ppermute | solution.py:46
  1.5 5.0 %collective-permute-start.3 = (bf16[256,256]{1,0:T(8,128)(2,1)}, bf16[256,256]{1,0:T(8,128)(2,1)S(1)}, u32[]{:S(2)}, u32[]{:S(2)}) collective-permute-start(bf16[256,256]{1,0:T(8,128)(2,1)} %values_in.1), channel_id=1, source_target_pairs={{0,8},{1,9},{2,10},{3,11},{4,12},{5,13},{6,14},{7,15},{8,16},{9,17... | collective-permute-start | bytes 393224 | tf_op jit(solution)/shard_map/ppermute | solution.py:46
  1.8 7.2 %collective-permute-start.1 = (bf16[256,256]{1,0:T(8,128)(2,1)}, bf16[256,256]{1,0:T(8,128)(2,1)S(1)}, u32[]{:S(2)}, u32[]{:S(2)}) collective-permute-start(bf16[256,256]{1,0:T(8,128)(2,1)} %values_in.1), channel_id=1, source_target_pairs={{0,4},{1,5},{2,6},{3,7},{4,0},{5,1},{6,2},{7,3},{8,12},{9,13},{10,... | collective-permute-start | bytes 393224 | tf_op jit(solution)/shard_map/ppermute | solution.py:46
  3.9 5.1 %collective-permute-start.4 = (bf16[256,256]{1,0:T(8,128)(2,1)S(1)}, bf16[256,256]{1,0:T(8,128)(2,1)S(1)}, u32[]{:S(2)}, u32[]{:S(2)}) collective-permute-start(bf16[256,256]{1,0:T(8,128)(2,1)S(1)} %collective-permute-done.2.refs_5_), channel_id=1, source_target_pairs={{0,1},{1,0},{2,3},{3,2},{4,5},{5,4},{6,7},{7,6},{8,16},{9,17},{10,... | collective-permute-start | bytes 393224 | tf_op jit(solution)/shard_map/ppermute | solution.py:46
  6.5 2.4 %collective-permute-start.6 = (bf16[256,256]{1,0:T(8,128)(2,1)S(1)}, bf16[256,256]{1,0:T(8,128)(2,1)S(1)}, u32[]{:S(2)}, u32[]{:S(2)}) collective-permute-start(bf16[256,256]{1,0:T(8,128)(2,1)S(1)} %collective-permute-done.2.refs_5_), channel_id=1, source_target_pairs={{0,1},{1,0},{2,3},{3,2},{4,5},{5,4},{6,7},{7,6},{8,12},{9,13},{10,... | collective-permute-start | bytes 393224 | tf_op jit(solution)/shard_map/ppermute | solution.py:46
  6.5 2.9 %collective-permute-start.5 = (bf16[256,256]{1,0:T(8,128)(2,1)S(1)}, bf16[256,256]{1,0:T(8,128)(2,1)S(1)}, u32[]{:S(2)}, u32[]{:S(2)}) collective-permute-start(bf16[256,256]{1,0:T(8,128)(2,1)S(1)} %collective-permute-done.3.refs_6_), channel_id=1, source_target_pairs={{0,1},{1,0},{2,3},{3,2},{4,5},{5,4},{6,7},{7,6},{8,16},{9,17},{10,... | collective-permute-start | bytes 393224 | tf_op jit(solution)/shard_map/ppermute | solution.py:46
  8.9 3.2 %collective-permute-start.7 = (bf16[256,256]{1,0:T(8,128)(2,1)S(1)}, bf16[256,256]{1,0:T(8,128)(2,1)S(1)}, u32[]{:S(2)}, u32[]{:S(2)}) collective-permute-start(bf16[256,256]{1,0:T(8,128)(2,1)S(1)} %collective-permute-done.3.refs_6_), channel_id=1, source_target_pairs={{0,1},{1,0},{2,3},{3,2},{4,5},{5,4},{6,7},{7,6},{8,12},{9,13},{10,... | collective-permute-start | bytes 393224 | tf_op jit(solution)/shard_map/ppermute | solution.py:46
  8.9 3.2 %collective-permute-start.8 = (bf16[256,256]{1,0:T(8,128)(2,1)S(1)}, bf16[256,256]{1,0:T(8,128)(2,1)S(1)}, u32[]{:S(2)}, u32[]{:S(2)}) collective-permute-start(bf16[256,256]{1,0:T(8,128)(2,1)S(1)} %collective-permute-done.6.refs_3_), channel_id=1, source_target_pairs={{0,1},{1,0},{2,3},{3,2},{4,5},{5,4},{6,7},{7,6},{8,16},{9,17},{10,... | collective-permute-start | bytes 393224 | tf_op jit(solution)/shard_map/ppermute | solution.py:46
  9.5 2.7 %collective-permute-start.9 = (bf16[256,256]{1,0:T(8,128)(2,1)S(1)}, bf16[256,256]{1,0:T(8,128)(2,1)S(1)}, u32[]{:S(2)}, u32[]{:S(2)}) collective-permute-start(bf16[256,256]{1,0:T(8,128)(2,1)S(1)} %collective-permute-done.5.refs_8_), channel_id=1, source_target_pairs={{0,1},{1,0},{2,3},{3,2},{4,5},{5,4},{6,7},{7,6},{8,9},{9,8},{10,11... | collective-permute-start | bytes 393224 | tf_op jit(solution)/shard_map/ppermute | solution.py:46
  13.7 1.7 %collective-permute-start.10 = (bf16[64,2176]{1,0:T(8,128)(2,1)S(1)}, bf16[64,2176]{1,0:T(8,128)(2,1)S(1)}, u32[]{:S(2)}, u32[]{:S(2)}) collective-permute-start(bf16[64,2176]{1,0:T(8,128)(2,1)S(1)} %get-tuple-element.56), channel_id=1, source_target_pairs={{0,1},{1,0},{2,3},{3,2},{4,5},{5,4},{6,7},{7,6},{8,9},{9,8},{10,11... | collective-permute-start | bytes 835592 | tf_op jit(solution)/shard_map/ppermute | solution.py:22
  15.4 1.9 %collective-permute-start.11 = (bf16[64,3200]{1,0:T(8,128)(2,1)S(1)}, bf16[64,3200]{1,0:T(8,128)(2,1)S(1)}, u32[]{:S(2)}, u32[]{:S(2)}) collective-permute-start(bf16[64,3200]{1,0:T(8,128)(2,1)S(1)} %get-tuple-element.61), channel_id=1, source_target_pairs={{0,1},{1,0},{2,3},{3,2},{4,5},{5,4},{6,7},{7,6},{8,9},{9,8},{10,11... | collective-permute-start | bytes 1228808 | tf_op jit(solution)/shard_map/ppermute | solution.py:22
  15.8 12.9 %collective-permute-start.15 = (bf16[64,1536]{1,0:T(8,128)(2,1)S(1)}, bf16[64,1536]{1,0:T(8,128)(2,1)S(1)}, u32[]{:S(2)}, u32[]{:S(2)}) collective-permute-start(bf16[64,1536]{1,0:T(8,128)(2,1)S(1)} %get-tuple-element.57), channel_id=1, source_target_pairs={{0,2},{1,3},{2,0},{3,1},{4,6},{5,7},{6,4},{7,5},{8,10},{9,11},{10,... | collective-permute-start | bytes 589832 | tf_op jit(solution)/shard_map/ppermute | solution.py:22
  17.4 23.6 %collective-permute-start.12 = (bf16[64,3200]{1,0:T(8,128)(2,1)S(1)}, bf16[64,3200]{1,0:T(8,128)(2,1)S(1)}, u32[]{:S(2)}, u32[]{:S(2)}) collective-permute-start(bf16[64,3200]{1,0:T(8,128)(2,1)S(1)} %add_up.3), channel_id=1, source_target_pairs={{0,2},{1,3},{2,0},{3,1},{4,6},{5,7},{6,4},{7,5},{8,10},{9,11},{10,... | collective-permute-start | bytes 1228808 | tf_op jit(solution)/shard_map/ppermute | solution.py:22
  19.8 16.8 %collective-permute-start.18 = (bf16[64,1792]{1,0:T(8,128)(2,1)S(1)}, bf16[64,1792]{1,0:T(8,128)(2,1)S(1)}, u32[]{:S(2)}, u32[]{:S(2)}) collective-permute-start(bf16[64,1792]{1,0:T(8,128)(2,1)S(1)} %get-tuple-element.66), channel_id=1, source_target_pairs={{0,1},{1,0},{2,3},{3,2},{4,5},{5,4},{6,7},{7,6},{8,9},{9,8},{10,11... | collective-permute-start | bytes 688136 | tf_op jit(solution)/shard_map/ppermute | solution.py:22
  19.9 11.7 %collective-permute-start.14 = (bf16[64,640]{1,0:T(8,128)(2,1)S(1)}, bf16[64,640]{1,0:T(8,128)(2,1)S(1)}, u32[]{:S(2)}, u32[]{:S(2)}) collective-permute-start(bf16[64,640]{1,0:T(8,128)(2,1)S(1)} %get-tuple-element.64), channel_id=1, source_target_pairs={{0,1},{1,0},{2,3},{3,2},{4,5},{5,4},{6,7},{7,6},{8,9},{9,8},{10,11... | collective-permute-start | bytes 245768 | tf_op jit(solution)/shard_map/ppermute | solution.py:46
  28.6 8.0 %collective-permute-start.19 = (bf16[64,1792]{1,0:T(8,128)(2,1)S(1)}, bf16[64,1792]{1,0:T(8,128)(2,1)S(1)}, u32[]{:S(2)}, u32[]{:S(2)}) collective-permute-start(bf16[64,1792]{1,0:T(8,128)(2,1)S(1)} %get-tuple-element.67), channel_id=1, source_target_pairs={{0,1},{1,0},{2,3},{3,2},{4,5},{5,4},{6,7},{7,6},{8,9},{9,8},{10,11... | collective-permute-start | bytes 688136 | tf_op jit(solution)/shard_map/ppermute | solution.py:22
  28.7 7.9 %collective-permute-start.20 = (bf16[64,1792]{1,0:T(8,128)(2,1)S(1)}, bf16[64,1792]{1,0:T(8,128)(2,1)S(1)}, u32[]{:S(2)}, u32[]{:S(2)}) collective-permute-start(bf16[64,1792]{1,0:T(8,128)(2,1)S(1)} %get-tuple-element.68), channel_id=1, source_target_pairs={{0,1},{1,0},{2,3},{3,2},{4,5},{5,4},{6,7},{7,6},{8,9},{9,8},{10,11... | collective-permute-start | bytes 688136 | tf_op jit(solution)/shard_map/ppermute | solution.py:22
  31.6 4.4 %collective-permute-start.16 = (bf16[64,640]{1,0:T(8,128)(2,1)S(1)}, bf16[64,640]{1,0:T(8,128)(2,1)S(1)}, u32[]{:S(2)}, u32[]{:S(2)}) collective-permute-start(bf16[64,640]{1,0:T(8,128)(2,1)S(1)} %collective-permute-done.14), channel_id=1, source_target_pairs={{0,1},{1,0},{2,3},{3,2},{4,5},{5,4},{6,7},{7,6},{8,9},{9,8},{10,11... | collective-permute-start | bytes 245768 | tf_op jit(solution)/shard_map/ppermute | solution.py:46
  36.0 4.4 %collective-permute-start.13 = (bf16[64,640]{1,0:T(8,128)(2,1)S(1)}, bf16[64,640]{1,0:T(8,128)(2,1)S(1)}, u32[]{:S(2)}, u32[]{:S(2)}) collective-permute-start(bf16[64,640]{1,0:T(8,128)(2,1)S(1)} %get-tuple-element.64), channel_id=1, source_target_pairs={{0,2},{1,3},{2,0},{3,1},{4,6},{5,7},{6,4},{7,5},{8,10},{9,11},{10,... | collective-permute-start | bytes 245768 | tf_op jit(solution)/shard_map/ppermute | solution.py:46
  36.6 4.4 %collective-permute-start.17 = (bf16[64,640]{1,0:T(8,128)(2,1)S(1)}, bf16[64,640]{1,0:T(8,128)(2,1)S(1)}, u32[]{:S(2)}, u32[]{:S(2)}) collective-permute-start(bf16[64,640]{1,0:T(8,128)(2,1)S(1)} %collective-permute-done.16), channel_id=1, source_target_pairs={{0,1},{1,0},{2,3},{3,2},{4,5},{5,4},{6,7},{7,6},{8,9},{9,8},{10,11... | collective-permute-start | bytes 245768 | tf_op jit(solution)/shard_map/ppermute | solution.py:46

commit v5 on v4

--- a/solution.py
+++ b/solution.py
@@ -498,12 +498,13 @@
     later_mine = after(later_mine, first_sum)
     (later_sum,) = add_up(later_mine, later_theirs, [columns - cuts[2]])
     later_part = hop(later_sum, "head", other_chip)
-    mine, *sends = project(after(near, later_sum), weight, (0, columns), 3)
+    mine, *sends = project(after(near, later_sum), weight, (0, columns), 2)
     theirs = [hop(send, "head", other_core) for send in sends]
     if n_ctx == 8:
+        arrived = move(after(relay_sum, mine), RELAY)
         direct = move(relay_sum, (), [i for i in range(n_ctx) if i not in LATE])
-        arrived = move(after(relay_sum, mine), RELAY)
-        relay_part = (direct, move(move(after(arrived, first_part), (), [ring[1] for ring in RELAY]), RELAY))
+        relayed = move(after(arrived, first_part), (), [ring[1] for ring in RELAY])
+        relay_part = (direct, move(after(relayed, direct), RELAY))
     else:
         relay_part = hop(relay_sum, "head", other_chip)
     out = combine(mine, theirs, [first_part], [0])

time: 42.1 us -> 42.7 us (1.014)
  the two profiles are of different devices: /device:TPU:24 before, /device:TPU:13 now
where the time goes in v5:
time: 42.7 us; the launch traced here: 42.5 us
  starting transfers between devices  18.4 us (43%)
  waiting for transfers between devices  15 us (35%)
  Pallas kernels  9.02 us (21%)
    ppermute x14, starting transfers between devices, move(): return lax.ppermute(block, ('ctx', 'head'), pairs)  12.9 us
    ppermute x14, waiting for transfers between devices, move(): return lax.ppermute(block, ('ctx', 'head'), pairs)  12.8 us
    ppermute x6, starting transfers between devices, hop(): return lax.ppermute(block, axis, pairs)  5.52 us
    pallas_call x1, Pallas kernels, attend_next(): pl.pallas_call(functools.partial(next_kernel, numbers), out_shape=state_s...  2.59 us
    ppermute x6, waiting for transfers between devices, hop(): return lax.ppermute(block, axis, pairs)  2.22 us
    pallas_call x2, Pallas kernels, combine(): pl.pallas_call(kernel, out_shape=jax.ShapeDtypeStruct(mine.shape, jnp.bfl...  1.66 us
    pallas_call x1, Pallas kernels, attend_first(): pl.pallas_call(first_kernel, out_shape=state_shapes(queries) + (pltpu.VME...  1.61 us
    pallas_call x2, Pallas kernels, project(): pl.pallas_call(functools.partial(project_kernel, columns), out_shape=proj...  1.54 us
  transfers between devices with their start and end apart: 20, of which 10 were waited for; matrix products, arithmetic and copies ran while one was open for 0% of the time, Pallas kernels for 15%

profile of v5, /device:TPU:13, one launch (start us, length us, event | category | flops | bytes accessed | tf_op | source)
XLA Modules:
  0.0 42.5 jit_solution(5850644458812749673)
XLA Ops:
  0.0 1.3 %collective-permute-start.2 = (bf16[256,256]{1,0:T(8,128)(2,1)}, bf16[256,256]{1,0:T(8,128)(2,1)S(1)}, u32[]{:S(2)}, u32[]{:S(2)}) collective-permute-start(bf16[256,256]{1,0:T(8,128)(2,1)} %keys_in.1), channel_id=1, source_target_pairs={{0,8},{1,9},{2,10},{3,11},{4,12},{5,13},{6,14},{7,15},{8,16},{9,17... | collective-permute-start | bytes 393224 | tf_op jit(solution)/shard_map/ppermute | solution.py:46
  1.3 0.2 collective-permute-start
  1.5 1.3 %collective-permute-start.1 = (bf16[256,256]{1,0:T(8,128)(2,1)}, bf16[256,256]{1,0:T(8,128)(2,1)S(1)}, u32[]{:S(2)}, u32[]{:S(2)}) collective-permute-start(bf16[256,256]{1,0:T(8,128)(2,1)} %values_in.1), channel_id=1, source_target_pairs={{0,4},{1,5},{2,6},{3,7},{4,0},{5,1},{6,2},{7,3},{8,12},{9,13},{10,... | collective-permute-start | bytes 393224 | tf_op jit(solution)/shard_map/ppermute | solution.py:46
  2.8 1.6 %attend_first.1 = (f32[1024,128]{1,0:T(8,128)S(1)}, f32[1024,128]{1,0:T(8,128)S(1)}, f32[1024,128]{1,0:T(8,128)S(1)}, bf16[256,512]{1,0:T(8,128)(2,1)S(1)}, f32[16,256]{1,0:T(8,128)S(1)}) custom-call(s32[16]{0:T(128)} %docs_in.1, bf16[256,512]{1,0:T(8,128)(2,1)} %queries_in.1, bf16[256,256]{1,0:T(8,128)(2,1)} %keys_in.1, bf16[256,256]{1,0:T(8,128)(2,1)} %values_in.1), custom_call_target="tpu_custom_call" | custom-call | flops 134217728 | tf_op jit(solution)/shard_map/attend_first/pallas_call | solution.py:202
  4.6 1.3 %collective-permute-start.4 = (bf16[256,256]{1,0:T(8,128)(2,1)S(1)}, bf16[256,256]{1,0:T(8,128)(2,1)S(1)}, u32[]{:S(2)}, u32[]{:S(2)}) collective-permute-start(bf16[256,256]{1,0:T(8,128)(2,1)S(1)} %collective-permute-done.2.refs_5_), channel_id=1, source_target_pairs={{0,1},{1,0},{2,3},{3,2},{4,5},{5,4},{6,7},{7,6},{8,16},{9,17},{10,... | collective-permute-start | bytes 393224 | tf_op jit(solution)/shard_map/ppermute | solution.py:46
  5.9 0.2 collective-permute-start.6
  6.1 1.3 %collective-permute-done.3.refs_6_ = bf16[256,256]{1,0:T(8,128)(2,1)S(1)} collective-permute-done((bf16[256,256]{1,0:T(8,128)(2,1)}, bf16[256,256]{1,0:T(8,128)(2,1)S(1)}, u32[]{:S(2)}, u32[]{:S(2)}) %collective-permute-start.3) | collective-permute-done | bytes 131104 | tf_op jit(solution)/shard_map/ppermute | solution.py:46
  7.4 1.3 %collective-permute-start.5 = (bf16[256,256]{1,0:T(8,128)(2,1)S(1)}, bf16[256,256]{1,0:T(8,128)(2,1)S(1)}, u32[]{:S(2)}, u32[]{:S(2)}) collective-permute-start(bf16[256,256]{1,0:T(8,128)(2,1)S(1)} %collective-permute-done.3.refs_6_), channel_id=1, source_target_pairs={{0,1},{1,0},{2,3},{3,2},{4,5},{5,4},{6,7},{7,6},{8,16},{9,17},{10,... | collective-permute-start | bytes 393224 | tf_op jit(solution)/shard_map/ppermute | solution.py:46
  8.7 0.2 collective-permute-start.7
  8.9 0.9 %collective-permute-done.4.refs_7_ = bf16[256,256]{1,0:T(8,128)(2,1)S(1)} collective-permute-done((bf16[256,256]{1,0:T(8,128)(2,1)S(1)}, bf16[256,256]{1,0:T(8,128)(2,1)S(1)}, u32[]{:S(2)}, u32[]{:S(2)}) %collective-permute-start.4) | collective-permute-done | bytes 131104 | tf_op jit(solution)/shard_map/ppermute | solution.py:46
  9.8 1.4 %collective-permute-done.6.refs_3_ = bf16[256,256]{1,0:T(8,128)(2,1)S(1)} collective-permute-done((bf16[256,256]{1,0:T(8,128)(2,1)S(1)}, bf16[256,256]{1,0:T(8,128)(2,1)S(1)}, u32[]{:S(2)}, u32[]{:S(2)}) %collective-permute-start.6) | collective-permute-done | bytes 131104 | tf_op jit(solution)/shard_map/ppermute | solution.py:46
  11.2 1.3 %collective-permute-done.5.refs_8_ = bf16[256,256]{1,0:T(8,128)(2,1)S(1)} collective-permute-done((bf16[256,256]{1,0:T(8,128)(2,1)S(1)}, bf16[256,256]{1,0:T(8,128)(2,1)S(1)}, u32[]{:S(2)}, u32[]{:S(2)}) %collective-permute-start.5) | collective-permute-done | bytes 131104 | tf_op jit(solution)/shard_map/ppermute | solution.py:46
  12.6 2.6 %collective-permute-start.9 = (bf16[256,256]{1,0:T(8,128)(2,1)S(1)}, bf16[256,256]{1,0:T(8,128)(2,1)S(1)}, u32[]{:S(2)}, u32[]{:S(2)}) collective-permute-start(bf16[256,256]{1,0:T(8,128)(2,1)S(1)} %collective-permute-done.5.refs_8_), channel_id=1, source_target_pairs={{0,1},{1,0},{2,3},{3,2},{4,5},{5,4},{6,7},{7,6},{8,9},{9,8},{10,11... | collective-permute-start | bytes 393224 | tf_op jit(solution)/shard_map/ppermute | solution.py:46
  15.2 2.6 %attend_next.1 = (f32[1024,128]{1,0:T(8,128)S(1)}, f32[1024,128]{1,0:T(8,128)S(1)}, f32[1024,128]{1,0:T(8,128)S(1)}, bf16[512,5376]{1,0:T(8,128)(2,1)S(1)}) custom-call(bf16[256,512]{1,0:T(8,128)(2,1)S(1)} %get-tuple-element.37.queries, f32[16,256]{1,0:T(8,128)S(1)} %get-tuple-element.38.open_beside, bf16[512,5376]{1,0:T(8,128)(2,1)} %weight_in.1, ...), custom_call_target="tpu_custom_call" | custom-call | flops 402653184 | bytes 5505024 | tf_op jit(solution)/shard_map/attend_next/pallas_call | solution.py:224
  17.8 1.5 %attend_last.1 = (bf16[128,512]{1,0:T(8,128)(2,1)S(1)}, bf16[128,512]{1,0:T(8,128)(2,1)S(1)}, f32[64,2176]{1,0:T(8,128)S(1)}, bf16[64,2176]{1,0:T(8,128)(2,1)S(1)}) custom-call(bf16[256,512]{1,0:T(8,128)(2,1)S(1)} %get-tuple-element.37.queries, bf16[512,5376]{1,0:T(8,128)(2,1)S(1)} %get-tuple-element.44.weight, f32[1024,128]{1,0:T(8,128)S(1)} %get-tuple-element.45.refs_0_, ...), custom_call_target="tpu_custom_call" | custom-call | flops 268435456 | tf_op jit(solution)/shard_map/attend_last/pallas_call | solution.py:267
  19.3 1.8 %collective-permute-start.10 = (bf16[64,2176]{1,0:T(8,128)(2,1)S(1)}, bf16[64,2176]{1,0:T(8,128)(2,1)S(1)}, u32[]{:S(2)}, u32[]{:S(2)}) collective-permute-start(bf16[64,2176]{1,0:T(8,128)(2,1)S(1)} %get-tuple-element.56), channel_id=1, source_target_pairs={{0,1},{1,0},{2,3},{3,2},{4,5},{5,4},{6,7},{7,6},{8,9},{9,8},{10,11... | collective-permute-start | bytes 835592 | tf_op jit(solution)/shard_map/ppermute | solution.py:22
  21.1 0.6 %project.2 = (f32[64,3200]{1,0:T(8,128)S(1)}, bf16[64,3200]{1,0:T(8,128)(2,1)S(1)}) custom-call(bf16[128,512]{1,0:T(8,128)(2,1)S(1)} %get-tuple-element.53.rows, bf16[512,5376]{1,0:T(8,128)(2,1)S(1)} %get-tuple-element.44.weight), custom_call_target="tpu_custom_call" | custom-call | flops 419430400 | tf_op jit(solution)/shard_map/project/pallas_call | solution.py:302
  21.8 0.6 %collective-permute-done.10.theirs = bf16[64,2176]{1,0:T(8,128)(2,1)S(1)} collective-permute-done((bf16[64,2176]{1,0:T(8,128)(2,1)S(1)}, bf16[64,2176]{1,0:T(8,128)(2,1)S(1)}, u32[]{:S(2)}, u32[]{:S(2)}) %collective-permute-start.10) | collective-permute-done | bytes 278560 | tf_op jit(solution)/shard_map/ppermute | solution.py:22
  22.4 0.4 %collective-permute-start.11 = (bf16[64,3200]{1,0:T(8,128)(2,1)S(1)}, bf16[64,3200]{1,0:T(8,128)(2,1)S(1)}, u32[]{:S(2)}, u32[]{:S(2)}) collective-permute-start(bf16[64,3200]{1,0:T(8,128)(2,1)S(1)} %get-tuple-element.61), channel_id=1, source_target_pairs={{0,1},{1,0},{2,3},{3,2},{4,5},{5,4},{6,7},{7,6},{8,9},{9,8},{10,11... | collective-permute-start | bytes 1228808 | tf_op jit(solution)/shard_map/ppermute | solution.py:22
  22.8 1.2 %collective-permute-start.15 = (bf16[64,1536]{1,0:T(8,128)(2,1)S(1)}, bf16[64,1536]{1,0:T(8,128)(2,1)S(1)}, u32[]{:S(2)}, u32[]{:S(2)}) collective-permute-start(bf16[64,1536]{1,0:T(8,128)(2,1)S(1)} %get-tuple-element.57), channel_id=1, source_target_pairs={{0,2},{1,3},{2,0},{3,1},{4,6},{5,7},{6,4},{7,5},{8,10},{9,11},{10,... | collective-permute-start | bytes 589832 | tf_op jit(solution)/shard_map/ppermute | solution.py:22
  24.0 0.2 collective-permute-done.11.theirs
  24.3 1.3 %collective-permute-start.12 = (bf16[64,3200]{1,0:T(8,128)(2,1)S(1)}, bf16[64,3200]{1,0:T(8,128)(2,1)S(1)}, u32[]{:S(2)}, u32[]{:S(2)}) collective-permute-start(bf16[64,3200]{1,0:T(8,128)(2,1)S(1)} %add_up.3), channel_id=1, source_target_pairs={{0,2},{1,3},{2,0},{3,1},{4,6},{5,7},{6,4},{7,5},{8,10},{9,11},{10,... | collective-permute-start | bytes 1228808 | tf_op jit(solution)/shard_map/ppermute | solution.py:22
  25.5 0.9 %project.3 = (f32[64,5376]{1,0:T(8,128)S(1)}, bf16[64,2688]{1,0:T(8,128)(2,1)S(1)}, bf16[64,2688]{1,0:T(8,128)(2,1)S(1)}) custom-call(bf16[128,512]{1,0:T(8,128)(2,1)S(1)} %get-tuple-element.62.rows, bf16[512,5376]{1,0:T(8,128)(2,1)S(1)} %get-tuple-element.44.weight), custom_call_target="tpu_custom_call" | custom-call | flops 704643072 | tf_op jit(solution)/shard_map/project/pallas_call | solution.py:302
  26.5 0.7 %collective-permute-start.18 = (bf16[64,2688]{1,0:T(8,128)(2,1)S(1)}, bf16[64,2688]{1,0:T(8,128)(2,1)S(1)}, u32[]{:S(2)}, u32[]{:S(2)}) collective-permute-start(bf16[64,2688]{1,0:T(8,128)(2,1)S(1)} %get-tuple-element.67), channel_id=1, source_target_pairs={{0,1},{1,0},{2,3},{3,2},{4,5},{5,4},{6,7},{7,6},{8,9},{9,8},{10,11... | collective-permute-start | bytes 1032200 | tf_op jit(solution)/shard_map/ppermute | solution.py:22
  27.3 0.4 %collective-permute-start.14 = (bf16[64,640]{1,0:T(8,128)(2,1)S(1)}, bf16[64,640]{1,0:T(8,128)(2,1)S(1)}, u32[]{:S(2)}, u32[]{:S(2)}) collective-permute-start(bf16[64,640]{1,0:T(8,128)(2,1)S(1)} %get-tuple-element.64), channel_id=1, source_target_pairs={{0,1},{1,0},{2,3},{3,2},{4,5},{5,4},{6,7},{7,6},{8,9},{9,8},{10,11... | collective-permute-start | bytes 245768 | tf_op jit(solution)/shard_map/ppermute | solution.py:46
  27.7 1.5 %collective-permute-done.15.refs_1_ = bf16[64,1536]{1,0:T(8,128)(2,1)S(1)} collective-permute-done((bf16[64,1536]{1,0:T(8,128)(2,1)S(1)}, bf16[64,1536]{1,0:T(8,128)(2,1)S(1)}, u32[]{:S(2)}, u32[]{:S(2)}) %collective-permute-start.15) | collective-permute-done | bytes 196640 | tf_op jit(solution)/shard_map/ppermute | solution.py:22
  29.2 1.2 %collective-permute-start.13 = (bf16[64,640]{1,0:T(8,128)(2,1)S(1)}, bf16[64,640]{1,0:T(8,128)(2,1)S(1)}, u32[]{:S(2)}, u32[]{:S(2)}) collective-permute-start(bf16[64,640]{1,0:T(8,128)(2,1)S(1)} %get-tuple-element.64), channel_id=1, source_target_pairs={{0,2},{1,3},{2,0},{3,1},{4,6},{5,7},{6,4},{7,5},{8,10},{9,11},{10,... | collective-permute-start | bytes 245768 | tf_op jit(solution)/shard_map/ppermute | solution.py:46
  30.4 1.8 %collective-permute-start.16 = (bf16[64,640]{1,0:T(8,128)(2,1)S(1)}, bf16[64,640]{1,0:T(8,128)(2,1)S(1)}, u32[]{:S(2)}, u32[]{:S(2)}) collective-permute-start(bf16[64,640]{1,0:T(8,128)(2,1)S(1)} %collective-permute-done.14), channel_id=1, source_target_pairs={{0,1},{1,0},{2,3},{3,2},{4,5},{5,4},{6,7},{7,6},{8,9},{9,8},{10,11... | collective-permute-start | bytes 245768 | tf_op jit(solution)/shard_map/ppermute | solution.py:46
  32.2 7.5 %collective-permute-done.13.refs_2_ = bf16[64,640]{1,0:T(8,128)(2,1)S(1)} collective-permute-done((bf16[64,640]{1,0:T(8,128)(2,1)S(1)}, bf16[64,640]{1,0:T(8,128)(2,1)S(1)}, u32[]{:S(2)}, u32[]{:S(2)}) %collective-permute-start.13) | collective-permute-done | bytes 81952 | tf_op jit(solution)/shard_map/ppermute | solution.py:46
  39.7 1.0 %collective-permute-start.17 = (bf16[64,640]{1,0:T(8,128)(2,1)S(1)}, bf16[64,640]{1,0:T(8,128)(2,1)S(1)}, u32[]{:S(2)}, u32[]{:S(2)}) collective-permute-start(bf16[64,640]{1,0:T(8,128)(2,1)S(1)} %collective-permute-done.16), channel_id=1, source_target_pairs={{0,1},{1,0},{2,3},{3,2},{4,5},{5,4},{6,7},{7,6},{8,9},{9,8},{10,11... | collective-permute-start | bytes 245768 | tf_op jit(solution)/shard_map/ppermute | solution.py:46
  40.7 0.7 %combine.2.refs_6_ = bf16[64,5376]{1,0:T(8,128)(2,1)} custom-call(f32[64,5376]{1,0:T(8,128)S(1)} %get-tuple-element.63.refs_0_, bf16[64,1536]{1,0:T(8,128)(2,1)S(1)} %collective-permute-done.15.refs_1_, bf16[64,2688]{1,0:T(8,128)(2,1)S(1)} %collective-permute-done.18.refs_2_.refs_4_, bf16[64,2688]{1,0:T(8,128)(2,1)S(1)} %collective-permute-done.19.refs_3_.refs_5_), custom_call_target="tpu_custom_call" | custom-call | tf_op jit(solution)/shard_map/combine/pallas_call | solution.py:371
  41.6 0.9 %combine.3 = bf16[64,5376]{1,0:T(8,128)(2,1)} custom-call(f32[64,5376]{1,0:T(8,128)S(1)} %get-tuple-element.63.refs_0_, bf16[64,3200]{1,0:T(8,128)(2,1)S(1)} %collective-permute-done.12.refs_1_, bf16[64,640]{1,0:T(8,128)(2,1)S(1)} %collective-permute-done.13.refs_2_, ...), custom_call_target="tpu_custom_call", output_to_operand_aliasing={{}: (6, {})} | custom-call | tf_op jit(solution)/shard_map/combine/pallas_call | solution.py:371
  (17 shorter events, 0.5 us)
Async XLA Ops:
  0.0 4.6 %collective-permute-start.2 = (bf16[256,256]{1,0:T(8,128)(2,1)}, bf16[256,256]{1,0:T(8,128)(2,1)S(1)}, u32[]{:S(2)}, u32[]{:S(2)}) collective-permute-start(bf16[256,256]{1,0:T(8,128)(2,1)} %keys_in.1), channel_id=1, source_target_pairs={{0,8},{1,9},{2,10},{3,11},{4,12},{5,13},{6,14},{7,15},{8,16},{9,17... | collective-permute-start | bytes 393224 | tf_op jit(solution)/shard_map/ppermute | solution.py:46
  1.3 4.6 %collective-permute-start = (bf16[256,256]{1,0:T(8,128)(2,1)}, bf16[256,256]{1,0:T(8,128)(2,1)S(1)}, u32[]{:S(2)}, u32[]{:S(2)}) collective-permute-start(bf16[256,256]{1,0:T(8,128)(2,1)} %keys_in.1), channel_id=1, source_target_pairs={{0,4},{1,5},{2,6},{3,7},{4,0},{5,1},{6,2},{7,3},{8,12},{9,13},{10,... | collective-permute-start | bytes 393224 | tf_op jit(solution)/shard_map/ppermute | solution.py:46
  1.5 5.9 %collective-permute-start.3 = (bf16[256,256]{1,0:T(8,128)(2,1)}, bf16[256,256]{1,0:T(8,128)(2,1)S(1)}, u32[]{:S(2)}, u32[]{:S(2)}) collective-permute-start(bf16[256,256]{1,0:T(8,128)(2,1)} %values_in.1), channel_id=1, source_target_pairs={{0,8},{1,9},{2,10},{3,11},{4,12},{5,13},{6,14},{7,15},{8,16},{9,17... | collective-permute-start | bytes 393224 | tf_op jit(solution)/shard_map/ppermute | solution.py:46
  1.5 7.2 %collective-permute-start.1 = (bf16[256,256]{1,0:T(8,128)(2,1)}, bf16[256,256]{1,0:T(8,128)(2,1)S(1)}, u32[]{:S(2)}, u32[]{:S(2)}) collective-permute-start(bf16[256,256]{1,0:T(8,128)(2,1)} %values_in.1), channel_id=1, source_target_pairs={{0,4},{1,5},{2,6},{3,7},{4,0},{5,1},{6,2},{7,3},{8,12},{9,13},{10,... | collective-permute-start | bytes 393224 | tf_op jit(solution)/shard_map/ppermute | solution.py:46
  4.6 5.3 %collective-permute-start.4 = (bf16[256,256]{1,0:T(8,128)(2,1)S(1)}, bf16[256,256]{1,0:T(8,128)(2,1)S(1)}, u32[]{:S(2)}, u32[]{:S(2)}) collective-permute-start(bf16[256,256]{1,0:T(8,128)(2,1)S(1)} %collective-permute-done.2.refs_5_), channel_id=1, source_target_pairs={{0,1},{1,0},{2,3},{3,2},{4,5},{5,4},{6,7},{7,6},{8,16},{9,17},{10,... | collective-permute-start | bytes 393224 | tf_op jit(solution)/shard_map/ppermute | solution.py:46
  5.9 5.4 %collective-permute-start.6 = (bf16[256,256]{1,0:T(8,128)(2,1)S(1)}, bf16[256,256]{1,0:T(8,128)(2,1)S(1)}, u32[]{:S(2)}, u32[]{:S(2)}) collective-permute-start(bf16[256,256]{1,0:T(8,128)(2,1)S(1)} %collective-permute-done.2.refs_5_), channel_id=1, source_target_pairs={{0,1},{1,0},{2,3},{3,2},{4,5},{5,4},{6,7},{7,6},{8,12},{9,13},{10,... | collective-permute-start | bytes 393224 | tf_op jit(solution)/shard_map/ppermute | solution.py:46
  7.4 5.2 %collective-permute-start.5 = (bf16[256,256]{1,0:T(8,128)(2,1)S(1)}, bf16[256,256]{1,0:T(8,128)(2,1)S(1)}, u32[]{:S(2)}, u32[]{:S(2)}) collective-permute-start(bf16[256,256]{1,0:T(8,128)(2,1)S(1)} %collective-permute-done.3.refs_6_), channel_id=1, source_target_pairs={{0,1},{1,0},{2,3},{3,2},{4,5},{5,4},{6,7},{7,6},{8,16},{9,17},{10,... | collective-permute-start | bytes 393224 | tf_op jit(solution)/shard_map/ppermute | solution.py:46
  8.7 9.1 %collective-permute-start.7 = (bf16[256,256]{1,0:T(8,128)(2,1)S(1)}, bf16[256,256]{1,0:T(8,128)(2,1)S(1)}, u32[]{:S(2)}, u32[]{:S(2)}) collective-permute-start(bf16[256,256]{1,0:T(8,128)(2,1)S(1)} %collective-permute-done.3.refs_6_), channel_id=1, source_target_pairs={{0,1},{1,0},{2,3},{3,2},{4,5},{5,4},{6,7},{7,6},{8,12},{9,13},{10,... | collective-permute-start | bytes 393224 | tf_op jit(solution)/shard_map/ppermute | solution.py:46
  11.2 6.6 %collective-permute-start.8 = (bf16[256,256]{1,0:T(8,128)(2,1)S(1)}, bf16[256,256]{1,0:T(8,128)(2,1)S(1)}, u32[]{:S(2)}, u32[]{:S(2)}) collective-permute-start(bf16[256,256]{1,0:T(8,128)(2,1)S(1)} %collective-permute-done.6.refs_3_), channel_id=1, source_target_pairs={{0,1},{1,0},{2,3},{3,2},{4,5},{5,4},{6,7},{7,6},{8,16},{9,17},{10,... | collective-permute-start | bytes 393224 | tf_op jit(solution)/shard_map/ppermute | solution.py:46
  12.6 5.3 %collective-permute-start.9 = (bf16[256,256]{1,0:T(8,128)(2,1)S(1)}, bf16[256,256]{1,0:T(8,128)(2,1)S(1)}, u32[]{:S(2)}, u32[]{:S(2)}) collective-permute-start(bf16[256,256]{1,0:T(8,128)(2,1)S(1)} %collective-permute-done.5.refs_8_), channel_id=1, source_target_pairs={{0,1},{1,0},{2,3},{3,2},{4,5},{5,4},{6,7},{7,6},{8,9},{9,8},{10,11... | collective-permute-start | bytes 393224 | tf_op jit(solution)/shard_map/ppermute | solution.py:46
  19.3 3.0 %collective-permute-start.10 = (bf16[64,2176]{1,0:T(8,128)(2,1)S(1)}, bf16[64,2176]{1,0:T(8,128)(2,1)S(1)}, u32[]{:S(2)}, u32[]{:S(2)}) collective-permute-start(bf16[64,2176]{1,0:T(8,128)(2,1)S(1)} %get-tuple-element.56), channel_id=1, source_target_pairs={{0,1},{1,0},{2,3},{3,2},{4,5},{5,4},{6,7},{7,6},{8,9},{9,8},{10,11... | collective-permute-start | bytes 835592 | tf_op jit(solution)/shard_map/ppermute | solution.py:22
  22.4 1.8 %collective-permute-start.11 = (bf16[64,3200]{1,0:T(8,128)(2,1)S(1)}, bf16[64,3200]{1,0:T(8,128)(2,1)S(1)}, u32[]{:S(2)}, u32[]{:S(2)}) collective-permute-start(bf16[64,3200]{1,0:T(8,128)(2,1)S(1)} %get-tuple-element.61), channel_id=1, source_target_pairs={{0,1},{1,0},{2,3},{3,2},{4,5},{5,4},{6,7},{7,6},{8,9},{9,8},{10,11... | collective-permute-start | bytes 1228808 | tf_op jit(solution)/shard_map/ppermute | solution.py:22
  22.8 6.4 %collective-permute-start.15 = (bf16[64,1536]{1,0:T(8,128)(2,1)S(1)}, bf16[64,1536]{1,0:T(8,128)(2,1)S(1)}, u32[]{:S(2)}, u32[]{:S(2)}) collective-permute-start(bf16[64,1536]{1,0:T(8,128)(2,1)S(1)} %get-tuple-element.57), channel_id=1, source_target_pairs={{0,2},{1,3},{2,0},{3,1},{4,6},{5,7},{6,4},{7,5},{8,10},{9,11},{10,... | collective-permute-start | bytes 589832 | tf_op jit(solution)/shard_map/ppermute | solution.py:22
  24.3 17.3 %collective-permute-start.12 = (bf16[64,3200]{1,0:T(8,128)(2,1)S(1)}, bf16[64,3200]{1,0:T(8,128)(2,1)S(1)}, u32[]{:S(2)}, u32[]{:S(2)}) collective-permute-start(bf16[64,3200]{1,0:T(8,128)(2,1)S(1)} %add_up.3), channel_id=1, source_target_pairs={{0,2},{1,3},{2,0},{3,1},{4,6},{5,7},{6,4},{7,5},{8,10},{9,11},{10,... | collective-permute-start | bytes 1228808 | tf_op jit(solution)/shard_map/ppermute | solution.py:22
  26.5 14.2 %collective-permute-start.18 = (bf16[64,2688]{1,0:T(8,128)(2,1)S(1)}, bf16[64,2688]{1,0:T(8,128)(2,1)S(1)}, u32[]{:S(2)}, u32[]{:S(2)}) collective-permute-start(bf16[64,2688]{1,0:T(8,128)(2,1)S(1)} %get-tuple-element.67), channel_id=1, source_target_pairs={{0,1},{1,0},{2,3},{3,2},{4,5},{5,4},{6,7},{7,6},{8,9},{9,8},{10,11... | collective-permute-start | bytes 1032200 | tf_op jit(solution)/shard_map/ppermute | solution.py:22
  27.2 13.5 %collective-permute-start.19 = (bf16[64,2688]{1,0:T(8,128)(2,1)S(1)}, bf16[64,2688]{1,0:T(8,128)(2,1)S(1)}, u32[]{:S(2)}, u32[]{:S(2)}) collective-permute-start(bf16[64,2688]{1,0:T(8,128)(2,1)S(1)} %get-tuple-element.68), channel_id=1, source_target_pairs={{0,1},{1,0},{2,3},{3,2},{4,5},{5,4},{6,7},{7,6},{8,9},{9,8},{10,11... | collective-permute-start | bytes 1032200 | tf_op jit(solution)/shard_map/ppermute | solution.py:22
  27.3 3.1 %collective-permute-start.14 = (bf16[64,640]{1,0:T(8,128)(2,1)S(1)}, bf16[64,640]{1,0:T(8,128)(2,1)S(1)}, u32[]{:S(2)}, u32[]{:S(2)}) collective-permute-start(bf16[64,640]{1,0:T(8,128)(2,1)S(1)} %get-tuple-element.64), channel_id=1, source_target_pairs={{0,1},{1,0},{2,3},{3,2},{4,5},{5,4},{6,7},{7,6},{8,9},{9,8},{10,11... | collective-permute-start | bytes 245768 | tf_op jit(solution)/shard_map/ppermute | solution.py:46
  29.2 10.5 %collective-permute-start.13 = (bf16[64,640]{1,0:T(8,128)(2,1)S(1)}, bf16[64,640]{1,0:T(8,128)(2,1)S(1)}, u32[]{:S(2)}, u32[]{:S(2)}) collective-permute-start(bf16[64,640]{1,0:T(8,128)(2,1)S(1)} %get-tuple-element.64), channel_id=1, source_target_pairs={{0,2},{1,3},{2,0},{3,1},{4,6},{5,7},{6,4},{7,5},{8,10},{9,11},{10,... | collective-permute-start | bytes 245768 | tf_op jit(solution)/shard_map/ppermute | solution.py:46
  30.4 9.3 %collective-permute-start.16 = (bf16[64,640]{1,0:T(8,128)(2,1)S(1)}, bf16[64,640]{1,0:T(8,128)(2,1)S(1)}, u32[]{:S(2)}, u32[]{:S(2)}) collective-permute-start(bf16[64,640]{1,0:T(8,128)(2,1)S(1)} %collective-permute-done.14), channel_id=1, source_target_pairs={{0,1},{1,0},{2,3},{3,2},{4,5},{5,4},{6,7},{7,6},{8,9},{9,8},{10,11... | collective-permute-start | bytes 245768 | tf_op jit(solution)/shard_map/ppermute | solution.py:46
  39.7 1.9 %collective-permute-start.17 = (bf16[64,640]{1,0:T(8,128)(2,1)S(1)}, bf16[64,640]{1,0:T(8,128)(2,1)S(1)}, u32[]{:S(2)}, u32[]{:S(2)}) collective-permute-start(bf16[64,640]{1,0:T(8,128)(2,1)S(1)} %collective-permute-done.16), channel_id=1, source_target_pairs={{0,1},{1,0},{2,3},{3,2},{4,5},{5,4},{6,7},{7,6},{8,9},{9,8},{10,11... | collective-permute-start | bytes 245768 | tf_op jit(solution)/shard_map/ppermute | solution.py:46

commit v6 on v4

--- a/solution.py
+++ b/solution.py
@@ -468,8 +468,9 @@
     other_core = [(i, i ^ 1) for i in range(heads)]
     other_chip = [(i, i ^ 2) for i in range(heads)]
     columns = out_weight.shape[1]
-    relay = columns // 8 // BLOCK * BLOCK
-    cuts = [0, columns * 2 // 7 // BLOCK * BLOCK, columns * 2 // 7 // BLOCK * BLOCK + relay]
+    relay = columns // 10 // BLOCK * BLOCK
+    early_columns = columns * 3 // 7 // BLOCK * BLOCK - BLOCK
+    cuts = [0, early_columns - relay, early_columns]
 
     if n_ctx == 8:
         by_two = [move(x, BY_TWO) for x in (keys, values)]
@@ -498,7 +499,7 @@
     later_mine = after(later_mine, first_sum)
     (later_sum,) = add_up(later_mine, later_theirs, [columns - cuts[2]])
     later_part = hop(later_sum, "head", other_chip)
-    mine, *sends = project(after(near, later_sum), weight, (0, columns), 3)
+    mine, *sends = project(after(near, later_sum), weight, (0, columns), 2)
     theirs = [hop(send, "head", other_core) for send in sends]
     if n_ctx == 8:
         direct = move(relay_sum, (), [i for i in range(n_ctx) if i not in LATE])

time: 42.1 us -> 41.2 us (0.979)
  the two profiles are of different devices: /device:TPU:24 before, /device:TPU:16 now
where the time goes in v6:
time: 41.2 us; the launch traced here: 41 us
  starting transfers between devices  18 us (44%)
  waiting for transfers between devices  13.9 us (34%)
  Pallas kernels  9.02 us (22%)
    ppermute x14, starting transfers between devices, move(): return lax.ppermute(block, ('ctx', 'head'), pairs)  14.1 us
    ppermute x14, waiting for transfers between devices, move(): return lax.ppermute(block, ('ctx', 'head'), pairs)  8.85 us
    ppermute x6, waiting for transfers between devices, hop(): return lax.ppermute(block, axis, pairs)  5.07 us
    ppermute x6, starting transfers between devices, hop(): return lax.ppermute(block, axis, pairs)  3.9 us
    pallas_call x1, Pallas kernels, attend_next(): pl.pallas_call(functools.partial(next_kernel, numbers), out_shape=state_s...  2.59 us
    pallas_call x2, Pallas kernels, combine(): pl.pallas_call(kernel, out_shape=jax.ShapeDtypeStruct(mine.shape, jnp.bfl...  1.66 us
    pallas_call x1, Pallas kernels, attend_first(): pl.pallas_call(first_kernel, out_shape=state_shapes(queries) + (pltpu.VME...  1.61 us
    pallas_call x2, Pallas kernels, project(): pl.pallas_call(functools.partial(project_kernel, columns), out_shape=proj...  1.54 us
  transfers between devices with their start and end apart: 20, of which 13 were waited for; matrix products, arithmetic and copies ran while one was open for 0% of the time, Pallas kernels for 16%

profile of v6, /device:TPU:16, one launch (start us, length us, event | category | flops | bytes accessed | tf_op | source)
XLA Modules:
  0.0 41.0 jit_solution(5445450194827699556)
XLA Ops:
  0.0 1.9 %collective-permute-start = (bf16[256,256]{1,0:T(8,128)(2,1)}, bf16[256,256]{1,0:T(8,128)(2,1)S(1)}, u32[]{:S(2)}, u32[]{:S(2)}) collective-permute-start(bf16[256,256]{1,0:T(8,128)(2,1)} %keys_in.1), channel_id=1, source_target_pairs={{0,4},{1,5},{2,6},{3,7},{4,0},{5,1},{6,2},{7,3},{8,12},{9,13},{10,... | collective-permute-start | bytes 393224 | tf_op jit(solution)/shard_map/ppermute | solution.py:46
  1.9 1.6 %collective-permute-start.3 = (bf16[256,256]{1,0:T(8,128)(2,1)}, bf16[256,256]{1,0:T(8,128)(2,1)S(1)}, u32[]{:S(2)}, u32[]{:S(2)}) collective-permute-start(bf16[256,256]{1,0:T(8,128)(2,1)} %values_in.1), channel_id=1, source_target_pairs={{0,8},{1,9},{2,10},{3,11},{4,12},{5,13},{6,14},{7,15},{8,16},{9,17... | collective-permute-start | bytes 393224 | tf_op jit(solution)/shard_map/ppermute | solution.py:46
  3.4 0.5 %collective-permute-start.1 = (bf16[256,256]{1,0:T(8,128)(2,1)}, bf16[256,256]{1,0:T(8,128)(2,1)S(1)}, u32[]{:S(2)}, u32[]{:S(2)}) collective-permute-start(bf16[256,256]{1,0:T(8,128)(2,1)} %values_in.1), channel_id=1, source_target_pairs={{0,4},{1,5},{2,6},{3,7},{4,0},{5,1},{6,2},{7,3},{8,12},{9,13},{10,... | collective-permute-start | bytes 393224 | tf_op jit(solution)/shard_map/ppermute | solution.py:46
  3.9 1.6 %attend_first.1 = (f32[1024,128]{1,0:T(8,128)S(1)}, f32[1024,128]{1,0:T(8,128)S(1)}, f32[1024,128]{1,0:T(8,128)S(1)}, bf16[256,512]{1,0:T(8,128)(2,1)S(1)}, f32[16,256]{1,0:T(8,128)S(1)}) custom-call(s32[16]{0:T(128)} %docs_in.1, bf16[256,512]{1,0:T(8,128)(2,1)} %queries_in.1, bf16[256,256]{1,0:T(8,128)(2,1)} %keys_in.1, bf16[256,256]{1,0:T(8,128)(2,1)} %values_in.1), custom_call_target="tpu_custom_call" | custom-call | flops 134217728 | tf_op jit(solution)/shard_map/attend_first/pallas_call | solution.py:202
  5.6 1.0 %collective-permute-done.2.refs_5_ = bf16[256,256]{1,0:T(8,128)(2,1)S(1)} collective-permute-done((bf16[256,256]{1,0:T(8,128)(2,1)}, bf16[256,256]{1,0:T(8,128)(2,1)S(1)}, u32[]{:S(2)}, u32[]{:S(2)}) %collective-permute-start.2) | collective-permute-done | bytes 131104 | tf_op jit(solution)/shard_map/ppermute | solution.py:46
  6.6 2.0 %collective-permute-start.6 = (bf16[256,256]{1,0:T(8,128)(2,1)S(1)}, bf16[256,256]{1,0:T(8,128)(2,1)S(1)}, u32[]{:S(2)}, u32[]{:S(2)}) collective-permute-start(bf16[256,256]{1,0:T(8,128)(2,1)S(1)} %collective-permute-done.2.refs_5_), channel_id=1, source_target_pairs={{0,1},{1,0},{2,3},{3,2},{4,5},{5,4},{6,7},{7,6},{8,12},{9,13},{10,... | collective-permute-start | bytes 393224 | tf_op jit(solution)/shard_map/ppermute | solution.py:46
  8.6 0.8 %collective-permute-done.3.refs_6_ = bf16[256,256]{1,0:T(8,128)(2,1)S(1)} collective-permute-done((bf16[256,256]{1,0:T(8,128)(2,1)}, bf16[256,256]{1,0:T(8,128)(2,1)S(1)}, u32[]{:S(2)}, u32[]{:S(2)}) %collective-permute-start.3) | collective-permute-done | bytes 131104 | tf_op jit(solution)/shard_map/ppermute | solution.py:46
  9.4 0.7 %collective-permute-start.5 = (bf16[256,256]{1,0:T(8,128)(2,1)S(1)}, bf16[256,256]{1,0:T(8,128)(2,1)S(1)}, u32[]{:S(2)}, u32[]{:S(2)}) collective-permute-start(bf16[256,256]{1,0:T(8,128)(2,1)S(1)} %collective-permute-done.3.refs_6_), channel_id=1, source_target_pairs={{0,1},{1,0},{2,3},{3,2},{4,5},{5,4},{6,7},{7,6},{8,16},{9,17},{10,... | collective-permute-start | bytes 393224 | tf_op jit(solution)/shard_map/ppermute | solution.py:46
  10.2 0.8 %collective-permute-start.7 = (bf16[256,256]{1,0:T(8,128)(2,1)S(1)}, bf16[256,256]{1,0:T(8,128)(2,1)S(1)}, u32[]{:S(2)}, u32[]{:S(2)}) collective-permute-start(bf16[256,256]{1,0:T(8,128)(2,1)S(1)} %collective-permute-done.3.refs_6_), channel_id=1, source_target_pairs={{0,1},{1,0},{2,3},{3,2},{4,5},{5,4},{6,7},{7,6},{8,12},{9,13},{10,... | collective-permute-start | bytes 393224 | tf_op jit(solution)/shard_map/ppermute | solution.py:46
  10.9 1.7 %collective-permute-done.4.refs_7_ = bf16[256,256]{1,0:T(8,128)(2,1)S(1)} collective-permute-done((bf16[256,256]{1,0:T(8,128)(2,1)S(1)}, bf16[256,256]{1,0:T(8,128)(2,1)S(1)}, u32[]{:S(2)}, u32[]{:S(2)}) %collective-permute-start.4) | collective-permute-done | bytes 131104 | tf_op jit(solution)/shard_map/ppermute | solution.py:46
  12.8 1.6 %collective-permute-start.8 = (bf16[256,256]{1,0:T(8,128)(2,1)S(1)}, bf16[256,256]{1,0:T(8,128)(2,1)S(1)}, u32[]{:S(2)}, u32[]{:S(2)}) collective-permute-start(bf16[256,256]{1,0:T(8,128)(2,1)S(1)} %collective-permute-done.6.refs_3_), channel_id=1, source_target_pairs={{0,1},{1,0},{2,3},{3,2},{4,5},{5,4},{6,7},{7,6},{8,16},{9,17},{10,... | collective-permute-start | bytes 393224 | tf_op jit(solution)/shard_map/ppermute | solution.py:46
  14.4 1.1 %collective-permute-done.5.refs_8_ = bf16[256,256]{1,0:T(8,128)(2,1)S(1)} collective-permute-done((bf16[256,256]{1,0:T(8,128)(2,1)S(1)}, bf16[256,256]{1,0:T(8,128)(2,1)S(1)}, u32[]{:S(2)}, u32[]{:S(2)}) %collective-permute-start.5) | collective-permute-done | bytes 131104 | tf_op jit(solution)/shard_map/ppermute | solution.py:46
  15.5 1.5 %collective-permute-start.9 = (bf16[256,256]{1,0:T(8,128)(2,1)S(1)}, bf16[256,256]{1,0:T(8,128)(2,1)S(1)}, u32[]{:S(2)}, u32[]{:S(2)}) collective-permute-start(bf16[256,256]{1,0:T(8,128)(2,1)S(1)} %collective-permute-done.5.refs_8_), channel_id=1, source_target_pairs={{0,1},{1,0},{2,3},{3,2},{4,5},{5,4},{6,7},{7,6},{8,9},{9,8},{10,11... | collective-permute-start | bytes 393224 | tf_op jit(solution)/shard_map/ppermute | solution.py:46
  17.0 2.6 %attend_next.1 = (f32[1024,128]{1,0:T(8,128)S(1)}, f32[1024,128]{1,0:T(8,128)S(1)}, f32[1024,128]{1,0:T(8,128)S(1)}, bf16[512,5376]{1,0:T(8,128)(2,1)S(1)}) custom-call(bf16[256,512]{1,0:T(8,128)(2,1)S(1)} %get-tuple-element.36.queries, f32[16,256]{1,0:T(8,128)S(1)} %get-tuple-element.37.open_beside, bf16[512,5376]{1,0:T(8,128)(2,1)} %weight_in.1, ...), custom_call_target="tpu_custom_call" | custom-call | flops 402653184 | bytes 5505024 | tf_op jit(solution)/shard_map/attend_next/pallas_call | solution.py:224
  19.6 0.9 %collective-permute-done.9.refs_6_ = bf16[256,256]{1,0:T(8,128)(2,1)S(1)} collective-permute-done((bf16[256,256]{1,0:T(8,128)(2,1)S(1)}, bf16[256,256]{1,0:T(8,128)(2,1)S(1)}, u32[]{:S(2)}, u32[]{:S(2)}) %collective-permute-start.9) | collective-permute-done | bytes 131104 | tf_op jit(solution)/shard_map/ppermute | solution.py:46
  20.4 1.5 %attend_last.1 = (bf16[128,512]{1,0:T(8,128)(2,1)S(1)}, bf16[128,512]{1,0:T(8,128)(2,1)S(1)}, f32[64,2176]{1,0:T(8,128)S(1)}, bf16[64,2176]{1,0:T(8,128)(2,1)S(1)}) custom-call(bf16[256,512]{1,0:T(8,128)(2,1)S(1)} %get-tuple-element.36.queries, bf16[512,5376]{1,0:T(8,128)(2,1)S(1)} %get-tuple-element.43.weight, f32[1024,128]{1,0:T(8,128)S(1)} %get-tuple-element.44.refs_0_, ...), custom_call_target="tpu_custom_call" | custom-call | flops 268435456 | tf_op jit(solution)/shard_map/attend_last/pallas_call | solution.py:267
  22.0 0.6 %project.2 = (f32[64,3200]{1,0:T(8,128)S(1)}, bf16[64,3200]{1,0:T(8,128)(2,1)S(1)}) custom-call(bf16[128,512]{1,0:T(8,128)(2,1)S(1)} %get-tuple-element.52.rows, bf16[512,5376]{1,0:T(8,128)(2,1)S(1)} %get-tuple-element.43.weight), custom_call_target="tpu_custom_call" | custom-call | flops 419430400 | tf_op jit(solution)/shard_map/project/pallas_call | solution.py:302
  22.6 0.9 %collective-permute-done.10.theirs = bf16[64,2176]{1,0:T(8,128)(2,1)S(1)} collective-permute-done((bf16[64,2176]{1,0:T(8,128)(2,1)S(1)}, bf16[64,2176]{1,0:T(8,128)(2,1)S(1)}, u32[]{:S(2)}, u32[]{:S(2)}) %collective-permute-start.10) | collective-permute-done | bytes 278560 | tf_op jit(solution)/shard_map/ppermute | solution.py:22
  23.6 0.2 collective-permute-start.11
  23.8 1.5 %collective-permute-start.15 = (bf16[64,1664]{1,0:T(8,128)(2,1)S(1)}, bf16[64,1664]{1,0:T(8,128)(2,1)S(1)}, u32[]{:S(2)}, u32[]{:S(2)}) collective-permute-start(bf16[64,1664]{1,0:T(8,128)(2,1)S(1)} %get-tuple-element.56), channel_id=1, source_target_pairs={{0,2},{1,3},{2,0},{3,1},{4,6},{5,7},{6,4},{7,5},{8,10},{9,11},{10,... | collective-permute-start | bytes 638984 | tf_op jit(solution)/shard_map/ppermute | solution.py:22
  25.5 1.6 %collective-permute-start.12 = (bf16[64,3200]{1,0:T(8,128)(2,1)S(1)}, bf16[64,3200]{1,0:T(8,128)(2,1)S(1)}, u32[]{:S(2)}, u32[]{:S(2)}) collective-permute-start(bf16[64,3200]{1,0:T(8,128)(2,1)S(1)} %add_up.3), channel_id=1, source_target_pairs={{0,2},{1,3},{2,0},{3,1},{4,6},{5,7},{6,4},{7,5},{8,10},{9,11},{10,... | collective-permute-start | bytes 1228808 | tf_op jit(solution)/shard_map/ppermute | solution.py:22
  27.1 0.9 %project.3 = (f32[64,5376]{1,0:T(8,128)S(1)}, bf16[64,2688]{1,0:T(8,128)(2,1)S(1)}, bf16[64,2688]{1,0:T(8,128)(2,1)S(1)}) custom-call(bf16[128,512]{1,0:T(8,128)(2,1)S(1)} %get-tuple-element.61.rows, bf16[512,5376]{1,0:T(8,128)(2,1)S(1)} %get-tuple-element.43.weight), custom_call_target="tpu_custom_call" | custom-call | flops 704643072 | tf_op jit(solution)/shard_map/project/pallas_call | solution.py:302
  28.1 0.5 %collective-permute-start.19 = (bf16[64,2688]{1,0:T(8,128)(2,1)S(1)}, bf16[64,2688]{1,0:T(8,128)(2,1)S(1)}, u32[]{:S(2)}, u32[]{:S(2)}) collective-permute-start(bf16[64,2688]{1,0:T(8,128)(2,1)S(1)} %get-tuple-element.66), channel_id=1, source_target_pairs={{0,1},{1,0},{2,3},{3,2},{4,5},{5,4},{6,7},{7,6},{8,9},{9,8},{10,11... | collective-permute-start | bytes 1032200 | tf_op jit(solution)/shard_map/ppermute | solution.py:22
  28.6 3.3 %collective-permute-done.15.refs_1_ = bf16[64,1664]{1,0:T(8,128)(2,1)S(1)} collective-permute-done((bf16[64,1664]{1,0:T(8,128)(2,1)S(1)}, bf16[64,1664]{1,0:T(8,128)(2,1)S(1)}, u32[]{:S(2)}, u32[]{:S(2)}) %collective-permute-start.15) | collective-permute-done | bytes 213024 | tf_op jit(solution)/shard_map/ppermute | solution.py:22
  31.9 0.9 %collective-permute-done.14 = bf16[64,512]{1,0:T(8,128)(2,1)S(1)} collective-permute-done((bf16[64,512]{1,0:T(8,128)(2,1)S(1)}, bf16[64,512]{1,0:T(8,128)(2,1)S(1)}, u32[]{:S(2)}, u32[]{:S(2)}) %collective-permute-start.14) | collective-permute-done | bytes 65568 | tf_op jit(solution)/shard_map/ppermute | solution.py:46
  32.8 0.5 %collective-permute-start.13 = (bf16[64,512]{1,0:T(8,128)(2,1)S(1)}, bf16[64,512]{1,0:T(8,128)(2,1)S(1)}, u32[]{:S(2)}, u32[]{:S(2)}) collective-permute-start(bf16[64,512]{1,0:T(8,128)(2,1)S(1)} %get-tuple-element.63), channel_id=1, source_target_pairs={{0,2},{1,3},{2,0},{3,1},{4,6},{5,7},{6,4},{7,5},{8,10},{9,11},{10,... | collective-permute-start | bytes 196616 | tf_op jit(solution)/shard_map/ppermute | solution.py:46
  33.3 0.7 %collective-permute-done.16 = bf16[64,512]{1,0:T(8,128)(2,1)S(1)} collective-permute-done((bf16[64,512]{1,0:T(8,128)(2,1)S(1)}, bf16[64,512]{1,0:T(8,128)(2,1)S(1)}, u32[]{:S(2)}, u32[]{:S(2)}) %collective-permute-start.16) | collective-permute-done | bytes 65568 | tf_op jit(solution)/shard_map/ppermute | solution.py:46
  34.1 3.1 %collective-permute-start.17 = (bf16[64,512]{1,0:T(8,128)(2,1)S(1)}, bf16[64,512]{1,0:T(8,128)(2,1)S(1)}, u32[]{:S(2)}, u32[]{:S(2)}) collective-permute-start(bf16[64,512]{1,0:T(8,128)(2,1)S(1)} %collective-permute-done.16), channel_id=1, source_target_pairs={{0,1},{1,0},{2,3},{3,2},{4,5},{5,4},{6,7},{7,6},{8,9},{9,8},{10,11... | collective-permute-start | bytes 196616 | tf_op jit(solution)/shard_map/ppermute | solution.py:46
  37.2 0.8 %combine.2.refs_6_ = bf16[64,5376]{1,0:T(8,128)(2,1)} custom-call(f32[64,5376]{1,0:T(8,128)S(1)} %get-tuple-element.62.refs_0_, bf16[64,1664]{1,0:T(8,128)(2,1)S(1)} %collective-permute-done.15.refs_1_, bf16[64,2688]{1,0:T(8,128)(2,1)S(1)} %collective-permute-done.18.refs_2_.refs_4_, bf16[64,2688]{1,0:T(8,128)(2,1)S(1)} %collective-permute-done.19.refs_3_.refs_5_), custom_call_target="tpu_custom_call" | custom-call | tf_op jit(solution)/shard_map/combine/pallas_call | solution.py:371
  38.0 1.5 %collective-permute-done.17.refs_3_ = bf16[64,512]{1,0:T(8,128)(2,1)S(1)} collective-permute-done((bf16[64,512]{1,0:T(8,128)(2,1)S(1)}, bf16[64,512]{1,0:T(8,128)(2,1)S(1)}, u32[]{:S(2)}, u32[]{:S(2)}) %collective-permute-start.17) | collective-permute-done | bytes 65568 | tf_op jit(solution)/shard_map/ppermute | solution.py:46
  39.4 0.7 %collective-permute-done.12.refs_1_ = bf16[64,3200]{1,0:T(8,128)(2,1)S(1)} collective-permute-done((bf16[64,3200]{1,0:T(8,128)(2,1)S(1)}, bf16[64,3200]{1,0:T(8,128)(2,1)S(1)}, u32[]{:S(2)}, u32[]{:S(2)}) %collective-permute-start.12) | collective-permute-done | bytes 409632 | tf_op jit(solution)/shard_map/ppermute | solution.py:22
  40.1 0.9 %combine.3 = bf16[64,5376]{1,0:T(8,128)(2,1)} custom-call(f32[64,5376]{1,0:T(8,128)S(1)} %get-tuple-element.62.refs_0_, bf16[64,3200]{1,0:T(8,128)(2,1)S(1)} %collective-permute-done.12.refs_1_, bf16[64,512]{1,0:T(8,128)(2,1)S(1)} %collective-permute-done.13.refs_2_, ...), custom_call_target="tpu_custom_call", output_to_operand_aliasing={{}: (6, {})} | custom-call | tf_op jit(solution)/shard_map/combine/pallas_call | solution.py:371
  (17 shorter events, 0.6 us)
Async XLA Ops:
  0.0 6.6 %collective-permute-start.2 = (bf16[256,256]{1,0:T(8,128)(2,1)}, bf16[256,256]{1,0:T(8,128)(2,1)S(1)}, u32[]{:S(2)}, u32[]{:S(2)}) collective-permute-start(bf16[256,256]{1,0:T(8,128)(2,1)} %keys_in.1), channel_id=1, source_target_pairs={{0,8},{1,9},{2,10},{3,11},{4,12},{5,13},{6,14},{7,15},{8,16},{9,17... | collective-permute-start | bytes 393224 | tf_op jit(solution)/shard_map/ppermute | solution.py:46
  0.0 6.6 %collective-permute-start = (bf16[256,256]{1,0:T(8,128)(2,1)}, bf16[256,256]{1,0:T(8,128)(2,1)S(1)}, u32[]{:S(2)}, u32[]{:S(2)}) collective-permute-start(bf16[256,256]{1,0:T(8,128)(2,1)} %keys_in.1), channel_id=1, source_target_pairs={{0,4},{1,5},{2,6},{3,7},{4,0},{5,1},{6,2},{7,3},{8,12},{9,13},{10,... | collective-permute-start | bytes 393224 | tf_op jit(solution)/shard_map/ppermute | solution.py:46
  1.9 7.5 %collective-permute-start.3 = (bf16[256,256]{1,0:T(8,128)(2,1)}, bf16[256,256]{1,0:T(8,128)(2,1)S(1)}, u32[]{:S(2)}, u32[]{:S(2)}) collective-permute-start(bf16[256,256]{1,0:T(8,128)(2,1)} %values_in.1), channel_id=1, source_target_pairs={{0,8},{1,9},{2,10},{3,11},{4,12},{5,13},{6,14},{7,15},{8,16},{9,17... | collective-permute-start | bytes 393224 | tf_op jit(solution)/shard_map/ppermute | solution.py:46
  3.4 6.7 %collective-permute-start.1 = (bf16[256,256]{1,0:T(8,128)(2,1)}, bf16[256,256]{1,0:T(8,128)(2,1)S(1)}, u32[]{:S(2)}, u32[]{:S(2)}) collective-permute-start(bf16[256,256]{1,0:T(8,128)(2,1)} %values_in.1), channel_id=1, source_target_pairs={{0,4},{1,5},{2,6},{3,7},{4,0},{5,1},{6,2},{7,3},{8,12},{9,13},{10,... | collective-permute-start | bytes 393224 | tf_op jit(solution)/shard_map/ppermute | solution.py:46
  6.6 6.0 %collective-permute-start.4 = (bf16[256,256]{1,0:T(8,128)(2,1)S(1)}, bf16[256,256]{1,0:T(8,128)(2,1)S(1)}, u32[]{:S(2)}, u32[]{:S(2)}) collective-permute-start(bf16[256,256]{1,0:T(8,128)(2,1)S(1)} %collective-permute-done.2.refs_5_), channel_id=1, source_target_pairs={{0,1},{1,0},{2,3},{3,2},{4,5},{5,4},{6,7},{7,6},{8,16},{9,17},{10,... | collective-permute-start | bytes 393224 | tf_op jit(solution)/shard_map/ppermute | solution.py:46
  6.6 6.2 %collective-permute-start.6 = (bf16[256,256]{1,0:T(8,128)(2,1)S(1)}, bf16[256,256]{1,0:T(8,128)(2,1)S(1)}, u32[]{:S(2)}, u32[]{:S(2)}) collective-permute-start(bf16[256,256]{1,0:T(8,128)(2,1)S(1)} %collective-permute-done.2.refs_5_), channel_id=1, source_target_pairs={{0,1},{1,0},{2,3},{3,2},{4,5},{5,4},{6,7},{7,6},{8,12},{9,13},{10,... | collective-permute-start | bytes 393224 | tf_op jit(solution)/shard_map/ppermute | solution.py:46
  9.4 6.1 %collective-permute-start.5 = (bf16[256,256]{1,0:T(8,128)(2,1)S(1)}, bf16[256,256]{1,0:T(8,128)(2,1)S(1)}, u32[]{:S(2)}, u32[]{:S(2)}) collective-permute-start(bf16[256,256]{1,0:T(8,128)(2,1)S(1)} %collective-permute-done.3.refs_6_), channel_id=1, source_target_pairs={{0,1},{1,0},{2,3},{3,2},{4,5},{5,4},{6,7},{7,6},{8,16},{9,17},{10,... | collective-permute-start | bytes 393224 | tf_op jit(solution)/shard_map/ppermute | solution.py:46
  10.2 9.4 %collective-permute-start.7 = (bf16[256,256]{1,0:T(8,128)(2,1)S(1)}, bf16[256,256]{1,0:T(8,128)(2,1)S(1)}, u32[]{:S(2)}, u32[]{:S(2)}) collective-permute-start(bf16[256,256]{1,0:T(8,128)(2,1)S(1)} %collective-permute-done.3.refs_6_), channel_id=1, source_target_pairs={{0,1},{1,0},{2,3},{3,2},{4,5},{5,4},{6,7},{7,6},{8,12},{9,13},{10,... | collective-permute-start | bytes 393224 | tf_op jit(solution)/shard_map/ppermute | solution.py:46
  12.8 6.8 %collective-permute-start.8 = (bf16[256,256]{1,0:T(8,128)(2,1)S(1)}, bf16[256,256]{1,0:T(8,128)(2,1)S(1)}, u32[]{:S(2)}, u32[]{:S(2)}) collective-permute-start(bf16[256,256]{1,0:T(8,128)(2,1)S(1)} %collective-permute-done.6.refs_3_), channel_id=1, source_target_pairs={{0,1},{1,0},{2,3},{3,2},{4,5},{5,4},{6,7},{7,6},{8,16},{9,17},{10,... | collective-permute-start | bytes 393224 | tf_op jit(solution)/shard_map/ppermute | solution.py:46
  15.5 5.0 %collective-permute-start.9 = (bf16[256,256]{1,0:T(8,128)(2,1)S(1)}, bf16[256,256]{1,0:T(8,128)(2,1)S(1)}, u32[]{:S(2)}, u32[]{:S(2)}) collective-permute-start(bf16[256,256]{1,0:T(8,128)(2,1)S(1)} %collective-permute-done.5.refs_8_), channel_id=1, source_target_pairs={{0,1},{1,0},{2,3},{3,2},{4,5},{5,4},{6,7},{7,6},{8,9},{9,8},{10,11... | collective-permute-start | bytes 393224 | tf_op jit(solution)/shard_map/ppermute | solution.py:46
  21.9 1.6 %collective-permute-start.10 = (bf16[64,2176]{1,0:T(8,128)(2,1)S(1)}, bf16[64,2176]{1,0:T(8,128)(2,1)S(1)}, u32[]{:S(2)}, u32[]{:S(2)}) collective-permute-start(bf16[64,2176]{1,0:T(8,128)(2,1)S(1)} %get-tuple-element.55), channel_id=1, source_target_pairs={{0,1},{1,0},{2,3},{3,2},{4,5},{5,4},{6,7},{7,6},{8,9},{9,8},{10,11... | collective-permute-start | bytes 835592 | tf_op jit(solution)/shard_map/ppermute | solution.py:22
  23.6 1.8 %collective-permute-start.11 = (bf16[64,3200]{1,0:T(8,128)(2,1)S(1)}, bf16[64,3200]{1,0:T(8,128)(2,1)S(1)}, u32[]{:S(2)}, u32[]{:S(2)}) collective-permute-start(bf16[64,3200]{1,0:T(8,128)(2,1)S(1)} %get-tuple-element.60), channel_id=1, source_target_pairs={{0,1},{1,0},{2,3},{3,2},{4,5},{5,4},{6,7},{7,6},{8,9},{9,8},{10,11... | collective-permute-start | bytes 1228808 | tf_op jit(solution)/shard_map/ppermute | solution.py:22
  23.8 8.1 %collective-permute-start.15 = (bf16[64,1664]{1,0:T(8,128)(2,1)S(1)}, bf16[64,1664]{1,0:T(8,128)(2,1)S(1)}, u32[]{:S(2)}, u32[]{:S(2)}) collective-permute-start(bf16[64,1664]{1,0:T(8,128)(2,1)S(1)} %get-tuple-element.56), channel_id=1, source_target_pairs={{0,2},{1,3},{2,0},{3,1},{4,6},{5,7},{6,4},{7,5},{8,10},{9,11},{10,... | collective-permute-start | bytes 638984 | tf_op jit(solution)/shard_map/ppermute | solution.py:22
  25.5 14.6 %collective-permute-start.12 = (bf16[64,3200]{1,0:T(8,128)(2,1)S(1)}, bf16[64,3200]{1,0:T(8,128)(2,1)S(1)}, u32[]{:S(2)}, u32[]{:S(2)}) collective-permute-start(bf16[64,3200]{1,0:T(8,128)(2,1)S(1)} %add_up.3), channel_id=1, source_target_pairs={{0,2},{1,3},{2,0},{3,1},{4,6},{5,7},{6,4},{7,5},{8,10},{9,11},{10,... | collective-permute-start | bytes 1228808 | tf_op jit(solution)/shard_map/ppermute | solution.py:22
  28.0 9.2 %collective-permute-start.18 = (bf16[64,2688]{1,0:T(8,128)(2,1)S(1)}, bf16[64,2688]{1,0:T(8,128)(2,1)S(1)}, u32[]{:S(2)}, u32[]{:S(2)}) collective-permute-start(bf16[64,2688]{1,0:T(8,128)(2,1)S(1)} %get-tuple-element.65), channel_id=1, source_target_pairs={{0,1},{1,0},{2,3},{3,2},{4,5},{5,4},{6,7},{7,6},{8,9},{9,8},{10,11... | collective-permute-start | bytes 1032200 | tf_op jit(solution)/shard_map/ppermute | solution.py:22
  28.1 9.1 %collective-permute-start.19 = (bf16[64,2688]{1,0:T(8,128)(2,1)S(1)}, bf16[64,2688]{1,0:T(8,128)(2,1)S(1)}, u32[]{:S(2)}, u32[]{:S(2)}) collective-permute-start(bf16[64,2688]{1,0:T(8,128)(2,1)S(1)} %get-tuple-element.66), channel_id=1, source_target_pairs={{0,1},{1,0},{2,3},{3,2},{4,5},{5,4},{6,7},{7,6},{8,9},{9,8},{10,11... | collective-permute-start | bytes 1032200 | tf_op jit(solution)/shard_map/ppermute | solution.py:22
  28.6 4.3 %collective-permute-start.14 = (bf16[64,512]{1,0:T(8,128)(2,1)S(1)}, bf16[64,512]{1,0:T(8,128)(2,1)S(1)}, u32[]{:S(2)}, u32[]{:S(2)}) collective-permute-start(bf16[64,512]{1,0:T(8,128)(2,1)S(1)} %get-tuple-element.63), channel_id=1, source_target_pairs={{0,1},{1,0},{2,3},{3,2},{4,5},{5,4},{6,7},{7,6},{8,9},{9,8},{10,11... | collective-permute-start | bytes 196616 | tf_op jit(solution)/shard_map/ppermute | solution.py:46
  32.8 1.3 %collective-permute-start.16 = (bf16[64,512]{1,0:T(8,128)(2,1)S(1)}, bf16[64,512]{1,0:T(8,128)(2,1)S(1)}, u32[]{:S(2)}, u32[]{:S(2)}) collective-permute-start(bf16[64,512]{1,0:T(8,128)(2,1)S(1)} %collective-permute-done.14), channel_id=1, source_target_pairs={{0,1},{1,0},{2,3},{3,2},{4,5},{5,4},{6,7},{7,6},{8,9},{9,8},{10,11... | collective-permute-start | bytes 196616 | tf_op jit(solution)/shard_map/ppermute | solution.py:46
  32.8 5.1 %collective-permute-start.13 = (bf16[64,512]{1,0:T(8,128)(2,1)S(1)}, bf16[64,512]{1,0:T(8,128)(2,1)S(1)}, u32[]{:S(2)}, u32[]{:S(2)}) collective-permute-start(bf16[64,512]{1,0:T(8,128)(2,1)S(1)} %get-tuple-element.63), channel_id=1, source_target_pairs={{0,2},{1,3},{2,0},{3,1},{4,6},{5,7},{6,4},{7,5},{8,10},{9,11},{10,... | collective-permute-start | bytes 196616 | tf_op jit(solution)/shard_map/ppermute | solution.py:46
  34.1 5.3 %collective-permute-start.17 = (bf16[64,512]{1,0:T(8,128)(2,1)S(1)}, bf16[64,512]{1,0:T(8,128)(2,1)S(1)}, u32[]{:S(2)}, u32[]{:S(2)}) collective-permute-start(bf16[64,512]{1,0:T(8,128)(2,1)S(1)} %collective-permute-done.16), channel_id=1, source_target_pairs={{0,1},{1,0},{2,3},{3,2},{4,5},{5,4},{6,7},{7,6},{8,9},{9,8},{10,11... | collective-permute-start | bytes 196616 | tf_op jit(solution)/shard_map/ppermute | solution.py:46

commit v7 on v6

--- a/solution.py
+++ b/solution.py
@@ -15,6 +15,7 @@
 VMEM = pl.BlockSpec(memory_space=pltpu.VMEM)
 SMEM = pl.BlockSpec(memory_space=pltpu.SMEM)
 HBM = pl.BlockSpec(memory_space=pltpu.HBM)
+SPAN = 1024
 LIMIT = pltpu.CompilerParams(vmem_limit_bytes=32 * 1024 * 1024)
 
 
@@ -338,22 +339,25 @@
     copies = []
     for i, (at, total) in enumerate(zip(cuts, totals)):
         options = across[sum(counts[:i]) : sum(counts[: i + 1])]
-        width = options[0].shape[1]
-        left = 0
-        for part in beside:
-            low, high = max(left, at), min(left + part.shape[1], at + width)
-            if low < high:
-                piece = mine[:, low:high] + part[:, low - left : high - left].astype(jnp.float32)
-                there = options[0][:, low - at : high - at].astype(jnp.float32)
-                if len(options) == 2:
-                    position = lax.axis_index("ctx")
-                    late = functools.reduce(jnp.logical_or, [position == i for i in LATE])
-                    relayed = options[1][:, low - at : high - at].astype(jnp.float32)
-                    there = jnp.where(late, relayed, there)
-                total[:, low - at : high - at] = (piece + there).astype(total.dtype)
-            left += part.shape[1]
-        copies.append(pltpu.make_async_copy(total, out.at[:, at : at + width], sems.at[i]))
-        copies[-1].start()
+        end = at + options[0].shape[1]
+        stops = {at, end} | set(range(0, mine.shape[1], SPAN))
+        for part in range(len(beside)):
+            stops.add(part * beside[0].shape[1])
+        stops = sorted(x for x in stops if at <= x <= end)
+        for low, high in zip(stops[:-1], stops[1:]):
+            part, left = beside[low // beside[0].shape[1]], low // beside[0].shape[1] * beside[0].shape[1]
+            columns = slice(low - at, high - at)
+            piece = mine[:, low:high] + part[:, low - left : high - left].astype(jnp.float32)
+            there = options[0][:, columns].astype(jnp.float32)
+            if len(options) == 2:
+                position = lax.axis_index("ctx")
+                late = functools.reduce(jnp.logical_or, [position == i for i in LATE])
+                there = jnp.where(late, options[1][:, columns].astype(jnp.float32), there)
+            total[:, columns] = (piece + there).astype(total.dtype)
+            copies.append(
+                pltpu.make_async_copy(total.at[:, columns], out.at[:, low:high], sems.at[len(copies)])
+            )
+            copies[-1].start()
     for copy in copies:
         copy.wait()
 
@@ -374,7 +378,7 @@
         in_specs=[VMEM] * inputs + [HBM] * len(outs),
         out_specs=HBM,
         scratch_shapes=[pltpu.VMEM(options[0].shape, jnp.bfloat16) for options in across]
-        + [pltpu.SemaphoreType.DMA((len(cuts),))],
+        + [pltpu.SemaphoreType.DMA((len(cuts) * (2 + len(beside) + mine.shape[1] // SPAN),))],
         input_output_aliases={inputs: 0} if outs else {},
         compiler_params=LIMIT,
         name="combine",

time: 41.2 us -> 41.3 us (level)
  no operation moved by 1% of the time
where the time goes in v7:
time: 41.3 us; the launch traced here: 41.1 us
  starting transfers between devices  18 us (44%)
  waiting for transfers between devices  13.9 us (34%)
  Pallas kernels  9.11 us (22%)
    ppermute x14, starting transfers between devices, move(): return lax.ppermute(block, ('ctx', 'head'), pairs)  14.1 us
    ppermute x14, waiting for transfers between devices, move(): return lax.ppermute(block, ('ctx', 'head'), pairs)  8.81 us
    ppermute x6, waiting for transfers between devices, hop(): return lax.ppermute(block, axis, pairs)  5.07 us
    ppermute x6, starting transfers between devices, hop(): return lax.ppermute(block, axis, pairs)  3.9 us
    pallas_call x1, Pallas kernels, attend_next(): pl.pallas_call(functools.partial(next_kernel, numbers), out_shape=state_s...  2.59 us
    pallas_call x2, Pallas kernels, combine(): pl.pallas_call(kernel, out_shape=jax.ShapeDtypeStruct(mine.shape, jnp.bfl...  1.75 us
    pallas_call x1, Pallas kernels, attend_first(): pl.pallas_call(first_kernel, out_shape=state_shapes(queries) + (pltpu.VME...  1.61 us
    pallas_call x2, Pallas kernels, project(): pl.pallas_call(functools.partial(project_kernel, columns), out_shape=proj...  1.54 us
  transfers between devices with their start and end apart: 20, of which 13 were waited for; matrix products, arithmetic and copies ran while one was open for 0% of the time, Pallas kernels for 16%

profile of v7, /device:TPU:16, one launch (start us, length us, event | category | flops | bytes accessed | tf_op | source)
XLA Modules:
  0.0 41.1 jit_solution(13670010281881211660)
XLA Ops:
  0.0 1.9 %collective-permute-start = (bf16[256,256]{1,0:T(8,128)(2,1)}, bf16[256,256]{1,0:T(8,128)(2,1)S(1)}, u32[]{:S(2)}, u32[]{:S(2)}) collective-permute-start(bf16[256,256]{1,0:T(8,128)(2,1)} %keys_in.1), channel_id=1, source_target_pairs={{0,4},{1,5},{2,6},{3,7},{4,0},{5,1},{6,2},{7,3},{8,12},{9,13},{10,... | collective-permute-start | bytes 393224 | tf_op jit(solution)/shard_map/ppermute | solution.py:47
  1.9 1.6 %collective-permute-start.3 = (bf16[256,256]{1,0:T(8,128)(2,1)}, bf16[256,256]{1,0:T(8,128)(2,1)S(1)}, u32[]{:S(2)}, u32[]{:S(2)}) collective-permute-start(bf16[256,256]{1,0:T(8,128)(2,1)} %values_in.1), channel_id=1, source_target_pairs={{0,8},{1,9},{2,10},{3,11},{4,12},{5,13},{6,14},{7,15},{8,16},{9,17... | collective-permute-start | bytes 393224 | tf_op jit(solution)/shard_map/ppermute | solution.py:47
  3.4 0.5 %collective-permute-start.1 = (bf16[256,256]{1,0:T(8,128)(2,1)}, bf16[256,256]{1,0:T(8,128)(2,1)S(1)}, u32[]{:S(2)}, u32[]{:S(2)}) collective-permute-start(bf16[256,256]{1,0:T(8,128)(2,1)} %values_in.1), channel_id=1, source_target_pairs={{0,4},{1,5},{2,6},{3,7},{4,0},{5,1},{6,2},{7,3},{8,12},{9,13},{10,... | collective-permute-start | bytes 393224 | tf_op jit(solution)/shard_map/ppermute | solution.py:47
  3.9 1.6 %attend_first.1 = (f32[1024,128]{1,0:T(8,128)S(1)}, f32[1024,128]{1,0:T(8,128)S(1)}, f32[1024,128]{1,0:T(8,128)S(1)}, bf16[256,512]{1,0:T(8,128)(2,1)S(1)}, f32[16,256]{1,0:T(8,128)S(1)}) custom-call(s32[16]{0:T(128)} %docs_in.1, bf16[256,512]{1,0:T(8,128)(2,1)} %queries_in.1, bf16[256,256]{1,0:T(8,128)(2,1)} %keys_in.1, bf16[256,256]{1,0:T(8,128)(2,1)} %values_in.1), custom_call_target="tpu_custom_call" | custom-call | flops 134217728 | tf_op jit(solution)/shard_map/attend_first/pallas_call | solution.py:203
  5.6 1.0 %collective-permute-done.2.refs_5_ = bf16[256,256]{1,0:T(8,128)(2,1)S(1)} collective-permute-done((bf16[256,256]{1,0:T(8,128)(2,1)}, bf16[256,256]{1,0:T(8,128)(2,1)S(1)}, u32[]{:S(2)}, u32[]{:S(2)}) %collective-permute-start.2) | collective-permute-done | bytes 131104 | tf_op jit(solution)/shard_map/ppermute | solution.py:47
  6.6 2.0 %collective-permute-start.6 = (bf16[256,256]{1,0:T(8,128)(2,1)S(1)}, bf16[256,256]{1,0:T(8,128)(2,1)S(1)}, u32[]{:S(2)}, u32[]{:S(2)}) collective-permute-start(bf16[256,256]{1,0:T(8,128)(2,1)S(1)} %collective-permute-done.2.refs_5_), channel_id=1, source_target_pairs={{0,1},{1,0},{2,3},{3,2},{4,5},{5,4},{6,7},{7,6},{8,12},{9,13},{10,... | collective-permute-start | bytes 393224 | tf_op jit(solution)/shard_map/ppermute | solution.py:47
  8.6 0.8 %collective-permute-done.3.refs_6_ = bf16[256,256]{1,0:T(8,128)(2,1)S(1)} collective-permute-done((bf16[256,256]{1,0:T(8,128)(2,1)}, bf16[256,256]{1,0:T(8,128)(2,1)S(1)}, u32[]{:S(2)}, u32[]{:S(2)}) %collective-permute-start.3) | collective-permute-done | bytes 131104 | tf_op jit(solution)/shard_map/ppermute | solution.py:47
  9.4 0.7 %collective-permute-start.5 = (bf16[256,256]{1,0:T(8,128)(2,1)S(1)}, bf16[256,256]{1,0:T(8,128)(2,1)S(1)}, u32[]{:S(2)}, u32[]{:S(2)}) collective-permute-start(bf16[256,256]{1,0:T(8,128)(2,1)S(1)} %collective-permute-done.3.refs_6_), channel_id=1, source_target_pairs={{0,1},{1,0},{2,3},{3,2},{4,5},{5,4},{6,7},{7,6},{8,16},{9,17},{10,... | collective-permute-start | bytes 393224 | tf_op jit(solution)/shard_map/ppermute | solution.py:47
  10.2 0.8 %collective-permute-start.7 = (bf16[256,256]{1,0:T(8,128)(2,1)S(1)}, bf16[256,256]{1,0:T(8,128)(2,1)S(1)}, u32[]{:S(2)}, u32[]{:S(2)}) collective-permute-start(bf16[256,256]{1,0:T(8,128)(2,1)S(1)} %collective-permute-done.3.refs_6_), channel_id=1, source_target_pairs={{0,1},{1,0},{2,3},{3,2},{4,5},{5,4},{6,7},{7,6},{8,12},{9,13},{10,... | collective-permute-start | bytes 393224 | tf_op jit(solution)/shard_map/ppermute | solution.py:47
  10.9 1.7 %collective-permute-done.4.refs_7_ = bf16[256,256]{1,0:T(8,128)(2,1)S(1)} collective-permute-done((bf16[256,256]{1,0:T(8,128)(2,1)S(1)}, bf16[256,256]{1,0:T(8,128)(2,1)S(1)}, u32[]{:S(2)}, u32[]{:S(2)}) %collective-permute-start.4) | collective-permute-done | bytes 131104 | tf_op jit(solution)/shard_map/ppermute | solution.py:47
  12.8 1.6 %collective-permute-start.8 = (bf16[256,256]{1,0:T(8,128)(2,1)S(1)}, bf16[256,256]{1,0:T(8,128)(2,1)S(1)}, u32[]{:S(2)}, u32[]{:S(2)}) collective-permute-start(bf16[256,256]{1,0:T(8,128)(2,1)S(1)} %collective-permute-done.6.refs_3_), channel_id=1, source_target_pairs={{0,1},{1,0},{2,3},{3,2},{4,5},{5,4},{6,7},{7,6},{8,16},{9,17},{10,... | collective-permute-start | bytes 393224 | tf_op jit(solution)/shard_map/ppermute | solution.py:47
  14.4 1.1 %collective-permute-done.5.refs_8_ = bf16[256,256]{1,0:T(8,128)(2,1)S(1)} collective-permute-done((bf16[256,256]{1,0:T(8,128)(2,1)S(1)}, bf16[256,256]{1,0:T(8,128)(2,1)S(1)}, u32[]{:S(2)}, u32[]{:S(2)}) %collective-permute-start.5) | collective-permute-done | bytes 131104 | tf_op jit(solution)/shard_map/ppermute | solution.py:47
  15.5 1.5 %collective-permute-start.9 = (bf16[256,256]{1,0:T(8,128)(2,1)S(1)}, bf16[256,256]{1,0:T(8,128)(2,1)S(1)}, u32[]{:S(2)}, u32[]{:S(2)}) collective-permute-start(bf16[256,256]{1,0:T(8,128)(2,1)S(1)} %collective-permute-done.5.refs_8_), channel_id=1, source_target_pairs={{0,1},{1,0},{2,3},{3,2},{4,5},{5,4},{6,7},{7,6},{8,9},{9,8},{10,11... | collective-permute-start | bytes 393224 | tf_op jit(solution)/shard_map/ppermute | solution.py:47
  17.0 2.6 %attend_next.1 = (f32[1024,128]{1,0:T(8,128)S(1)}, f32[1024,128]{1,0:T(8,128)S(1)}, f32[1024,128]{1,0:T(8,128)S(1)}, bf16[512,5376]{1,0:T(8,128)(2,1)S(1)}) custom-call(bf16[256,512]{1,0:T(8,128)(2,1)S(1)} %get-tuple-element.36.queries, f32[16,256]{1,0:T(8,128)S(1)} %get-tuple-element.37.open_beside, bf16[512,5376]{1,0:T(8,128)(2,1)} %weight_in.1, ...), custom_call_target="tpu_custom_call" | custom-call | flops 402653184 | bytes 5505024 | tf_op jit(solution)/shard_map/attend_next/pallas_call | solution.py:225
  19.6 0.9 %collective-permute-done.9.refs_6_ = bf16[256,256]{1,0:T(8,128)(2,1)S(1)} collective-permute-done((bf16[256,256]{1,0:T(8,128)(2,1)S(1)}, bf16[256,256]{1,0:T(8,128)(2,1)S(1)}, u32[]{:S(2)}, u32[]{:S(2)}) %collective-permute-start.9) | collective-permute-done | bytes 131104 | tf_op jit(solution)/shard_map/ppermute | solution.py:47
  20.4 1.5 %attend_last.1 = (bf16[128,512]{1,0:T(8,128)(2,1)S(1)}, bf16[128,512]{1,0:T(8,128)(2,1)S(1)}, f32[64,2176]{1,0:T(8,128)S(1)}, bf16[64,2176]{1,0:T(8,128)(2,1)S(1)}) custom-call(bf16[256,512]{1,0:T(8,128)(2,1)S(1)} %get-tuple-element.36.queries, bf16[512,5376]{1,0:T(8,128)(2,1)S(1)} %get-tuple-element.43.weight, f32[1024,128]{1,0:T(8,128)S(1)} %get-tuple-element.44.refs_0_, ...), custom_call_target="tpu_custom_call" | custom-call | flops 268435456 | tf_op jit(solution)/shard_map/attend_last/pallas_call | solution.py:268
  22.0 0.6 %project.2 = (f32[64,3200]{1,0:T(8,128)S(1)}, bf16[64,3200]{1,0:T(8,128)(2,1)S(1)}) custom-call(bf16[128,512]{1,0:T(8,128)(2,1)S(1)} %get-tuple-element.52.rows, bf16[512,5376]{1,0:T(8,128)(2,1)S(1)} %get-tuple-element.43.weight), custom_call_target="tpu_custom_call" | custom-call | flops 419430400 | tf_op jit(solution)/shard_map/project/pallas_call | solution.py:303
  22.6 0.9 %collective-permute-done.10.theirs = bf16[64,2176]{1,0:T(8,128)(2,1)S(1)} collective-permute-done((bf16[64,2176]{1,0:T(8,128)(2,1)S(1)}, bf16[64,2176]{1,0:T(8,128)(2,1)S(1)}, u32[]{:S(2)}, u32[]{:S(2)}) %collective-permute-start.10) | collective-permute-done | bytes 278560 | tf_op jit(solution)/shard_map/ppermute | solution.py:23
  23.6 0.2 collective-permute-start.11
  23.8 1.5 %collective-permute-start.15 = (bf16[64,1664]{1,0:T(8,128)(2,1)S(1)}, bf16[64,1664]{1,0:T(8,128)(2,1)S(1)}, u32[]{:S(2)}, u32[]{:S(2)}) collective-permute-start(bf16[64,1664]{1,0:T(8,128)(2,1)S(1)} %get-tuple-element.56), channel_id=1, source_target_pairs={{0,2},{1,3},{2,0},{3,1},{4,6},{5,7},{6,4},{7,5},{8,10},{9,11},{10,... | collective-permute-start | bytes 638984 | tf_op jit(solution)/shard_map/ppermute | solution.py:23
  25.5 1.6 %collective-permute-start.12 = (bf16[64,3200]{1,0:T(8,128)(2,1)S(1)}, bf16[64,3200]{1,0:T(8,128)(2,1)S(1)}, u32[]{:S(2)}, u32[]{:S(2)}) collective-permute-start(bf16[64,3200]{1,0:T(8,128)(2,1)S(1)} %add_up.3), channel_id=1, source_target_pairs={{0,2},{1,3},{2,0},{3,1},{4,6},{5,7},{6,4},{7,5},{8,10},{9,11},{10,... | collective-permute-start | bytes 1228808 | tf_op jit(solution)/shard_map/ppermute | solution.py:23
  27.1 0.9 %project.3 = (f32[64,5376]{1,0:T(8,128)S(1)}, bf16[64,2688]{1,0:T(8,128)(2,1)S(1)}, bf16[64,2688]{1,0:T(8,128)(2,1)S(1)}) custom-call(bf16[128,512]{1,0:T(8,128)(2,1)S(1)} %get-tuple-element.61.rows, bf16[512,5376]{1,0:T(8,128)(2,1)S(1)} %get-tuple-element.43.weight), custom_call_target="tpu_custom_call" | custom-call | flops 704643072 | tf_op jit(solution)/shard_map/project/pallas_call | solution.py:303
  28.1 0.5 %collective-permute-start.19 = (bf16[64,2688]{1,0:T(8,128)(2,1)S(1)}, bf16[64,2688]{1,0:T(8,128)(2,1)S(1)}, u32[]{:S(2)}, u32[]{:S(2)}) collective-permute-start(bf16[64,2688]{1,0:T(8,128)(2,1)S(1)} %get-tuple-element.66), channel_id=1, source_target_pairs={{0,1},{1,0},{2,3},{3,2},{4,5},{5,4},{6,7},{7,6},{8,9},{9,8},{10,11... | collective-permute-start | bytes 1032200 | tf_op jit(solution)/shard_map/ppermute | solution.py:23
  28.6 3.3 %collective-permute-done.15.refs_1_ = bf16[64,1664]{1,0:T(8,128)(2,1)S(1)} collective-permute-done((bf16[64,1664]{1,0:T(8,128)(2,1)S(1)}, bf16[64,1664]{1,0:T(8,128)(2,1)S(1)}, u32[]{:S(2)}, u32[]{:S(2)}) %collective-permute-start.15) | collective-permute-done | bytes 213024 | tf_op jit(solution)/shard_map/ppermute | solution.py:23
  31.9 0.9 %collective-permute-done.14 = bf16[64,512]{1,0:T(8,128)(2,1)S(1)} collective-permute-done((bf16[64,512]{1,0:T(8,128)(2,1)S(1)}, bf16[64,512]{1,0:T(8,128)(2,1)S(1)}, u32[]{:S(2)}, u32[]{:S(2)}) %collective-permute-start.14) | collective-permute-done | bytes 65568 | tf_op jit(solution)/shard_map/ppermute | solution.py:47
  32.8 0.5 %collective-permute-start.13 = (bf16[64,512]{1,0:T(8,128)(2,1)S(1)}, bf16[64,512]{1,0:T(8,128)(2,1)S(1)}, u32[]{:S(2)}, u32[]{:S(2)}) collective-permute-start(bf16[64,512]{1,0:T(8,128)(2,1)S(1)} %get-tuple-element.63), channel_id=1, source_target_pairs={{0,2},{1,3},{2,0},{3,1},{4,6},{5,7},{6,4},{7,5},{8,10},{9,11},{10,... | collective-permute-start | bytes 196616 | tf_op jit(solution)/shard_map/ppermute | solution.py:47
  33.3 0.7 %collective-permute-done.16 = bf16[64,512]{1,0:T(8,128)(2,1)S(1)} collective-permute-done((bf16[64,512]{1,0:T(8,128)(2,1)S(1)}, bf16[64,512]{1,0:T(8,128)(2,1)S(1)}, u32[]{:S(2)}, u32[]{:S(2)}) %collective-permute-start.16) | collective-permute-done | bytes 65568 | tf_op jit(solution)/shard_map/ppermute | solution.py:47
  34.1 3.1 %collective-permute-start.17 = (bf16[64,512]{1,0:T(8,128)(2,1)S(1)}, bf16[64,512]{1,0:T(8,128)(2,1)S(1)}, u32[]{:S(2)}, u32[]{:S(2)}) collective-permute-start(bf16[64,512]{1,0:T(8,128)(2,1)S(1)} %collective-permute-done.16), channel_id=1, source_target_pairs={{0,1},{1,0},{2,3},{3,2},{4,5},{5,4},{6,7},{7,6},{8,9},{9,8},{10,11... | collective-permute-start | bytes 196616 | tf_op jit(solution)/shard_map/ppermute | solution.py:47
  37.2 0.8 %combine.2.refs_6_ = bf16[64,5376]{1,0:T(8,128)(2,1)} custom-call(f32[64,5376]{1,0:T(8,128)S(1)} %get-tuple-element.62.refs_0_, bf16[64,1664]{1,0:T(8,128)(2,1)S(1)} %collective-permute-done.15.refs_1_, bf16[64,2688]{1,0:T(8,128)(2,1)S(1)} %collective-permute-done.18.refs_2_.refs_4_, bf16[64,2688]{1,0:T(8,128)(2,1)S(1)} %collective-permute-done.19.refs_3_.refs_5_), custom_call_target="tpu_custom_call" | custom-call | tf_op jit(solution)/shard_map/combine/pallas_call | solution.py:375
  38.0 1.4 %collective-permute-done.17.refs_3_ = bf16[64,512]{1,0:T(8,128)(2,1)S(1)} collective-permute-done((bf16[64,512]{1,0:T(8,128)(2,1)S(1)}, bf16[64,512]{1,0:T(8,128)(2,1)S(1)}, u32[]{:S(2)}, u32[]{:S(2)}) %collective-permute-start.17) | collective-permute-done | bytes 65568 | tf_op jit(solution)/shard_map/ppermute | solution.py:47
  39.4 0.7 %collective-permute-done.12.refs_1_ = bf16[64,3200]{1,0:T(8,128)(2,1)S(1)} collective-permute-done((bf16[64,3200]{1,0:T(8,128)(2,1)S(1)}, bf16[64,3200]{1,0:T(8,128)(2,1)S(1)}, u32[]{:S(2)}, u32[]{:S(2)}) %collective-permute-start.12) | collective-permute-done | bytes 409632 | tf_op jit(solution)/shard_map/ppermute | solution.py:23
  40.1 1.0 %combine.3 = bf16[64,5376]{1,0:T(8,128)(2,1)} custom-call(f32[64,5376]{1,0:T(8,128)S(1)} %get-tuple-element.62.refs_0_, bf16[64,3200]{1,0:T(8,128)(2,1)S(1)} %collective-permute-done.12.refs_1_, bf16[64,512]{1,0:T(8,128)(2,1)S(1)} %collective-permute-done.13.refs_2_, ...), custom_call_target="tpu_custom_call", output_to_operand_aliasing={{}: (6, {})} | custom-call | tf_op jit(solution)/shard_map/combine/pallas_call | solution.py:375
  (17 shorter events, 0.6 us)
Async XLA Ops:
  0.0 6.6 %collective-permute-start.2 = (bf16[256,256]{1,0:T(8,128)(2,1)}, bf16[256,256]{1,0:T(8,128)(2,1)S(1)}, u32[]{:S(2)}, u32[]{:S(2)}) collective-permute-start(bf16[256,256]{1,0:T(8,128)(2,1)} %keys_in.1), channel_id=1, source_target_pairs={{0,8},{1,9},{2,10},{3,11},{4,12},{5,13},{6,14},{7,15},{8,16},{9,17... | collective-permute-start | bytes 393224 | tf_op jit(solution)/shard_map/ppermute | solution.py:47
  0.0 6.6 %collective-permute-start = (bf16[256,256]{1,0:T(8,128)(2,1)}, bf16[256,256]{1,0:T(8,128)(2,1)S(1)}, u32[]{:S(2)}, u32[]{:S(2)}) collective-permute-start(bf16[256,256]{1,0:T(8,128)(2,1)} %keys_in.1), channel_id=1, source_target_pairs={{0,4},{1,5},{2,6},{3,7},{4,0},{5,1},{6,2},{7,3},{8,12},{9,13},{10,... | collective-permute-start | bytes 393224 | tf_op jit(solution)/shard_map/ppermute | solution.py:47
  1.9 7.5 %collective-permute-start.3 = (bf16[256,256]{1,0:T(8,128)(2,1)}, bf16[256,256]{1,0:T(8,128)(2,1)S(1)}, u32[]{:S(2)}, u32[]{:S(2)}) collective-permute-start(bf16[256,256]{1,0:T(8,128)(2,1)} %values_in.1), channel_id=1, source_target_pairs={{0,8},{1,9},{2,10},{3,11},{4,12},{5,13},{6,14},{7,15},{8,16},{9,17... | collective-permute-start | bytes 393224 | tf_op jit(solution)/shard_map/ppermute | solution.py:47
  3.4 6.7 %collective-permute-start.1 = (bf16[256,256]{1,0:T(8,128)(2,1)}, bf16[256,256]{1,0:T(8,128)(2,1)S(1)}, u32[]{:S(2)}, u32[]{:S(2)}) collective-permute-start(bf16[256,256]{1,0:T(8,128)(2,1)} %values_in.1), channel_id=1, source_target_pairs={{0,4},{1,5},{2,6},{3,7},{4,0},{5,1},{6,2},{7,3},{8,12},{9,13},{10,... | collective-permute-start | bytes 393224 | tf_op jit(solution)/shard_map/ppermute | solution.py:47
  6.6 6.0 %collective-permute-start.4 = (bf16[256,256]{1,0:T(8,128)(2,1)S(1)}, bf16[256,256]{1,0:T(8,128)(2,1)S(1)}, u32[]{:S(2)}, u32[]{:S(2)}) collective-permute-start(bf16[256,256]{1,0:T(8,128)(2,1)S(1)} %collective-permute-done.2.refs_5_), channel_id=1, source_target_pairs={{0,1},{1,0},{2,3},{3,2},{4,5},{5,4},{6,7},{7,6},{8,16},{9,17},{10,... | collective-permute-start | bytes 393224 | tf_op jit(solution)/shard_map/ppermute | solution.py:47
  6.6 6.2 %collective-permute-start.6 = (bf16[256,256]{1,0:T(8,128)(2,1)S(1)}, bf16[256,256]{1,0:T(8,128)(2,1)S(1)}, u32[]{:S(2)}, u32[]{:S(2)}) collective-permute-start(bf16[256,256]{1,0:T(8,128)(2,1)S(1)} %collective-permute-done.2.refs_5_), channel_id=1, source_target_pairs={{0,1},{1,0},{2,3},{3,2},{4,5},{5,4},{6,7},{7,6},{8,12},{9,13},{10,... | collective-permute-start | bytes 393224 | tf_op jit(solution)/shard_map/ppermute | solution.py:47
  9.4 6.1 %collective-permute-start.5 = (bf16[256,256]{1,0:T(8,128)(2,1)S(1)}, bf16[256,256]{1,0:T(8,128)(2,1)S(1)}, u32[]{:S(2)}, u32[]{:S(2)}) collective-permute-start(bf16[256,256]{1,0:T(8,128)(2,1)S(1)} %collective-permute-done.3.refs_6_), channel_id=1, source_target_pairs={{0,1},{1,0},{2,3},{3,2},{4,5},{5,4},{6,7},{7,6},{8,16},{9,17},{10,... | collective-permute-start | bytes 393224 | tf_op jit(solution)/shard_map/ppermute | solution.py:47
  10.2 9.4 %collective-permute-start.7 = (bf16[256,256]{1,0:T(8,128)(2,1)S(1)}, bf16[256,256]{1,0:T(8,128)(2,1)S(1)}, u32[]{:S(2)}, u32[]{:S(2)}) collective-permute-start(bf16[256,256]{1,0:T(8,128)(2,1)S(1)} %collective-permute-done.3.refs_6_), channel_id=1, source_target_pairs={{0,1},{1,0},{2,3},{3,2},{4,5},{5,4},{6,7},{7,6},{8,12},{9,13},{10,... | collective-permute-start | bytes 393224 | tf_op jit(solution)/shard_map/ppermute | solution.py:47
  12.8 6.8 %collective-permute-start.8 = (bf16[256,256]{1,0:T(8,128)(2,1)S(1)}, bf16[256,256]{1,0:T(8,128)(2,1)S(1)}, u32[]{:S(2)}, u32[]{:S(2)}) collective-permute-start(bf16[256,256]{1,0:T(8,128)(2,1)S(1)} %collective-permute-done.6.refs_3_), channel_id=1, source_target_pairs={{0,1},{1,0},{2,3},{3,2},{4,5},{5,4},{6,7},{7,6},{8,16},{9,17},{10,... | collective-permute-start | bytes 393224 | tf_op jit(solution)/shard_map/ppermute | solution.py:47
  15.5 5.0 %collective-permute-start.9 = (bf16[256,256]{1,0:T(8,128)(2,1)S(1)}, bf16[256,256]{1,0:T(8,128)(2,1)S(1)}, u32[]{:S(2)}, u32[]{:S(2)}) collective-permute-start(bf16[256,256]{1,0:T(8,128)(2,1)S(1)} %collective-permute-done.5.refs_8_), channel_id=1, source_target_pairs={{0,1},{1,0},{2,3},{3,2},{4,5},{5,4},{6,7},{7,6},{8,9},{9,8},{10,11... | collective-permute-start | bytes 393224 | tf_op jit(solution)/shard_map/ppermute | solution.py:47
  21.9 1.6 %collective-permute-start.10 = (bf16[64,2176]{1,0:T(8,128)(2,1)S(1)}, bf16[64,2176]{1,0:T(8,128)(2,1)S(1)}, u32[]{:S(2)}, u32[]{:S(2)}) collective-permute-start(bf16[64,2176]{1,0:T(8,128)(2,1)S(1)} %get-tuple-element.55), channel_id=1, source_target_pairs={{0,1},{1,0},{2,3},{3,2},{4,5},{5,4},{6,7},{7,6},{8,9},{9,8},{10,11... | collective-permute-start | bytes 835592 | tf_op jit(solution)/shard_map/ppermute | solution.py:23
  23.6 1.8 %collective-permute-start.11 = (bf16[64,3200]{1,0:T(8,128)(2,1)S(1)}, bf16[64,3200]{1,0:T(8,128)(2,1)S(1)}, u32[]{:S(2)}, u32[]{:S(2)}) collective-permute-start(bf16[64,3200]{1,0:T(8,128)(2,1)S(1)} %get-tuple-element.60), channel_id=1, source_target_pairs={{0,1},{1,0},{2,3},{3,2},{4,5},{5,4},{6,7},{7,6},{8,9},{9,8},{10,11... | collective-permute-start | bytes 1228808 | tf_op jit(solution)/shard_map/ppermute | solution.py:23
  23.8 8.1 %collective-permute-start.15 = (bf16[64,1664]{1,0:T(8,128)(2,1)S(1)}, bf16[64,1664]{1,0:T(8,128)(2,1)S(1)}, u32[]{:S(2)}, u32[]{:S(2)}) collective-permute-start(bf16[64,1664]{1,0:T(8,128)(2,1)S(1)} %get-tuple-element.56), channel_id=1, source_target_pairs={{0,2},{1,3},{2,0},{3,1},{4,6},{5,7},{6,4},{7,5},{8,10},{9,11},{10,... | collective-permute-start | bytes 638984 | tf_op jit(solution)/shard_map/ppermute | solution.py:23
  25.5 14.6 %collective-permute-start.12 = (bf16[64,3200]{1,0:T(8,128)(2,1)S(1)}, bf16[64,3200]{1,0:T(8,128)(2,1)S(1)}, u32[]{:S(2)}, u32[]{:S(2)}) collective-permute-start(bf16[64,3200]{1,0:T(8,128)(2,1)S(1)} %add_up.3), channel_id=1, source_target_pairs={{0,2},{1,3},{2,0},{3,1},{4,6},{5,7},{6,4},{7,5},{8,10},{9,11},{10,... | collective-permute-start | bytes 1228808 | tf_op jit(solution)/shard_map/ppermute | solution.py:23
  28.0 9.2 %collective-permute-start.18 = (bf16[64,2688]{1,0:T(8,128)(2,1)S(1)}, bf16[64,2688]{1,0:T(8,128)(2,1)S(1)}, u32[]{:S(2)}, u32[]{:S(2)}) collective-permute-start(bf16[64,2688]{1,0:T(8,128)(2,1)S(1)} %get-tuple-element.65), channel_id=1, source_target_pairs={{0,1},{1,0},{2,3},{3,2},{4,5},{5,4},{6,7},{7,6},{8,9},{9,8},{10,11... | collective-permute-start | bytes 1032200 | tf_op jit(solution)/shard_map/ppermute | solution.py:23
  28.1 9.1 %collective-permute-start.19 = (bf16[64,2688]{1,0:T(8,128)(2,1)S(1)}, bf16[64,2688]{1,0:T(8,128)(2,1)S(1)}, u32[]{:S(2)}, u32[]{:S(2)}) collective-permute-start(bf16[64,2688]{1,0:T(8,128)(2,1)S(1)} %get-tuple-element.66), channel_id=1, source_target_pairs={{0,1},{1,0},{2,3},{3,2},{4,5},{5,4},{6,7},{7,6},{8,9},{9,8},{10,11... | collective-permute-start | bytes 1032200 | tf_op jit(solution)/shard_map/ppermute | solution.py:23
  28.6 4.3 %collective-permute-start.14 = (bf16[64,512]{1,0:T(8,128)(2,1)S(1)}, bf16[64,512]{1,0:T(8,128)(2,1)S(1)}, u32[]{:S(2)}, u32[]{:S(2)}) collective-permute-start(bf16[64,512]{1,0:T(8,128)(2,1)S(1)} %get-tuple-element.63), channel_id=1, source_target_pairs={{0,1},{1,0},{2,3},{3,2},{4,5},{5,4},{6,7},{7,6},{8,9},{9,8},{10,11... | collective-permute-start | bytes 196616 | tf_op jit(solution)/shard_map/ppermute | solution.py:47
  32.8 1.3 %collective-permute-start.16 = (bf16[64,512]{1,0:T(8,128)(2,1)S(1)}, bf16[64,512]{1,0:T(8,128)(2,1)S(1)}, u32[]{:S(2)}, u32[]{:S(2)}) collective-permute-start(bf16[64,512]{1,0:T(8,128)(2,1)S(1)} %collective-permute-done.14), channel_id=1, source_target_pairs={{0,1},{1,0},{2,3},{3,2},{4,5},{5,4},{6,7},{7,6},{8,9},{9,8},{10,11... | collective-permute-start | bytes 196616 | tf_op jit(solution)/shard_map/ppermute | solution.py:47
  32.8 5.2 %collective-permute-start.13 = (bf16[64,512]{1,0:T(8,128)(2,1)S(1)}, bf16[64,512]{1,0:T(8,128)(2,1)S(1)}, u32[]{:S(2)}, u32[]{:S(2)}) collective-permute-start(bf16[64,512]{1,0:T(8,128)(2,1)S(1)} %get-tuple-element.63), channel_id=1, source_target_pairs={{0,2},{1,3},{2,0},{3,1},{4,6},{5,7},{6,4},{7,5},{8,10},{9,11},{10,... | collective-permute-start | bytes 196616 | tf_op jit(solution)/shard_map/ppermute | solution.py:47
  34.1 5.3 %collective-permute-start.17 = (bf16[64,512]{1,0:T(8,128)(2,1)S(1)}, bf16[64,512]{1,0:T(8,128)(2,1)S(1)}, u32[]{:S(2)}, u32[]{:S(2)}) collective-permute-start(bf16[64,512]{1,0:T(8,128)(2,1)S(1)} %collective-permute-done.16), channel_id=1, source_target_pairs={{0,1},{1,0},{2,3},{3,2},{4,5},{5,4},{6,7},{7,6},{8,9},{9,8},{10,11... | collective-permute-start | bytes 196616 | tf_op jit(solution)/shard_map/ppermute | solution.py:47

commit v8 on v6

--- a/solution.py
+++ b/solution.py
@@ -144,13 +144,19 @@
     return list(zip(refs[0::2], refs[1::2]))
 
 
-def first_kernel(docs_in, queries_in, keys_in, values_in, *refs):
-    *state, queries, open_beside, docs, keys, values, sems = refs
-    places = ((docs_in, docs), (queries_in, queries), (keys_in, keys), (values_in, values))
+def first_kernel(split, docs_in, queries_in, keys_in, values_in, weight_in, *refs):
+    *state, queries, open_beside, weight, docs, keys, values, sems = refs
+    places = (
+        (docs_in, docs),
+        (queries_in, queries),
+        (keys_in, keys),
+        (values_in, values),
+        (weight_in.at[:, :split], weight.at[:, :split]),
+    )
     fetches = [pltpu.make_async_copy(a, b, sems.at[i]) for i, (a, b) in enumerate(places)]
     for fetch in fetches:
         fetch.start()
-    for fetch in fetches:
+    for fetch in fetches[:4]:
         fetch.wait()
     position = lax.axis_index("ctx")
     q_blocks = queries.shape[0] // BLOCK
@@ -167,11 +173,12 @@
             part = open_beside.at[a * 8 : (a + 1) * 8, b * BLOCK : (b + 1) * BLOCK]
             part[...] = jnp.full(part.shape, doors(1, a, b), jnp.float32)
     absorb((0,), doors, queries, [(keys, values)], None, store_state(state))
-
-
-def next_kernel(numbers, queries, open_beside, weight_in, *refs):
+    fetches[4].wait()
+
+
+def next_kernel(numbers, split, queries, open_beside, weight_in, _, *refs):
     *refs, weight, sem = refs
-    fetch = pltpu.make_async_copy(weight_in, weight, sem)
+    fetch = pltpu.make_async_copy(weight_in.at[:, split:], weight.at[:, split:], sem)
     fetch.start()
     pairs = 2 * len(numbers)
 
@@ -197,35 +204,37 @@
     return (pltpu.VMEM((rows, HEAD_SIZE), jnp.float32),) * 3
 
 
-def attend_first(docs, queries, keys, values):
+def attend_first(docs, queries, keys, values, weight, split):
     n_query = queries.shape[0]
     return pl.pallas_call(
-        first_kernel,
+        functools.partial(first_kernel, split),
         out_shape=state_shapes(queries)
         + (
             pltpu.VMEM(queries.shape, queries.dtype),
             pltpu.VMEM((8 * n_query // BLOCK, n_query), jnp.float32),
+            pltpu.VMEM(weight.shape, weight.dtype),
         ),
-        in_specs=[HBM] * 4,
-        out_specs=(VMEM,) * 5,
+        in_specs=[HBM] * 5,
+        out_specs=(VMEM,) * 6,
         scratch_shapes=[
             pltpu.SMEM(docs.shape, docs.dtype),
             pltpu.VMEM(keys.shape, keys.dtype),
             pltpu.VMEM(values.shape, values.dtype),
-            pltpu.SemaphoreType.DMA((4,)),
+            pltpu.SemaphoreType.DMA((5,)),
         ],
         compiler_params=LIMIT,
         cost_estimate=attend_cost(queries, (0,)),
         name="attend_first",
-    )(*[pltpu.with_memory_space_constraint(x, pltpu.HBM) for x in (docs, queries, keys, values)])
-
-
-def attend_next(queries, open_beside, weight, state, chunks, numbers):
-    return pl.pallas_call(
-        functools.partial(next_kernel, numbers),
+    )(*[pltpu.with_memory_space_constraint(x, pltpu.HBM) for x in (docs, queries, keys, values, weight)])
+
+
+def attend_next(queries, open_beside, weight, part, split, state, chunks, numbers):
+    return pl.pallas_call(
+        functools.partial(next_kernel, numbers, split),
         out_shape=state_shapes(queries) + (pltpu.VMEM(weight.shape, weight.dtype),),
-        in_specs=[VMEM, VMEM, HBM] + [VMEM] * (3 + 2 * len(chunks)),
+        in_specs=[VMEM, VMEM, HBM] + [VMEM] * (4 + 2 * len(chunks)),
         out_specs=(VMEM,) * 4,
+        input_output_aliases={3: 3},
         scratch_shapes=[pltpu.SemaphoreType.DMA],
         compiler_params=LIMIT,
         cost_estimate=attend_cost(queries, numbers, 2 * weight.size),
@@ -234,9 +243,27 @@
         queries,
         open_beside,
         pltpu.with_memory_space_constraint(weight, pltpu.HBM),
+        part,
         *state,
         *[x for pair in chunks for x in pair],
     )
+
+
+def middle_kernel(numbers, queries, *refs):
+    pairs = 2 * len(numbers)
+    absorb(numbers, None, queries, pairs_of(refs[3 : 3 + pairs]), refs[:3], store_state(refs[3 + pairs :]))
+
+
+def attend_middle(queries, state, chunks, numbers):
+    return pl.pallas_call(
+        functools.partial(middle_kernel, numbers),
+        out_shape=state_shapes(queries),
+        in_specs=[VMEM] * (4 + 2 * len(chunks)),
+        out_specs=(VMEM,) * 3,
+        compiler_params=LIMIT,
+        cost_estimate=attend_cost(queries, numbers),
+        name="attend_middle",
+    )(queries, *state, *[x for pair in chunks for x in pair])
 
 
 def last_kernel(numbers, columns, queries, weight, *refs):
@@ -475,7 +502,10 @@
     if n_ctx == 8:
         by_two = [move(x, BY_TWO) for x in (keys, values)]
         beside = [move(x, BESIDE) for x in (keys, values)]
-        *state, fetched, open_beside = attend_first(doc_ids, queries, keys, values)
+        split = columns // 3 // BLOCK * BLOCK
+        *state, fetched, open_beside, part = attend_first(
+            doc_ids, queries, keys, values, out_weight, split
+        )
         by_four = [move(after(x, state[0]), AGAIN) for x in by_two]
         swap_two = [
             move(after(after(by_two[0], beside[0]), state[0]), ACROSS),
@@ -483,9 +513,12 @@
         ]
         swap_four = [move(after(swap_two[0], by_four[0]), AGAIN), move(by_four[1], LAST)]
         chunks = [beside, by_two, by_four]
-        *state, weight = attend_next(fetched, open_beside, out_weight, state, chunks, (1, 2, 3))
-        chunks = [swap_two, swap_four]
-        far, near, mine, send = attend_last(fetched, weight, state, chunks, (4, 5), (0, cuts[2]))
+        *state, weight = attend_next(
+            fetched, open_beside, out_weight, part, split, state, chunks, (1, 2, 3)
+        )
+        state = attend_middle(fetched, state, [swap_two], (4,))
+        chunks = [swap_four]
+        far, near, mine, send = attend_last(fetched, weight, state, chunks, (5,), (0, cuts[2]))
     else:
         weight = out_weight
         attended = ring_attention(queries, keys, values, doc_ids, n_ctx, position)

time: 41.2 us -> 40.9 us (level)
    pallas_call x2 -> x3, Pallas kernels: 4.19 us -> 4.48 us  [the longest x1 2.06 us: attend_next(): pl.pallas_call(functools.partial(next_kernel, numbers, split), out_shape=...]
  transfers between devices with their start and end apart: 20 -> 20, of which waited for: 13 -> 13; matrix products, arithmetic and copies ran while one was open for 0% -> 0% of each run, Pallas kernels for 16% -> 17%
where the time goes in v8:
time: 40.9 us; the launch traced here: 40.7 us
  starting transfers between devices  17.9 us (44%)
  waiting for transfers between devices  13.8 us (34%)
  Pallas kernels  8.94 us (22%)
    ppermute x14, starting transfers between devices, move(): return lax.ppermute(block, ('ctx', 'head'), pairs)  14 us
    ppermute x14, waiting for transfers between devices, move(): return lax.ppermute(block, ('ctx', 'head'), pairs)  8.62 us
    ppermute x6, waiting for transfers between devices, hop(): return lax.ppermute(block, axis, pairs)  5.19 us
    ppermute x6, starting transfers between devices, hop(): return lax.ppermute(block, axis, pairs)  3.82 us
    pallas_call x1, Pallas kernels, attend_next(): pl.pallas_call(functools.partial(next_kernel, numbers, split), out_shape=...  2.06 us
    pallas_call x1, Pallas kernels, attend_first(): pl.pallas_call(functools.partial(first_kernel, split), out_shape=state_sh...  1.77 us
    pallas_call x2, Pallas kernels, combine(): pl.pallas_call(kernel, out_shape=jax.ShapeDtypeStruct(mine.shape, jnp.bfl...  1.66 us
    pallas_call x2, Pallas kernels, project(): pl.pallas_call(functools.partial(project_kernel, columns), out_shape=proj...  1.54 us
  transfers between devices with their start and end apart: 20, of which 13 were waited for; matrix products, arithmetic and copies ran while one was open for 0% of the time, Pallas kernels for 17%

profile of v8, /device:TPU:16, one launch (start us, length us, event | category | flops | bytes accessed | tf_op | source)
XLA Modules:
  0.0 40.7 jit_solution(16943940260193557174)
XLA Ops:
  0.0 1.9 %collective-permute-start = (bf16[256,256]{1,0:T(8,128)(2,1)}, bf16[256,256]{1,0:T(8,128)(2,1)S(1)}, u32[]{:S(2)}, u32[]{:S(2)}) collective-permute-start(bf16[256,256]{1,0:T(8,128)(2,1)} %keys_in.1), channel_id=1, source_target_pairs={{0,4},{1,5},{2,6},{3,7},{4,0},{5,1},{6,2},{7,3},{8,12},{9,13},{10,... | collective-permute-start | bytes 393224 | tf_op jit(solution)/shard_map/ppermute | solution.py:46
  1.9 1.6 %collective-permute-start.3 = (bf16[256,256]{1,0:T(8,128)(2,1)}, bf16[256,256]{1,0:T(8,128)(2,1)S(1)}, u32[]{:S(2)}, u32[]{:S(2)}) collective-permute-start(bf16[256,256]{1,0:T(8,128)(2,1)} %values_in.1), channel_id=1, source_target_pairs={{0,8},{1,9},{2,10},{3,11},{4,12},{5,13},{6,14},{7,15},{8,16},{9,17... | collective-permute-start | bytes 393224 | tf_op jit(solution)/shard_map/ppermute | solution.py:46
  3.4 0.5 %collective-permute-start.1 = (bf16[256,256]{1,0:T(8,128)(2,1)}, bf16[256,256]{1,0:T(8,128)(2,1)S(1)}, u32[]{:S(2)}, u32[]{:S(2)}) collective-permute-start(bf16[256,256]{1,0:T(8,128)(2,1)} %values_in.1), channel_id=1, source_target_pairs={{0,4},{1,5},{2,6},{3,7},{4,0},{5,1},{6,2},{7,3},{8,12},{9,13},{10,... | collective-permute-start | bytes 393224 | tf_op jit(solution)/shard_map/ppermute | solution.py:46
  3.9 1.8 %attend_first.1 = (f32[1024,128]{1,0:T(8,128)S(1)}, f32[1024,128]{1,0:T(8,128)S(1)}, f32[1024,128]{1,0:T(8,128)S(1)}, bf16[256,512]{1,0:T(8,128)(2,1)S(1)}, f32[...) custom-call(s32[16]{0:T(128)} %docs_in.1, bf16[256,512]{1,0:T(8,128)(2,1)} %queries_in.1, bf16[256,256]{1,0:T(8,128)(2,1)} %keys_in.1, ...), custom_call_target="tpu_custom_call" | custom-call | flops 134217728 | tf_op jit(solution)/shard_map/attend_first/pallas_call | solution.py:209
  5.7 0.9 %collective-permute-done.2.refs_5_ = bf16[256,256]{1,0:T(8,128)(2,1)S(1)} collective-permute-done((bf16[256,256]{1,0:T(8,128)(2,1)}, bf16[256,256]{1,0:T(8,128)(2,1)S(1)}, u32[]{:S(2)}, u32[]{:S(2)}) %collective-permute-start.2) | collective-permute-done | bytes 131104 | tf_op jit(solution)/shard_map/ppermute | solution.py:46
  6.6 2.0 %collective-permute-start.6 = (bf16[256,256]{1,0:T(8,128)(2,1)S(1)}, bf16[256,256]{1,0:T(8,128)(2,1)S(1)}, u32[]{:S(2)}, u32[]{:S(2)}) collective-permute-start(bf16[256,256]{1,0:T(8,128)(2,1)S(1)} %collective-permute-done.2.refs_5_), channel_id=1, source_target_pairs={{0,1},{1,0},{2,3},{3,2},{4,5},{5,4},{6,7},{7,6},{8,12},{9,13},{10,... | collective-permute-start | bytes 393224 | tf_op jit(solution)/shard_map/ppermute | solution.py:46
  8.6 0.8 %collective-permute-done.3.refs_6_ = bf16[256,256]{1,0:T(8,128)(2,1)S(1)} collective-permute-done((bf16[256,256]{1,0:T(8,128)(2,1)}, bf16[256,256]{1,0:T(8,128)(2,1)S(1)}, u32[]{:S(2)}, u32[]{:S(2)}) %collective-permute-start.3) | collective-permute-done | bytes 131104 | tf_op jit(solution)/shard_map/ppermute | solution.py:46
  9.4 0.7 %collective-permute-start.5 = (bf16[256,256]{1,0:T(8,128)(2,1)S(1)}, bf16[256,256]{1,0:T(8,128)(2,1)S(1)}, u32[]{:S(2)}, u32[]{:S(2)}) collective-permute-start(bf16[256,256]{1,0:T(8,128)(2,1)S(1)} %collective-permute-done.3.refs_6_), channel_id=1, source_target_pairs={{0,1},{1,0},{2,3},{3,2},{4,5},{5,4},{6,7},{7,6},{8,16},{9,17},{10,... | collective-permute-start | bytes 393224 | tf_op jit(solution)/shard_map/ppermute | solution.py:46
  10.2 0.8 %collective-permute-start.7 = (bf16[256,256]{1,0:T(8,128)(2,1)S(1)}, bf16[256,256]{1,0:T(8,128)(2,1)S(1)}, u32[]{:S(2)}, u32[]{:S(2)}) collective-permute-start(bf16[256,256]{1,0:T(8,128)(2,1)S(1)} %collective-permute-done.3.refs_6_), channel_id=1, source_target_pairs={{0,1},{1,0},{2,3},{3,2},{4,5},{5,4},{6,7},{7,6},{8,12},{9,13},{10,... | collective-permute-start | bytes 393224 | tf_op jit(solution)/shard_map/ppermute | solution.py:46
  10.9 1.7 %collective-permute-done.4.refs_7_ = bf16[256,256]{1,0:T(8,128)(2,1)S(1)} collective-permute-done((bf16[256,256]{1,0:T(8,128)(2,1)S(1)}, bf16[256,256]{1,0:T(8,128)(2,1)S(1)}, u32[]{:S(2)}, u32[]{:S(2)}) %collective-permute-start.4) | collective-permute-done | bytes 131104 | tf_op jit(solution)/shard_map/ppermute | solution.py:46
  12.8 1.5 %collective-permute-start.8 = (bf16[256,256]{1,0:T(8,128)(2,1)S(1)}, bf16[256,256]{1,0:T(8,128)(2,1)S(1)}, u32[]{:S(2)}, u32[]{:S(2)}) collective-permute-start(bf16[256,256]{1,0:T(8,128)(2,1)S(1)} %collective-permute-done.6.refs_3_), channel_id=1, source_target_pairs={{0,1},{1,0},{2,3},{3,2},{4,5},{5,4},{6,7},{7,6},{8,16},{9,17},{10,... | collective-permute-start | bytes 393224 | tf_op jit(solution)/shard_map/ppermute | solution.py:46
  14.4 1.1 %collective-permute-done.5.refs_8_ = bf16[256,256]{1,0:T(8,128)(2,1)S(1)} collective-permute-done((bf16[256,256]{1,0:T(8,128)(2,1)S(1)}, bf16[256,256]{1,0:T(8,128)(2,1)S(1)}, u32[]{:S(2)}, u32[]{:S(2)}) %collective-permute-start.5) | collective-permute-done | bytes 131104 | tf_op jit(solution)/shard_map/ppermute | solution.py:46
  15.5 1.4 %collective-permute-start.9 = (bf16[256,256]{1,0:T(8,128)(2,1)S(1)}, bf16[256,256]{1,0:T(8,128)(2,1)S(1)}, u32[]{:S(2)}, u32[]{:S(2)}) collective-permute-start(bf16[256,256]{1,0:T(8,128)(2,1)S(1)} %collective-permute-done.5.refs_8_), channel_id=1, source_target_pairs={{0,1},{1,0},{2,3},{3,2},{4,5},{5,4},{6,7},{7,6},{8,9},{9,8},{10,11... | collective-permute-start | bytes 393224 | tf_op jit(solution)/shard_map/ppermute | solution.py:46
  17.0 2.1 %attend_next.1 = (f32[1024,128]{1,0:T(8,128)S(1)}, f32[1024,128]{1,0:T(8,128)S(1)}, f32[1024,128]{1,0:T(8,128)S(1)}, bf16[512,5376]{1,0:T(8,128)(2,1)S(1)}) custom-call(bf16[256,512]{1,0:T(8,128)(2,1)S(1)} %get-tuple-element.40.queries, f32[16,256]{1,0:T(8,128)S(1)} %get-tuple-element.41.open_beside, ...), custom_call_target="tpu_custom_call", output_to_operand_aliasing={{3}: (3, {})} | custom-call | flops 402653184 | bytes 5505024 | tf_op jit(solution)/shard_map/attend_next/pallas_call | solution.py:232
  19.0 0.6 %attend_middle.1 = (f32[1024,128]{1,0:T(8,128)S(1)}, f32[1024,128]{1,0:T(8,128)S(1)}, f32[1024,128]{1,0:T(8,128)S(1)}) custom-call(bf16[256,512]{1,0:T(8,128)(2,1)S(1)} %get-tuple-element.40.queries, f32[1024,128]{1,0:T(8,128)S(1)} %get-tuple-element.49.refs_0_, f32[1024,128]{1,0:T(8,128)S(1)} %get-tuple-element.50.refs_1_, ...), custom_call_target="tpu_custom_call" | custom-call | flops 134217728 | tf_op jit(solution)/shard_map/attend_middle/pallas_call | solution.py:258
  19.7 0.8 %collective-permute-done.9.refs_4_ = bf16[256,256]{1,0:T(8,128)(2,1)S(1)} collective-permute-done((bf16[256,256]{1,0:T(8,128)(2,1)S(1)}, bf16[256,256]{1,0:T(8,128)(2,1)S(1)}, u32[]{:S(2)}, u32[]{:S(2)}) %collective-permute-start.9) | collective-permute-done | bytes 131104 | tf_op jit(solution)/shard_map/ppermute | solution.py:46
  20.5 1.1 %attend_last.1 = (bf16[128,512]{1,0:T(8,128)(2,1)S(1)}, bf16[128,512]{1,0:T(8,128)(2,1)S(1)}, f32[64,2176]{1,0:T(8,128)S(1)}, bf16[64,2176]{1,0:T(8,128)(2,1)S(1)}) custom-call(bf16[256,512]{1,0:T(8,128)(2,1)S(1)} %get-tuple-element.40.queries, bf16[512,5376]{1,0:T(8,128)(2,1)S(1)} %get-tuple-element.48.weight, f32[1024,128]{1,0:T(8,128)S(1)} %get-tuple-element.55.refs_0_, ...), custom_call_target="tpu_custom_call" | custom-call | flops 134217728 | tf_op jit(solution)/shard_map/attend_last/pallas_call | solution.py:294
  21.7 0.6 %project.2 = (f32[64,3200]{1,0:T(8,128)S(1)}, bf16[64,3200]{1,0:T(8,128)(2,1)S(1)}) custom-call(bf16[128,512]{1,0:T(8,128)(2,1)S(1)} %get-tuple-element.60.rows, bf16[512,5376]{1,0:T(8,128)(2,1)S(1)} %get-tuple-element.48.weight), custom_call_target="tpu_custom_call" | custom-call | flops 419430400 | tf_op jit(solution)/shard_map/project/pallas_call | solution.py:329
  22.3 0.9 %collective-permute-done.10.theirs = bf16[64,2176]{1,0:T(8,128)(2,1)S(1)} collective-permute-done((bf16[64,2176]{1,0:T(8,128)(2,1)S(1)}, bf16[64,2176]{1,0:T(8,128)(2,1)S(1)}, u32[]{:S(2)}, u32[]{:S(2)}) %collective-permute-start.10) | collective-permute-done | bytes 278560 | tf_op jit(solution)/shard_map/ppermute | solution.py:22
  23.5 1.5 %collective-permute-start.15 = (bf16[64,1664]{1,0:T(8,128)(2,1)S(1)}, bf16[64,1664]{1,0:T(8,128)(2,1)S(1)}, u32[]{:S(2)}, u32[]{:S(2)}) collective-permute-start(bf16[64,1664]{1,0:T(8,128)(2,1)S(1)} %get-tuple-element.64), channel_id=1, source_target_pairs={{0,2},{1,3},{2,0},{3,1},{4,6},{5,7},{6,4},{7,5},{8,10},{9,11},{10,... | collective-permute-start | bytes 638984 | tf_op jit(solution)/shard_map/ppermute | solution.py:22
  25.2 1.5 %collective-permute-start.12 = (bf16[64,3200]{1,0:T(8,128)(2,1)S(1)}, bf16[64,3200]{1,0:T(8,128)(2,1)S(1)}, u32[]{:S(2)}, u32[]{:S(2)}) collective-permute-start(bf16[64,3200]{1,0:T(8,128)(2,1)S(1)} %add_up.3), channel_id=1, source_target_pairs={{0,2},{1,3},{2,0},{3,1},{4,6},{5,7},{6,4},{7,5},{8,10},{9,11},{10,... | collective-permute-start | bytes 1228808 | tf_op jit(solution)/shard_map/ppermute | solution.py:22
  26.7 0.9 %project.3 = (f32[64,5376]{1,0:T(8,128)S(1)}, bf16[64,2688]{1,0:T(8,128)(2,1)S(1)}, bf16[64,2688]{1,0:T(8,128)(2,1)S(1)}) custom-call(bf16[128,512]{1,0:T(8,128)(2,1)S(1)} %get-tuple-element.69.rows, bf16[512,5376]{1,0:T(8,128)(2,1)S(1)} %get-tuple-element.48.weight), custom_call_target="tpu_custom_call" | custom-call | flops 704643072 | tf_op jit(solution)/shard_map/project/pallas_call | solution.py:329
  27.7 0.5 %collective-permute-start.19 = (bf16[64,2688]{1,0:T(8,128)(2,1)S(1)}, bf16[64,2688]{1,0:T(8,128)(2,1)S(1)}, u32[]{:S(2)}, u32[]{:S(2)}) collective-permute-start(bf16[64,2688]{1,0:T(8,128)(2,1)S(1)} %get-tuple-element.74), channel_id=1, source_target_pairs={{0,1},{1,0},{2,3},{3,2},{4,5},{5,4},{6,7},{7,6},{8,9},{9,8},{10,11... | collective-permute-start | bytes 1032200 | tf_op jit(solution)/shard_map/ppermute | solution.py:22
  28.2 3.4 %collective-permute-done.15.refs_1_ = bf16[64,1664]{1,0:T(8,128)(2,1)S(1)} collective-permute-done((bf16[64,1664]{1,0:T(8,128)(2,1)S(1)}, bf16[64,1664]{1,0:T(8,128)(2,1)S(1)}, u32[]{:S(2)}, u32[]{:S(2)}) %collective-permute-start.15) | collective-permute-done | bytes 213024 | tf_op jit(solution)/shard_map/ppermute | solution.py:22
  31.6 0.9 %collective-permute-done.14 = bf16[64,512]{1,0:T(8,128)(2,1)S(1)} collective-permute-done((bf16[64,512]{1,0:T(8,128)(2,1)S(1)}, bf16[64,512]{1,0:T(8,128)(2,1)S(1)}, u32[]{:S(2)}, u32[]{:S(2)}) %collective-permute-start.14) | collective-permute-done | bytes 65568 | tf_op jit(solution)/shard_map/ppermute | solution.py:46
  32.5 0.5 %collective-permute-start.13 = (bf16[64,512]{1,0:T(8,128)(2,1)S(1)}, bf16[64,512]{1,0:T(8,128)(2,1)S(1)}, u32[]{:S(2)}, u32[]{:S(2)}) collective-permute-start(bf16[64,512]{1,0:T(8,128)(2,1)S(1)} %get-tuple-element.71), channel_id=1, source_target_pairs={{0,2},{1,3},{2,0},{3,1},{4,6},{5,7},{6,4},{7,5},{8,10},{9,11},{10,... | collective-permute-start | bytes 196616 | tf_op jit(solution)/shard_map/ppermute | solution.py:46
  33.0 0.7 %collective-permute-done.16 = bf16[64,512]{1,0:T(8,128)(2,1)S(1)} collective-permute-done((bf16[64,512]{1,0:T(8,128)(2,1)S(1)}, bf16[64,512]{1,0:T(8,128)(2,1)S(1)}, u32[]{:S(2)}, u32[]{:S(2)}) %collective-permute-start.16) | collective-permute-done | bytes 65568 | tf_op jit(solution)/shard_map/ppermute | solution.py:46
  33.7 3.1 %collective-permute-start.17 = (bf16[64,512]{1,0:T(8,128)(2,1)S(1)}, bf16[64,512]{1,0:T(8,128)(2,1)S(1)}, u32[]{:S(2)}, u32[]{:S(2)}) collective-permute-start(bf16[64,512]{1,0:T(8,128)(2,1)S(1)} %collective-permute-done.16), channel_id=1, source_target_pairs={{0,1},{1,0},{2,3},{3,2},{4,5},{5,4},{6,7},{7,6},{8,9},{9,8},{10,11... | collective-permute-start | bytes 196616 | tf_op jit(solution)/shard_map/ppermute | solution.py:46
  36.8 0.8 %combine.2.refs_6_ = bf16[64,5376]{1,0:T(8,128)(2,1)} custom-call(f32[64,5376]{1,0:T(8,128)S(1)} %get-tuple-element.70.refs_0_, bf16[64,1664]{1,0:T(8,128)(2,1)S(1)} %collective-permute-done.15.refs_1_, bf16[64,2688]{1,0:T(8,128)(2,1)S(1)} %collective-permute-done.18.refs_2_.refs_4_, bf16[64,2688]{1,0:T(8,128)(2,1)S(1)} %collective-permute-done.19.refs_3_.refs_5_), custom_call_target="tpu_custom_call" | custom-call | tf_op jit(solution)/shard_map/combine/pallas_call | solution.py:398
  37.6 1.5 %collective-permute-done.17.refs_3_ = bf16[64,512]{1,0:T(8,128)(2,1)S(1)} collective-permute-done((bf16[64,512]{1,0:T(8,128)(2,1)S(1)}, bf16[64,512]{1,0:T(8,128)(2,1)S(1)}, u32[]{:S(2)}, u32[]{:S(2)}) %collective-permute-start.17) | collective-permute-done | bytes 65568 | tf_op jit(solution)/shard_map/ppermute | solution.py:46
  39.1 0.7 %collective-permute-done.12.refs_1_ = bf16[64,3200]{1,0:T(8,128)(2,1)S(1)} collective-permute-done((bf16[64,3200]{1,0:T(8,128)(2,1)S(1)}, bf16[64,3200]{1,0:T(8,128)(2,1)S(1)}, u32[]{:S(2)}, u32[]{:S(2)}) %collective-permute-start.12) | collective-permute-done | bytes 409632 | tf_op jit(solution)/shard_map/ppermute | solution.py:22
  39.8 0.9 %combine.3 = bf16[64,5376]{1,0:T(8,128)(2,1)} custom-call(f32[64,5376]{1,0:T(8,128)S(1)} %get-tuple-element.70.refs_0_, bf16[64,3200]{1,0:T(8,128)(2,1)S(1)} %collective-permute-done.12.refs_1_, bf16[64,512]{1,0:T(8,128)(2,1)S(1)} %collective-permute-done.13.refs_2_, ...), custom_call_target="tpu_custom_call", output_to_operand_aliasing={{}: (6, {})} | custom-call | tf_op jit(solution)/shard_map/combine/pallas_call | solution.py:398
  (18 shorter events, 0.8 us)
Async XLA Ops:
  0.0 6.6 %collective-permute-start.2 = (bf16[256,256]{1,0:T(8,128)(2,1)}, bf16[256,256]{1,0:T(8,128)(2,1)S(1)}, u32[]{:S(2)}, u32[]{:S(2)}) collective-permute-start(bf16[256,256]{1,0:T(8,128)(2,1)} %keys_in.1), channel_id=1, source_target_pairs={{0,8},{1,9},{2,10},{3,11},{4,12},{5,13},{6,14},{7,15},{8,16},{9,17... | collective-permute-start | bytes 393224 | tf_op jit(solution)/shard_map/ppermute | solution.py:46
  0.0 6.6 %collective-permute-start = (bf16[256,256]{1,0:T(8,128)(2,1)}, bf16[256,256]{1,0:T(8,128)(2,1)S(1)}, u32[]{:S(2)}, u32[]{:S(2)}) collective-permute-start(bf16[256,256]{1,0:T(8,128)(2,1)} %keys_in.1), channel_id=1, source_target_pairs={{0,4},{1,5},{2,6},{3,7},{4,0},{5,1},{6,2},{7,3},{8,12},{9,13},{10,... | collective-permute-start | bytes 393224 | tf_op jit(solution)/shard_map/ppermute | solution.py:46
  1.9 7.5 %collective-permute-start.3 = (bf16[256,256]{1,0:T(8,128)(2,1)}, bf16[256,256]{1,0:T(8,128)(2,1)S(1)}, u32[]{:S(2)}, u32[]{:S(2)}) collective-permute-start(bf16[256,256]{1,0:T(8,128)(2,1)} %values_in.1), channel_id=1, source_target_pairs={{0,8},{1,9},{2,10},{3,11},{4,12},{5,13},{6,14},{7,15},{8,16},{9,17... | collective-permute-start | bytes 393224 | tf_op jit(solution)/shard_map/ppermute | solution.py:46
  3.4 6.7 %collective-permute-start.1 = (bf16[256,256]{1,0:T(8,128)(2,1)}, bf16[256,256]{1,0:T(8,128)(2,1)S(1)}, u32[]{:S(2)}, u32[]{:S(2)}) collective-permute-start(bf16[256,256]{1,0:T(8,128)(2,1)} %values_in.1), channel_id=1, source_target_pairs={{0,4},{1,5},{2,6},{3,7},{4,0},{5,1},{6,2},{7,3},{8,12},{9,13},{10,... | collective-permute-start | bytes 393224 | tf_op jit(solution)/shard_map/ppermute | solution.py:46
  6.6 6.0 %collective-permute-start.4 = (bf16[256,256]{1,0:T(8,128)(2,1)S(1)}, bf16[256,256]{1,0:T(8,128)(2,1)S(1)}, u32[]{:S(2)}, u32[]{:S(2)}) collective-permute-start(bf16[256,256]{1,0:T(8,128)(2,1)S(1)} %collective-permute-done.2.refs_5_), channel_id=1, source_target_pairs={{0,1},{1,0},{2,3},{3,2},{4,5},{5,4},{6,7},{7,6},{8,16},{9,17},{10,... | collective-permute-start | bytes 393224 | tf_op jit(solution)/shard_map/ppermute | solution.py:46
  6.6 6.2 %collective-permute-start.6 = (bf16[256,256]{1,0:T(8,128)(2,1)S(1)}, bf16[256,256]{1,0:T(8,128)(2,1)S(1)}, u32[]{:S(2)}, u32[]{:S(2)}) collective-permute-start(bf16[256,256]{1,0:T(8,128)(2,1)S(1)} %collective-permute-done.2.refs_5_), channel_id=1, source_target_pairs={{0,1},{1,0},{2,3},{3,2},{4,5},{5,4},{6,7},{7,6},{8,12},{9,13},{10,... | collective-permute-start | bytes 393224 | tf_op jit(solution)/shard_map/ppermute | solution.py:46
  9.4 6.1 %collective-permute-start.5 = (bf16[256,256]{1,0:T(8,128)(2,1)S(1)}, bf16[256,256]{1,0:T(8,128)(2,1)S(1)}, u32[]{:S(2)}, u32[]{:S(2)}) collective-permute-start(bf16[256,256]{1,0:T(8,128)(2,1)S(1)} %collective-permute-done.3.refs_6_), channel_id=1, source_target_pairs={{0,1},{1,0},{2,3},{3,2},{4,5},{5,4},{6,7},{7,6},{8,16},{9,17},{10,... | collective-permute-start | bytes 393224 | tf_op jit(solution)/shard_map/ppermute | solution.py:46
  10.2 8.9 %collective-permute-start.7 = (bf16[256,256]{1,0:T(8,128)(2,1)S(1)}, bf16[256,256]{1,0:T(8,128)(2,1)S(1)}, u32[]{:S(2)}, u32[]{:S(2)}) collective-permute-start(bf16[256,256]{1,0:T(8,128)(2,1)S(1)} %collective-permute-done.3.refs_6_), channel_id=1, source_target_pairs={{0,1},{1,0},{2,3},{3,2},{4,5},{5,4},{6,7},{7,6},{8,12},{9,13},{10,... | collective-permute-start | bytes 393224 | tf_op jit(solution)/shard_map/ppermute | solution.py:46
  12.8 6.9 %collective-permute-start.8 = (bf16[256,256]{1,0:T(8,128)(2,1)S(1)}, bf16[256,256]{1,0:T(8,128)(2,1)S(1)}, u32[]{:S(2)}, u32[]{:S(2)}) collective-permute-start(bf16[256,256]{1,0:T(8,128)(2,1)S(1)} %collective-permute-done.6.refs_3_), channel_id=1, source_target_pairs={{0,1},{1,0},{2,3},{3,2},{4,5},{5,4},{6,7},{7,6},{8,16},{9,17},{10,... | collective-permute-start | bytes 393224 | tf_op jit(solution)/shard_map/ppermute | solution.py:46
  15.5 5.0 %collective-permute-start.9 = (bf16[256,256]{1,0:T(8,128)(2,1)S(1)}, bf16[256,256]{1,0:T(8,128)(2,1)S(1)}, u32[]{:S(2)}, u32[]{:S(2)}) collective-permute-start(bf16[256,256]{1,0:T(8,128)(2,1)S(1)} %collective-permute-done.5.refs_8_), channel_id=1, source_target_pairs={{0,1},{1,0},{2,3},{3,2},{4,5},{5,4},{6,7},{7,6},{8,9},{9,8},{10,11... | collective-permute-start | bytes 393224 | tf_op jit(solution)/shard_map/ppermute | solution.py:46
  21.6 1.6 %collective-permute-start.10 = (bf16[64,2176]{1,0:T(8,128)(2,1)S(1)}, bf16[64,2176]{1,0:T(8,128)(2,1)S(1)}, u32[]{:S(2)}, u32[]{:S(2)}) collective-permute-start(bf16[64,2176]{1,0:T(8,128)(2,1)S(1)} %get-tuple-element.63), channel_id=1, source_target_pairs={{0,1},{1,0},{2,3},{3,2},{4,5},{5,4},{6,7},{7,6},{8,9},{9,8},{10,11... | collective-permute-start | bytes 835592 | tf_op jit(solution)/shard_map/ppermute | solution.py:22
  23.3 1.8 %collective-permute-start.11 = (bf16[64,3200]{1,0:T(8,128)(2,1)S(1)}, bf16[64,3200]{1,0:T(8,128)(2,1)S(1)}, u32[]{:S(2)}, u32[]{:S(2)}) collective-permute-start(bf16[64,3200]{1,0:T(8,128)(2,1)S(1)} %get-tuple-element.68), channel_id=1, source_target_pairs={{0,1},{1,0},{2,3},{3,2},{4,5},{5,4},{6,7},{7,6},{8,9},{9,8},{10,11... | collective-permute-start | bytes 1228808 | tf_op jit(solution)/shard_map/ppermute | solution.py:22
  23.5 8.1 %collective-permute-start.15 = (bf16[64,1664]{1,0:T(8,128)(2,1)S(1)}, bf16[64,1664]{1,0:T(8,128)(2,1)S(1)}, u32[]{:S(2)}, u32[]{:S(2)}) collective-permute-start(bf16[64,1664]{1,0:T(8,128)(2,1)S(1)} %get-tuple-element.64), channel_id=1, source_target_pairs={{0,2},{1,3},{2,0},{3,1},{4,6},{5,7},{6,4},{7,5},{8,10},{9,11},{10,... | collective-permute-start | bytes 638984 | tf_op jit(solution)/shard_map/ppermute | solution.py:22
  25.2 14.6 %collective-permute-start.12 = (bf16[64,3200]{1,0:T(8,128)(2,1)S(1)}, bf16[64,3200]{1,0:T(8,128)(2,1)S(1)}, u32[]{:S(2)}, u32[]{:S(2)}) collective-permute-start(bf16[64,3200]{1,0:T(8,128)(2,1)S(1)} %add_up.3), channel_id=1, source_target_pairs={{0,2},{1,3},{2,0},{3,1},{4,6},{5,7},{6,4},{7,5},{8,10},{9,11},{10,... | collective-permute-start | bytes 1228808 | tf_op jit(solution)/shard_map/ppermute | solution.py:22
  27.6 9.2 %collective-permute-start.18 = (bf16[64,2688]{1,0:T(8,128)(2,1)S(1)}, bf16[64,2688]{1,0:T(8,128)(2,1)S(1)}, u32[]{:S(2)}, u32[]{:S(2)}) collective-permute-start(bf16[64,2688]{1,0:T(8,128)(2,1)S(1)} %get-tuple-element.73), channel_id=1, source_target_pairs={{0,1},{1,0},{2,3},{3,2},{4,5},{5,4},{6,7},{7,6},{8,9},{9,8},{10,11... | collective-permute-start | bytes 1032200 | tf_op jit(solution)/shard_map/ppermute | solution.py:22
  27.7 9.1 %collective-permute-start.19 = (bf16[64,2688]{1,0:T(8,128)(2,1)S(1)}, bf16[64,2688]{1,0:T(8,128)(2,1)S(1)}, u32[]{:S(2)}, u32[]{:S(2)}) collective-permute-start(bf16[64,2688]{1,0:T(8,128)(2,1)S(1)} %get-tuple-element.74), channel_id=1, source_target_pairs={{0,1},{1,0},{2,3},{3,2},{4,5},{5,4},{6,7},{7,6},{8,9},{9,8},{10,11... | collective-permute-start | bytes 1032200 | tf_op jit(solution)/shard_map/ppermute | solution.py:22
  28.2 4.3 %collective-permute-start.14 = (bf16[64,512]{1,0:T(8,128)(2,1)S(1)}, bf16[64,512]{1,0:T(8,128)(2,1)S(1)}, u32[]{:S(2)}, u32[]{:S(2)}) collective-permute-start(bf16[64,512]{1,0:T(8,128)(2,1)S(1)} %get-tuple-element.71), channel_id=1, source_target_pairs={{0,1},{1,0},{2,3},{3,2},{4,5},{5,4},{6,7},{7,6},{8,9},{9,8},{10,11... | collective-permute-start | bytes 196616 | tf_op jit(solution)/shard_map/ppermute | solution.py:46
  32.5 1.3 %collective-permute-start.16 = (bf16[64,512]{1,0:T(8,128)(2,1)S(1)}, bf16[64,512]{1,0:T(8,128)(2,1)S(1)}, u32[]{:S(2)}, u32[]{:S(2)}) collective-permute-start(bf16[64,512]{1,0:T(8,128)(2,1)S(1)} %collective-permute-done.14), channel_id=1, source_target_pairs={{0,1},{1,0},{2,3},{3,2},{4,5},{5,4},{6,7},{7,6},{8,9},{9,8},{10,11... | collective-permute-start | bytes 196616 | tf_op jit(solution)/shard_map/ppermute | solution.py:46
  32.5 5.1 %collective-permute-start.13 = (bf16[64,512]{1,0:T(8,128)(2,1)S(1)}, bf16[64,512]{1,0:T(8,128)(2,1)S(1)}, u32[]{:S(2)}, u32[]{:S(2)}) collective-permute-start(bf16[64,512]{1,0:T(8,128)(2,1)S(1)} %get-tuple-element.71), channel_id=1, source_target_pairs={{0,2},{1,3},{2,0},{3,1},{4,6},{5,7},{6,4},{7,5},{8,10},{9,11},{10,... | collective-permute-start | bytes 196616 | tf_op jit(solution)/shard_map/ppermute | solution.py:46
  33.7 5.3 %collective-permute-start.17 = (bf16[64,512]{1,0:T(8,128)(2,1)S(1)}, bf16[64,512]{1,0:T(8,128)(2,1)S(1)}, u32[]{:S(2)}, u32[]{:S(2)}) collective-permute-start(bf16[64,512]{1,0:T(8,128)(2,1)S(1)} %collective-permute-done.16), channel_id=1, source_target_pairs={{0,1},{1,0},{2,3},{3,2},{4,5},{5,4},{6,7},{7,6},{8,9},{9,8},{10,11... | collective-permute-start | bytes 196616 | tf_op jit(solution)/shard_map/ppermute | solution.py:46

commit v9 on v8

--- a/solution.py
+++ b/solution.py
@@ -518,19 +518,19 @@
         )
         state = attend_middle(fetched, state, [swap_two], (4,))
         chunks = [swap_four]
-        far, near, mine, send = attend_last(fetched, weight, state, chunks, (5,), (0, cuts[2]))
+        far, near, mine, send = attend_last(fetched, weight, state, chunks, (5,), (0, cuts[1]))
     else:
         weight = out_weight
         attended = ring_attention(queries, keys, values, doc_ids, n_ctx, position)
         far, near = part_rows(attended, place)
-        mine, send = project(far, weight, (0, cuts[2]))
+        mine, send = project(far, weight, (0, cuts[1]))
     theirs = hop(send, "head", other_core)
-    later_mine, later_send = project(far, weight, (cuts[2], columns))
-    first_sum, relay_sum = add_up(mine, theirs, [cuts[1], cuts[2] - cuts[1]])
+    later_mine, later_send = project(far, weight, (cuts[1], columns))
+    (first_sum,) = add_up(mine, theirs, [cuts[1]])
     first_part = hop(first_sum, "head", other_chip)
-    later_theirs = hop(after(later_send, relay_sum), "head", other_core)
+    later_theirs = hop(after(later_send, first_sum), "head", other_core)
     later_mine = after(later_mine, first_sum)
-    (later_sum,) = add_up(later_mine, later_theirs, [columns - cuts[2]])
+    relay_sum, later_sum = add_up(later_mine, later_theirs, [cuts[2] - cuts[1], columns - cuts[2]])
     later_part = hop(later_sum, "head", other_chip)
     mine, *sends = project(after(near, later_sum), weight, (0, columns), 2)
     theirs = [hop(send, "head", other_core) for send in sends]

time: 40.9 us -> 40.7 us (level)
  no operation moved by 1% of the time
where the time goes in v9:
time: 40.7 us; the launch traced here: 40.6 us
  starting transfers between devices  17.9 us (44%)
  waiting for transfers between devices  13.6 us (33%)
  Pallas kernels  8.95 us (22%)
    ppermute x14, starting transfers between devices, move(): return lax.ppermute(block, ('ctx', 'head'), pairs)  14 us
    ppermute x14, waiting for transfers between devices, move(): return lax.ppermute(block, ('ctx', 'head'), pairs)  8.73 us
    ppermute x6, waiting for transfers between devices, hop(): return lax.ppermute(block, axis, pairs)  4.91 us
    ppermute x6, starting transfers between devices, hop(): return lax.ppermute(block, axis, pairs)  3.82 us
    pallas_call x1, Pallas kernels, attend_next(): pl.pallas_call(functools.partial(next_kernel, numbers, split), out_shape=...  2.06 us
    pallas_call x1, Pallas kernels, attend_first(): pl.pallas_call(functools.partial(first_kernel, split), out_shape=state_sh...  1.77 us
    pallas_call x2, Pallas kernels, combine(): pl.pallas_call(kernel, out_shape=jax.ShapeDtypeStruct(mine.shape, jnp.bfl...  1.66 us
    pallas_call x2, Pallas kernels, project(): pl.pallas_call(functools.partial(project_kernel, columns), out_shape=proj...  1.61 us
  transfers between devices with their start and end apart: 20, of which 13 were waited for; matrix products, arithmetic and copies ran while one was open for 0% of the time, Pallas kernels for 17%

profile of v9, /device:TPU:16, one launch (start us, length us, event | category | flops | bytes accessed | tf_op | source)
XLA Modules:
  0.0 40.6 jit_solution(8720900369435243860)
XLA Ops:
  0.0 1.9 %collective-permute-start = (bf16[256,256]{1,0:T(8,128)(2,1)}, bf16[256,256]{1,0:T(8,128)(2,1)S(1)}, u32[]{:S(2)}, u32[]{:S(2)}) collective-permute-start(bf16[256,256]{1,0:T(8,128)(2,1)} %keys_in.1), channel_id=1, source_target_pairs={{0,4},{1,5},{2,6},{3,7},{4,0},{5,1},{6,2},{7,3},{8,12},{9,13},{10,... | collective-permute-start | bytes 393224 | tf_op jit(solution)/shard_map/ppermute | solution.py:46
  1.9 1.6 %collective-permute-start.3 = (bf16[256,256]{1,0:T(8,128)(2,1)}, bf16[256,256]{1,0:T(8,128)(2,1)S(1)}, u32[]{:S(2)}, u32[]{:S(2)}) collective-permute-start(bf16[256,256]{1,0:T(8,128)(2,1)} %values_in.1), channel_id=1, source_target_pairs={{0,8},{1,9},{2,10},{3,11},{4,12},{5,13},{6,14},{7,15},{8,16},{9,17... | collective-permute-start | bytes 393224 | tf_op jit(solution)/shard_map/ppermute | solution.py:46
  3.4 0.5 %collective-permute-start.1 = (bf16[256,256]{1,0:T(8,128)(2,1)}, bf16[256,256]{1,0:T(8,128)(2,1)S(1)}, u32[]{:S(2)}, u32[]{:S(2)}) collective-permute-start(bf16[256,256]{1,0:T(8,128)(2,1)} %values_in.1), channel_id=1, source_target_pairs={{0,4},{1,5},{2,6},{3,7},{4,0},{5,1},{6,2},{7,3},{8,12},{9,13},{10,... | collective-permute-start | bytes 393224 | tf_op jit(solution)/shard_map/ppermute | solution.py:46
  3.9 1.8 %attend_first.1 = (f32[1024,128]{1,0:T(8,128)S(1)}, f32[1024,128]{1,0:T(8,128)S(1)}, f32[1024,128]{1,0:T(8,128)S(1)}, bf16[256,512]{1,0:T(8,128)(2,1)S(1)}, f32[...) custom-call(s32[16]{0:T(128)} %docs_in.1, bf16[256,512]{1,0:T(8,128)(2,1)} %queries_in.1, bf16[256,256]{1,0:T(8,128)(2,1)} %keys_in.1, ...), custom_call_target="tpu_custom_call" | custom-call | flops 134217728 | tf_op jit(solution)/shard_map/attend_first/pallas_call | solution.py:209
  5.7 0.9 %collective-permute-done.2.refs_5_ = bf16[256,256]{1,0:T(8,128)(2,1)S(1)} collective-permute-done((bf16[256,256]{1,0:T(8,128)(2,1)}, bf16[256,256]{1,0:T(8,128)(2,1)S(1)}, u32[]{:S(2)}, u32[]{:S(2)}) %collective-permute-start.2) | collective-permute-done | bytes 131104 | tf_op jit(solution)/shard_map/ppermute | solution.py:46
  6.6 2.0 %collective-permute-start.6 = (bf16[256,256]{1,0:T(8,128)(2,1)S(1)}, bf16[256,256]{1,0:T(8,128)(2,1)S(1)}, u32[]{:S(2)}, u32[]{:S(2)}) collective-permute-start(bf16[256,256]{1,0:T(8,128)(2,1)S(1)} %collective-permute-done.2.refs_5_), channel_id=1, source_target_pairs={{0,1},{1,0},{2,3},{3,2},{4,5},{5,4},{6,7},{7,6},{8,12},{9,13},{10,... | collective-permute-start | bytes 393224 | tf_op jit(solution)/shard_map/ppermute | solution.py:46
  8.6 0.8 %collective-permute-done.3.refs_6_ = bf16[256,256]{1,0:T(8,128)(2,1)S(1)} collective-permute-done((bf16[256,256]{1,0:T(8,128)(2,1)}, bf16[256,256]{1,0:T(8,128)(2,1)S(1)}, u32[]{:S(2)}, u32[]{:S(2)}) %collective-permute-start.3) | collective-permute-done | bytes 131104 | tf_op jit(solution)/shard_map/ppermute | solution.py:46
  9.4 0.7 %collective-permute-start.5 = (bf16[256,256]{1,0:T(8,128)(2,1)S(1)}, bf16[256,256]{1,0:T(8,128)(2,1)S(1)}, u32[]{:S(2)}, u32[]{:S(2)}) collective-permute-start(bf16[256,256]{1,0:T(8,128)(2,1)S(1)} %collective-permute-done.3.refs_6_), channel_id=1, source_target_pairs={{0,1},{1,0},{2,3},{3,2},{4,5},{5,4},{6,7},{7,6},{8,16},{9,17},{10,... | collective-permute-start | bytes 393224 | tf_op jit(solution)/shard_map/ppermute | solution.py:46
  10.2 0.8 %collective-permute-start.7 = (bf16[256,256]{1,0:T(8,128)(2,1)S(1)}, bf16[256,256]{1,0:T(8,128)(2,1)S(1)}, u32[]{:S(2)}, u32[]{:S(2)}) collective-permute-start(bf16[256,256]{1,0:T(8,128)(2,1)S(1)} %collective-permute-done.3.refs_6_), channel_id=1, source_target_pairs={{0,1},{1,0},{2,3},{3,2},{4,5},{5,4},{6,7},{7,6},{8,12},{9,13},{10,... | collective-permute-start | bytes 393224 | tf_op jit(solution)/shard_map/ppermute | solution.py:46
  10.9 1.7 %collective-permute-done.4.refs_7_ = bf16[256,256]{1,0:T(8,128)(2,1)S(1)} collective-permute-done((bf16[256,256]{1,0:T(8,128)(2,1)S(1)}, bf16[256,256]{1,0:T(8,128)(2,1)S(1)}, u32[]{:S(2)}, u32[]{:S(2)}) %collective-permute-start.4) | collective-permute-done | bytes 131104 | tf_op jit(solution)/shard_map/ppermute | solution.py:46
  12.8 1.5 %collective-permute-start.8 = (bf16[256,256]{1,0:T(8,128)(2,1)S(1)}, bf16[256,256]{1,0:T(8,128)(2,1)S(1)}, u32[]{:S(2)}, u32[]{:S(2)}) collective-permute-start(bf16[256,256]{1,0:T(8,128)(2,1)S(1)} %collective-permute-done.6.refs_3_), channel_id=1, source_target_pairs={{0,1},{1,0},{2,3},{3,2},{4,5},{5,4},{6,7},{7,6},{8,16},{9,17},{10,... | collective-permute-start | bytes 393224 | tf_op jit(solution)/shard_map/ppermute | solution.py:46
  14.4 1.1 %collective-permute-done.5.refs_8_ = bf16[256,256]{1,0:T(8,128)(2,1)S(1)} collective-permute-done((bf16[256,256]{1,0:T(8,128)(2,1)S(1)}, bf16[256,256]{1,0:T(8,128)(2,1)S(1)}, u32[]{:S(2)}, u32[]{:S(2)}) %collective-permute-start.5) | collective-permute-done | bytes 131104 | tf_op jit(solution)/shard_map/ppermute | solution.py:46
  15.5 1.4 %collective-permute-start.9 = (bf16[256,256]{1,0:T(8,128)(2,1)S(1)}, bf16[256,256]{1,0:T(8,128)(2,1)S(1)}, u32[]{:S(2)}, u32[]{:S(2)}) collective-permute-start(bf16[256,256]{1,0:T(8,128)(2,1)S(1)} %collective-permute-done.5.refs_8_), channel_id=1, source_target_pairs={{0,1},{1,0},{2,3},{3,2},{4,5},{5,4},{6,7},{7,6},{8,9},{9,8},{10,11... | collective-permute-start | bytes 393224 | tf_op jit(solution)/shard_map/ppermute | solution.py:46
  17.0 2.1 %attend_next.1 = (f32[1024,128]{1,0:T(8,128)S(1)}, f32[1024,128]{1,0:T(8,128)S(1)}, f32[1024,128]{1,0:T(8,128)S(1)}, bf16[512,5376]{1,0:T(8,128)(2,1)S(1)}) custom-call(bf16[256,512]{1,0:T(8,128)(2,1)S(1)} %get-tuple-element.40.queries, f32[16,256]{1,0:T(8,128)S(1)} %get-tuple-element.41.open_beside, ...), custom_call_target="tpu_custom_call", output_to_operand_aliasing={{3}: (3, {})} | custom-call | flops 402653184 | bytes 5505024 | tf_op jit(solution)/shard_map/attend_next/pallas_call | solution.py:232
  19.0 0.6 %attend_middle.1 = (f32[1024,128]{1,0:T(8,128)S(1)}, f32[1024,128]{1,0:T(8,128)S(1)}, f32[1024,128]{1,0:T(8,128)S(1)}) custom-call(bf16[256,512]{1,0:T(8,128)(2,1)S(1)} %get-tuple-element.40.queries, f32[1024,128]{1,0:T(8,128)S(1)} %get-tuple-element.49.refs_0_, f32[1024,128]{1,0:T(8,128)S(1)} %get-tuple-element.50.refs_1_, ...), custom_call_target="tpu_custom_call" | custom-call | flops 134217728 | tf_op jit(solution)/shard_map/attend_middle/pallas_call | solution.py:258
  19.7 0.8 %collective-permute-done.9.refs_4_ = bf16[256,256]{1,0:T(8,128)(2,1)S(1)} collective-permute-done((bf16[256,256]{1,0:T(8,128)(2,1)S(1)}, bf16[256,256]{1,0:T(8,128)(2,1)S(1)}, u32[]{:S(2)}, u32[]{:S(2)}) %collective-permute-start.9) | collective-permute-done | bytes 131104 | tf_op jit(solution)/shard_map/ppermute | solution.py:46
  20.5 1.1 %attend_last.1 = (bf16[128,512]{1,0:T(8,128)(2,1)S(1)}, bf16[128,512]{1,0:T(8,128)(2,1)S(1)}, f32[64,1664]{1,0:T(8,128)S(1)}, bf16[64,1664]{1,0:T(8,128)(2,1)S(1)}) custom-call(bf16[256,512]{1,0:T(8,128)(2,1)S(1)} %get-tuple-element.40.queries, bf16[512,5376]{1,0:T(8,128)(2,1)S(1)} %get-tuple-element.48.weight, f32[1024,128]{1,0:T(8,128)S(1)} %get-tuple-element.55.refs_0_, ...), custom_call_target="tpu_custom_call" | custom-call | flops 134217728 | tf_op jit(solution)/shard_map/attend_last/pallas_call | solution.py:294
  21.6 0.7 %project.2 = (f32[64,3712]{1,0:T(8,128)S(1)}, bf16[64,3712]{1,0:T(8,128)(2,1)S(1)}) custom-call(bf16[128,512]{1,0:T(8,128)(2,1)S(1)} %get-tuple-element.60.rows, bf16[512,5376]{1,0:T(8,128)(2,1)S(1)} %get-tuple-element.48.weight), custom_call_target="tpu_custom_call" | custom-call | flops 486539264 | tf_op jit(solution)/shard_map/project/pallas_call | solution.py:329
  22.3 0.8 %collective-permute-done.10.theirs = bf16[64,1664]{1,0:T(8,128)(2,1)S(1)} collective-permute-done((bf16[64,1664]{1,0:T(8,128)(2,1)S(1)}, bf16[64,1664]{1,0:T(8,128)(2,1)S(1)}, u32[]{:S(2)}, u32[]{:S(2)}) %collective-permute-start.10) | collective-permute-done | bytes 213024 | tf_op jit(solution)/shard_map/ppermute | solution.py:22
  23.3 1.5 %collective-permute-start.15 = (bf16[64,1664]{1,0:T(8,128)(2,1)S(1)}, bf16[64,1664]{1,0:T(8,128)(2,1)S(1)}, u32[]{:S(2)}, u32[]{:S(2)}) collective-permute-start(bf16[64,1664]{1,0:T(8,128)(2,1)S(1)} %add_up.2), channel_id=1, source_target_pairs={{0,2},{1,3},{2,0},{3,1},{4,6},{5,7},{6,4},{7,5},{8,10},{9,11},{10,... | collective-permute-start | bytes 638984 | tf_op jit(solution)/shard_map/ppermute | solution.py:22
  25.1 1.5 %collective-permute-start.12 = (bf16[64,3200]{1,0:T(8,128)(2,1)S(1)}, bf16[64,3200]{1,0:T(8,128)(2,1)S(1)}, u32[]{:S(2)}, u32[]{:S(2)}) collective-permute-start(bf16[64,3200]{1,0:T(8,128)(2,1)S(1)} %get-tuple-element.67), channel_id=1, source_target_pairs={{0,2},{1,3},{2,0},{3,1},{4,6},{5,7},{6,4},{7,5},{8,10},{9,11},{10,... | collective-permute-start | bytes 1228808 | tf_op jit(solution)/shard_map/ppermute | solution.py:22
  26.6 0.9 %project.3 = (f32[64,5376]{1,0:T(8,128)S(1)}, bf16[64,2688]{1,0:T(8,128)(2,1)S(1)}, bf16[64,2688]{1,0:T(8,128)(2,1)S(1)}) custom-call(bf16[128,512]{1,0:T(8,128)(2,1)S(1)} %get-tuple-element.68.rows, bf16[512,5376]{1,0:T(8,128)(2,1)S(1)} %get-tuple-element.48.weight), custom_call_target="tpu_custom_call" | custom-call | flops 704643072 | tf_op jit(solution)/shard_map/project/pallas_call | solution.py:329
  27.7 0.5 %collective-permute-start.19 = (bf16[64,2688]{1,0:T(8,128)(2,1)S(1)}, bf16[64,2688]{1,0:T(8,128)(2,1)S(1)}, u32[]{:S(2)}, u32[]{:S(2)}) collective-permute-start(bf16[64,2688]{1,0:T(8,128)(2,1)S(1)} %get-tuple-element.74), channel_id=1, source_target_pairs={{0,1},{1,0},{2,3},{3,2},{4,5},{5,4},{6,7},{7,6},{8,9},{9,8},{10,11... | collective-permute-start | bytes 1032200 | tf_op jit(solution)/shard_map/ppermute | solution.py:22
  28.2 3.3 %collective-permute-done.15.refs_1_ = bf16[64,1664]{1,0:T(8,128)(2,1)S(1)} collective-permute-done((bf16[64,1664]{1,0:T(8,128)(2,1)S(1)}, bf16[64,1664]{1,0:T(8,128)(2,1)S(1)}, u32[]{:S(2)}, u32[]{:S(2)}) %collective-permute-start.15) | collective-permute-done | bytes 213024 | tf_op jit(solution)/shard_map/ppermute | solution.py:22
  31.4 1.0 %collective-permute-done.14 = bf16[64,512]{1,0:T(8,128)(2,1)S(1)} collective-permute-done((bf16[64,512]{1,0:T(8,128)(2,1)S(1)}, bf16[64,512]{1,0:T(8,128)(2,1)S(1)}, u32[]{:S(2)}, u32[]{:S(2)}) %collective-permute-start.14) | collective-permute-done | bytes 65568 | tf_op jit(solution)/shard_map/ppermute | solution.py:46
  32.4 0.5 %collective-permute-start.13 = (bf16[64,512]{1,0:T(8,128)(2,1)S(1)}, bf16[64,512]{1,0:T(8,128)(2,1)S(1)}, u32[]{:S(2)}, u32[]{:S(2)}) collective-permute-start(bf16[64,512]{1,0:T(8,128)(2,1)S(1)} %get-tuple-element.71), channel_id=1, source_target_pairs={{0,2},{1,3},{2,0},{3,1},{4,6},{5,7},{6,4},{7,5},{8,10},{9,11},{10,... | collective-permute-start | bytes 196616 | tf_op jit(solution)/shard_map/ppermute | solution.py:46
  32.9 0.7 %collective-permute-done.16 = bf16[64,512]{1,0:T(8,128)(2,1)S(1)} collective-permute-done((bf16[64,512]{1,0:T(8,128)(2,1)S(1)}, bf16[64,512]{1,0:T(8,128)(2,1)S(1)}, u32[]{:S(2)}, u32[]{:S(2)}) %collective-permute-start.16) | collective-permute-done | bytes 65568 | tf_op jit(solution)/shard_map/ppermute | solution.py:46
  33.7 3.1 %collective-permute-start.17 = (bf16[64,512]{1,0:T(8,128)(2,1)S(1)}, bf16[64,512]{1,0:T(8,128)(2,1)S(1)}, u32[]{:S(2)}, u32[]{:S(2)}) collective-permute-start(bf16[64,512]{1,0:T(8,128)(2,1)S(1)} %collective-permute-done.16), channel_id=1, source_target_pairs={{0,1},{1,0},{2,3},{3,2},{4,5},{5,4},{6,7},{7,6},{8,9},{9,8},{10,11... | collective-permute-start | bytes 196616 | tf_op jit(solution)/shard_map/ppermute | solution.py:46
  36.8 0.8 %combine.2.refs_6_ = bf16[64,5376]{1,0:T(8,128)(2,1)} custom-call(f32[64,5376]{1,0:T(8,128)S(1)} %get-tuple-element.69.refs_0_, bf16[64,1664]{1,0:T(8,128)(2,1)S(1)} %collective-permute-done.15.refs_1_, bf16[64,2688]{1,0:T(8,128)(2,1)S(1)} %collective-permute-done.18.refs_2_.refs_4_, bf16[64,2688]{1,0:T(8,128)(2,1)S(1)} %collective-permute-done.19.refs_3_.refs_5_), custom_call_target="tpu_custom_call" | custom-call | tf_op jit(solution)/shard_map/combine/pallas_call | solution.py:398
  37.6 1.5 %collective-permute-done.17.refs_3_ = bf16[64,512]{1,0:T(8,128)(2,1)S(1)} collective-permute-done((bf16[64,512]{1,0:T(8,128)(2,1)S(1)}, bf16[64,512]{1,0:T(8,128)(2,1)S(1)}, u32[]{:S(2)}, u32[]{:S(2)}) %collective-permute-start.17) | collective-permute-done | bytes 65568 | tf_op jit(solution)/shard_map/ppermute | solution.py:46
  39.0 0.6 %collective-permute-done.12.refs_1_ = bf16[64,3200]{1,0:T(8,128)(2,1)S(1)} collective-permute-done((bf16[64,3200]{1,0:T(8,128)(2,1)S(1)}, bf16[64,3200]{1,0:T(8,128)(2,1)S(1)}, u32[]{:S(2)}, u32[]{:S(2)}) %collective-permute-start.12) | collective-permute-done | bytes 409632 | tf_op jit(solution)/shard_map/ppermute | solution.py:22
  39.6 0.9 %combine.3 = bf16[64,5376]{1,0:T(8,128)(2,1)} custom-call(f32[64,5376]{1,0:T(8,128)S(1)} %get-tuple-element.69.refs_0_, bf16[64,3200]{1,0:T(8,128)(2,1)S(1)} %collective-permute-done.12.refs_1_, bf16[64,512]{1,0:T(8,128)(2,1)S(1)} %collective-permute-done.13.refs_2_, ...), custom_call_target="tpu_custom_call", output_to_operand_aliasing={{}: (6, {})} | custom-call | tf_op jit(solution)/shard_map/combine/pallas_call | solution.py:398
  (18 shorter events, 0.9 us)
Async XLA Ops:
  0.0 6.6 %collective-permute-start.2 = (bf16[256,256]{1,0:T(8,128)(2,1)}, bf16[256,256]{1,0:T(8,128)(2,1)S(1)}, u32[]{:S(2)}, u32[]{:S(2)}) collective-permute-start(bf16[256,256]{1,0:T(8,128)(2,1)} %keys_in.1), channel_id=1, source_target_pairs={{0,8},{1,9},{2,10},{3,11},{4,12},{5,13},{6,14},{7,15},{8,16},{9,17... | collective-permute-start | bytes 393224 | tf_op jit(solution)/shard_map/ppermute | solution.py:46
  0.0 6.6 %collective-permute-start = (bf16[256,256]{1,0:T(8,128)(2,1)}, bf16[256,256]{1,0:T(8,128)(2,1)S(1)}, u32[]{:S(2)}, u32[]{:S(2)}) collective-permute-start(bf16[256,256]{1,0:T(8,128)(2,1)} %keys_in.1), channel_id=1, source_target_pairs={{0,4},{1,5},{2,6},{3,7},{4,0},{5,1},{6,2},{7,3},{8,12},{9,13},{10,... | collective-permute-start | bytes 393224 | tf_op jit(solution)/shard_map/ppermute | solution.py:46
  1.9 7.5 %collective-permute-start.3 = (bf16[256,256]{1,0:T(8,128)(2,1)}, bf16[256,256]{1,0:T(8,128)(2,1)S(1)}, u32[]{:S(2)}, u32[]{:S(2)}) collective-permute-start(bf16[256,256]{1,0:T(8,128)(2,1)} %values_in.1), channel_id=1, source_target_pairs={{0,8},{1,9},{2,10},{3,11},{4,12},{5,13},{6,14},{7,15},{8,16},{9,17... | collective-permute-start | bytes 393224 | tf_op jit(solution)/shard_map/ppermute | solution.py:46
  3.4 6.7 %collective-permute-start.1 = (bf16[256,256]{1,0:T(8,128)(2,1)}, bf16[256,256]{1,0:T(8,128)(2,1)S(1)}, u32[]{:S(2)}, u32[]{:S(2)}) collective-permute-start(bf16[256,256]{1,0:T(8,128)(2,1)} %values_in.1), channel_id=1, source_target_pairs={{0,4},{1,5},{2,6},{3,7},{4,0},{5,1},{6,2},{7,3},{8,12},{9,13},{10,... | collective-permute-start | bytes 393224 | tf_op jit(solution)/shard_map/ppermute | solution.py:46
  6.6 6.0 %collective-permute-start.4 = (bf16[256,256]{1,0:T(8,128)(2,1)S(1)}, bf16[256,256]{1,0:T(8,128)(2,1)S(1)}, u32[]{:S(2)}, u32[]{:S(2)}) collective-permute-start(bf16[256,256]{1,0:T(8,128)(2,1)S(1)} %collective-permute-done.2.refs_5_), channel_id=1, source_target_pairs={{0,1},{1,0},{2,3},{3,2},{4,5},{5,4},{6,7},{7,6},{8,16},{9,17},{10,... | collective-permute-start | bytes 393224 | tf_op jit(solution)/shard_map/ppermute | solution.py:46
  6.6 6.2 %collective-permute-start.6 = (bf16[256,256]{1,0:T(8,128)(2,1)S(1)}, bf16[256,256]{1,0:T(8,128)(2,1)S(1)}, u32[]{:S(2)}, u32[]{:S(2)}) collective-permute-start(bf16[256,256]{1,0:T(8,128)(2,1)S(1)} %collective-permute-done.2.refs_5_), channel_id=1, source_target_pairs={{0,1},{1,0},{2,3},{3,2},{4,5},{5,4},{6,7},{7,6},{8,12},{9,13},{10,... | collective-permute-start | bytes 393224 | tf_op jit(solution)/shard_map/ppermute | solution.py:46
  9.4 6.1 %collective-permute-start.5 = (bf16[256,256]{1,0:T(8,128)(2,1)S(1)}, bf16[256,256]{1,0:T(8,128)(2,1)S(1)}, u32[]{:S(2)}, u32[]{:S(2)}) collective-permute-start(bf16[256,256]{1,0:T(8,128)(2,1)S(1)} %collective-permute-done.3.refs_6_), channel_id=1, source_target_pairs={{0,1},{1,0},{2,3},{3,2},{4,5},{5,4},{6,7},{7,6},{8,16},{9,17},{10,... | collective-permute-start | bytes 393224 | tf_op jit(solution)/shard_map/ppermute | solution.py:46
  10.2 8.9 %collective-permute-start.7 = (bf16[256,256]{1,0:T(8,128)(2,1)S(1)}, bf16[256,256]{1,0:T(8,128)(2,1)S(1)}, u32[]{:S(2)}, u32[]{:S(2)}) collective-permute-start(bf16[256,256]{1,0:T(8,128)(2,1)S(1)} %collective-permute-done.3.refs_6_), channel_id=1, source_target_pairs={{0,1},{1,0},{2,3},{3,2},{4,5},{5,4},{6,7},{7,6},{8,12},{9,13},{10,... | collective-permute-start | bytes 393224 | tf_op jit(solution)/shard_map/ppermute | solution.py:46
  12.8 6.9 %collective-permute-start.8 = (bf16[256,256]{1,0:T(8,128)(2,1)S(1)}, bf16[256,256]{1,0:T(8,128)(2,1)S(1)}, u32[]{:S(2)}, u32[]{:S(2)}) collective-permute-start(bf16[256,256]{1,0:T(8,128)(2,1)S(1)} %collective-permute-done.6.refs_3_), channel_id=1, source_target_pairs={{0,1},{1,0},{2,3},{3,2},{4,5},{5,4},{6,7},{7,6},{8,16},{9,17},{10,... | collective-permute-start | bytes 393224 | tf_op jit(solution)/shard_map/ppermute | solution.py:46
  15.5 5.0 %collective-permute-start.9 = (bf16[256,256]{1,0:T(8,128)(2,1)S(1)}, bf16[256,256]{1,0:T(8,128)(2,1)S(1)}, u32[]{:S(2)}, u32[]{:S(2)}) collective-permute-start(bf16[256,256]{1,0:T(8,128)(2,1)S(1)} %collective-permute-done.5.refs_8_), channel_id=1, source_target_pairs={{0,1},{1,0},{2,3},{3,2},{4,5},{5,4},{6,7},{7,6},{8,9},{9,8},{10,11... | collective-permute-start | bytes 393224 | tf_op jit(solution)/shard_map/ppermute | solution.py:46
  21.6 1.5 %collective-permute-start.10 = (bf16[64,1664]{1,0:T(8,128)(2,1)S(1)}, bf16[64,1664]{1,0:T(8,128)(2,1)S(1)}, u32[]{:S(2)}, u32[]{:S(2)}) collective-permute-start(bf16[64,1664]{1,0:T(8,128)(2,1)S(1)} %get-tuple-element.63), channel_id=1, source_target_pairs={{0,1},{1,0},{2,3},{3,2},{4,5},{5,4},{6,7},{7,6},{8,9},{9,8},{10,11... | collective-permute-start | bytes 638984 | tf_op jit(solution)/shard_map/ppermute | solution.py:22
  23.1 1.9 %collective-permute-start.11 = (bf16[64,3712]{1,0:T(8,128)(2,1)S(1)}, bf16[64,3712]{1,0:T(8,128)(2,1)S(1)}, u32[]{:S(2)}, u32[]{:S(2)}) collective-permute-start(bf16[64,3712]{1,0:T(8,128)(2,1)S(1)} %get-tuple-element.66), channel_id=1, source_target_pairs={{0,1},{1,0},{2,3},{3,2},{4,5},{5,4},{6,7},{7,6},{8,9},{9,8},{10,11... | collective-permute-start | bytes 1425416 | tf_op jit(solution)/shard_map/ppermute | solution.py:22
  23.3 8.1 %collective-permute-start.15 = (bf16[64,1664]{1,0:T(8,128)(2,1)S(1)}, bf16[64,1664]{1,0:T(8,128)(2,1)S(1)}, u32[]{:S(2)}, u32[]{:S(2)}) collective-permute-start(bf16[64,1664]{1,0:T(8,128)(2,1)S(1)} %add_up.2), channel_id=1, source_target_pairs={{0,2},{1,3},{2,0},{3,1},{4,6},{5,7},{6,4},{7,5},{8,10},{9,11},{10,... | collective-permute-start | bytes 638984 | tf_op jit(solution)/shard_map/ppermute | solution.py:22
  25.1 14.5 %collective-permute-start.12 = (bf16[64,3200]{1,0:T(8,128)(2,1)S(1)}, bf16[64,3200]{1,0:T(8,128)(2,1)S(1)}, u32[]{:S(2)}, u32[]{:S(2)}) collective-permute-start(bf16[64,3200]{1,0:T(8,128)(2,1)S(1)} %get-tuple-element.67), channel_id=1, source_target_pairs={{0,2},{1,3},{2,0},{3,1},{4,6},{5,7},{6,4},{7,5},{8,10},{9,11},{10,... | collective-permute-start | bytes 1228808 | tf_op jit(solution)/shard_map/ppermute | solution.py:22
  27.6 9.2 %collective-permute-start.18 = (bf16[64,2688]{1,0:T(8,128)(2,1)S(1)}, bf16[64,2688]{1,0:T(8,128)(2,1)S(1)}, u32[]{:S(2)}, u32[]{:S(2)}) collective-permute-start(bf16[64,2688]{1,0:T(8,128)(2,1)S(1)} %get-tuple-element.73), channel_id=1, source_target_pairs={{0,1},{1,0},{2,3},{3,2},{4,5},{5,4},{6,7},{7,6},{8,9},{9,8},{10,11... | collective-permute-start | bytes 1032200 | tf_op jit(solution)/shard_map/ppermute | solution.py:22
  27.7 9.1 %collective-permute-start.19 = (bf16[64,2688]{1,0:T(8,128)(2,1)S(1)}, bf16[64,2688]{1,0:T(8,128)(2,1)S(1)}, u32[]{:S(2)}, u32[]{:S(2)}) collective-permute-start(bf16[64,2688]{1,0:T(8,128)(2,1)S(1)} %get-tuple-element.74), channel_id=1, source_target_pairs={{0,1},{1,0},{2,3},{3,2},{4,5},{5,4},{6,7},{7,6},{8,9},{9,8},{10,11... | collective-permute-start | bytes 1032200 | tf_op jit(solution)/shard_map/ppermute | solution.py:22
  28.1 4.3 %collective-permute-start.14 = (bf16[64,512]{1,0:T(8,128)(2,1)S(1)}, bf16[64,512]{1,0:T(8,128)(2,1)S(1)}, u32[]{:S(2)}, u32[]{:S(2)}) collective-permute-start(bf16[64,512]{1,0:T(8,128)(2,1)S(1)} %get-tuple-element.71), channel_id=1, source_target_pairs={{0,1},{1,0},{2,3},{3,2},{4,5},{5,4},{6,7},{7,6},{8,9},{9,8},{10,11... | collective-permute-start | bytes 196616 | tf_op jit(solution)/shard_map/ppermute | solution.py:46
  32.4 1.3 %collective-permute-start.16 = (bf16[64,512]{1,0:T(8,128)(2,1)S(1)}, bf16[64,512]{1,0:T(8,128)(2,1)S(1)}, u32[]{:S(2)}, u32[]{:S(2)}) collective-permute-start(bf16[64,512]{1,0:T(8,128)(2,1)S(1)} %collective-permute-done.14), channel_id=1, source_target_pairs={{0,1},{1,0},{2,3},{3,2},{4,5},{5,4},{6,7},{7,6},{8,9},{9,8},{10,11... | collective-permute-start | bytes 196616 | tf_op jit(solution)/shard_map/ppermute | solution.py:46
  32.4 5.1 %collective-permute-start.13 = (bf16[64,512]{1,0:T(8,128)(2,1)S(1)}, bf16[64,512]{1,0:T(8,128)(2,1)S(1)}, u32[]{:S(2)}, u32[]{:S(2)}) collective-permute-start(bf16[64,512]{1,0:T(8,128)(2,1)S(1)} %get-tuple-element.71), channel_id=1, source_target_pairs={{0,2},{1,3},{2,0},{3,1},{4,6},{5,7},{6,4},{7,5},{8,10},{9,11},{10,... | collective-permute-start | bytes 196616 | tf_op jit(solution)/shard_map/ppermute | solution.py:46
  33.7 5.3 %collective-permute-start.17 = (bf16[64,512]{1,0:T(8,128)(2,1)S(1)}, bf16[64,512]{1,0:T(8,128)(2,1)S(1)}, u32[]{:S(2)}, u32[]{:S(2)}) collective-permute-start(bf16[64,512]{1,0:T(8,128)(2,1)S(1)} %collective-permute-done.16), channel_id=1, source_target_pairs={{0,1},{1,0},{2,3},{3,2},{4,5},{5,4},{6,7},{7,6},{8,9},{9,8},{10,11... | collective-permute-start | bytes 196616 | tf_op jit(solution)/shard_map/ppermute | solution.py:46

commit v10 on v9

--- a/solution.py
+++ b/solution.py
@@ -495,7 +495,7 @@
     other_core = [(i, i ^ 1) for i in range(heads)]
     other_chip = [(i, i ^ 2) for i in range(heads)]
     columns = out_weight.shape[1]
-    relay = columns // 10 // BLOCK * BLOCK
+    relay = columns // 8 // BLOCK * BLOCK
     early_columns = columns * 3 // 7 // BLOCK * BLOCK - BLOCK
     cuts = [0, early_columns - relay, early_columns]
 

time: 40.7 us -> 41.6 us (1.022)
  the two profiles are of different devices: /device:TPU:16 before, /device:TPU:24 now
where the time goes in v10:
time: 41.6 us; the launch traced here: 41.4 us
  starting transfers between devices  18.5 us (44%)
  waiting for transfers between devices  13.8 us (33%)
  Pallas kernels  8.91 us (21%)
    ppermute x14, starting transfers between devices, move(): return lax.ppermute(block, ('ctx', 'head'), pairs)  14 us
    ppermute x14, waiting for transfers between devices, move(): return lax.ppermute(block, ('ctx', 'head'), pairs)  13.4 us
    ppermute x6, starting transfers between devices, hop(): return lax.ppermute(block, axis, pairs)  4.58 us
    pallas_call x1, Pallas kernels, attend_next(): pl.pallas_call(functools.partial(next_kernel, numbers, split), out_shape=...  2.06 us
    pallas_call x1, Pallas kernels, attend_first(): pl.pallas_call(functools.partial(first_kernel, split), out_shape=state_sh...  1.77 us
    pallas_call x2, Pallas kernels, combine(): pl.pallas_call(kernel, out_shape=jax.ShapeDtypeStruct(mine.shape, jnp.bfl...  1.66 us
    pallas_call x2, Pallas kernels, project(): pl.pallas_call(functools.partial(project_kernel, columns), out_shape=proj...  1.6 us
    pallas_call x1, Pallas kernels, attend_last(): pl.pallas_call(functools.partial(last_kernel, numbers, columns), out_shap...  1.05 us
  transfers between devices with their start and end apart: 20, of which 7 were waited for; matrix products, arithmetic and copies ran while one was open for 0% of the time, Pallas kernels for 17%

profile of v10, /device:TPU:24, one launch (start us, length us, event | category | flops | bytes accessed | tf_op | source)
XLA Modules:
  0.0 41.4 jit_solution(11714096201996488187)
XLA Ops:
  0.0 1.5 %collective-permute-start = (bf16[256,256]{1,0:T(8,128)(2,1)}, bf16[256,256]{1,0:T(8,128)(2,1)S(1)}, u32[]{:S(2)}, u32[]{:S(2)}) collective-permute-start(bf16[256,256]{1,0:T(8,128)(2,1)} %keys_in.1), channel_id=1, source_target_pairs={{0,4},{1,5},{2,6},{3,7},{4,0},{5,1},{6,2},{7,3},{8,12},{9,13},{10,... | collective-permute-start | bytes 393224 | tf_op jit(solution)/shard_map/ppermute | solution.py:46
  1.5 0.2 collective-permute-start.3
  1.8 0.5 %collective-permute-start.1 = (bf16[256,256]{1,0:T(8,128)(2,1)}, bf16[256,256]{1,0:T(8,128)(2,1)S(1)}, u32[]{:S(2)}, u32[]{:S(2)}) collective-permute-start(bf16[256,256]{1,0:T(8,128)(2,1)} %values_in.1), channel_id=1, source_target_pairs={{0,4},{1,5},{2,6},{3,7},{4,0},{5,1},{6,2},{7,3},{8,12},{9,13},{10,... | collective-permute-start | bytes 393224 | tf_op jit(solution)/shard_map/ppermute | solution.py:46
  2.3 1.8 %attend_first.1 = (f32[1024,128]{1,0:T(8,128)S(1)}, f32[1024,128]{1,0:T(8,128)S(1)}, f32[1024,128]{1,0:T(8,128)S(1)}, bf16[256,512]{1,0:T(8,128)(2,1)S(1)}, f32[...) custom-call(s32[16]{0:T(128)} %docs_in.1, bf16[256,512]{1,0:T(8,128)(2,1)} %queries_in.1, bf16[256,256]{1,0:T(8,128)(2,1)} %keys_in.1, ...), custom_call_target="tpu_custom_call" | custom-call | flops 134217728 | tf_op jit(solution)/shard_map/attend_first/pallas_call | solution.py:209
  4.0 0.1 collective-permute-start.4
  4.1 2.4 %collective-permute-done.refs_3_ = bf16[256,256]{1,0:T(8,128)(2,1)S(1)} collective-permute-done((bf16[256,256]{1,0:T(8,128)(2,1)}, bf16[256,256]{1,0:T(8,128)(2,1)S(1)}, u32[]{:S(2)}, u32[]{:S(2)}) %collective-permute-start) | collective-permute-done | bytes 131104 | tf_op jit(solution)/shard_map/ppermute | solution.py:46
  6.5 0.5 %collective-permute-start.5 = (bf16[256,256]{1,0:T(8,128)(2,1)S(1)}, bf16[256,256]{1,0:T(8,128)(2,1)S(1)}, u32[]{:S(2)}, u32[]{:S(2)}) collective-permute-start(bf16[256,256]{1,0:T(8,128)(2,1)S(1)} %collective-permute-done.3.refs_6_), channel_id=1, source_target_pairs={{0,1},{1,0},{2,3},{3,2},{4,5},{5,4},{6,7},{7,6},{8,16},{9,17},{10,... | collective-permute-start | bytes 393224 | tf_op jit(solution)/shard_map/ppermute | solution.py:46
  7.0 1.9 %collective-permute-done.1.refs_4_ = bf16[256,256]{1,0:T(8,128)(2,1)S(1)} collective-permute-done((bf16[256,256]{1,0:T(8,128)(2,1)}, bf16[256,256]{1,0:T(8,128)(2,1)S(1)}, u32[]{:S(2)}, u32[]{:S(2)}) %collective-permute-start.1) | collective-permute-done | bytes 131104 | tf_op jit(solution)/shard_map/ppermute | solution.py:46
  8.9 0.5 %collective-permute-start.8 = (bf16[256,256]{1,0:T(8,128)(2,1)S(1)}, bf16[256,256]{1,0:T(8,128)(2,1)S(1)}, u32[]{:S(2)}, u32[]{:S(2)}) collective-permute-start(bf16[256,256]{1,0:T(8,128)(2,1)S(1)} %collective-permute-done.6.refs_3_), channel_id=1, source_target_pairs={{0,1},{1,0},{2,3},{3,2},{4,5},{5,4},{6,7},{7,6},{8,16},{9,17},{10,... | collective-permute-start | bytes 393224 | tf_op jit(solution)/shard_map/ppermute | solution.py:46
  9.5 0.1 collective-permute-start.9
  9.5 2.1 %attend_next.1 = (f32[1024,128]{1,0:T(8,128)S(1)}, f32[1024,128]{1,0:T(8,128)S(1)}, f32[1024,128]{1,0:T(8,128)S(1)}, bf16[512,5376]{1,0:T(8,128)(2,1)S(1)}) custom-call(bf16[256,512]{1,0:T(8,128)(2,1)S(1)} %get-tuple-element.40.queries, f32[16,256]{1,0:T(8,128)S(1)} %get-tuple-element.41.open_beside, ...), custom_call_target="tpu_custom_call", output_to_operand_aliasing={{3}: (3, {})} | custom-call | flops 402653184 | bytes 5505024 | tf_op jit(solution)/shard_map/attend_next/pallas_call | solution.py:232
  11.6 0.6 %attend_middle.1 = (f32[1024,128]{1,0:T(8,128)S(1)}, f32[1024,128]{1,0:T(8,128)S(1)}, f32[1024,128]{1,0:T(8,128)S(1)}) custom-call(bf16[256,512]{1,0:T(8,128)(2,1)S(1)} %get-tuple-element.40.queries, f32[1024,128]{1,0:T(8,128)S(1)} %get-tuple-element.49.refs_0_, f32[1024,128]{1,0:T(8,128)S(1)} %get-tuple-element.50.refs_1_, ...), custom_call_target="tpu_custom_call" | custom-call | flops 134217728 | tf_op jit(solution)/shard_map/attend_middle/pallas_call | solution.py:258
  12.3 1.0 %attend_last.1 = (bf16[128,512]{1,0:T(8,128)(2,1)S(1)}, bf16[128,512]{1,0:T(8,128)(2,1)S(1)}, f32[64,1536]{1,0:T(8,128)S(1)}, bf16[64,1536]{1,0:T(8,128)(2,1)S(1)}) custom-call(bf16[256,512]{1,0:T(8,128)(2,1)S(1)} %get-tuple-element.40.queries, bf16[512,5376]{1,0:T(8,128)(2,1)S(1)} %get-tuple-element.48.weight, f32[1024,128]{1,0:T(8,128)S(1)} %get-tuple-element.55.refs_0_, ...), custom_call_target="tpu_custom_call" | custom-call | flops 134217728 | tf_op jit(solution)/shard_map/attend_last/pallas_call | solution.py:294
  13.3 0.5 %collective-permute-start.10 = (bf16[64,1536]{1,0:T(8,128)(2,1)S(1)}, bf16[64,1536]{1,0:T(8,128)(2,1)S(1)}, u32[]{:S(2)}, u32[]{:S(2)}) collective-permute-start(bf16[64,1536]{1,0:T(8,128)(2,1)S(1)} %get-tuple-element.63), channel_id=1, source_target_pairs={{0,1},{1,0},{2,3},{3,2},{4,5},{5,4},{6,7},{7,6},{8,9},{9,8},{10,11... | collective-permute-start | bytes 589832 | tf_op jit(solution)/shard_map/ppermute | solution.py:22
  13.9 0.7 %project.2 = (f32[64,3840]{1,0:T(8,128)S(1)}, bf16[64,3840]{1,0:T(8,128)(2,1)S(1)}) custom-call(bf16[128,512]{1,0:T(8,128)(2,1)S(1)} %get-tuple-element.60.rows, bf16[512,5376]{1,0:T(8,128)(2,1)S(1)} %get-tuple-element.48.weight), custom_call_target="tpu_custom_call" | custom-call | flops 503316480 | tf_op jit(solution)/shard_map/project/pallas_call | solution.py:329
  14.5 0.4 collective-permute-done.10.theirs
  15.0 0.4 %collective-permute-start.11 = (bf16[64,3840]{1,0:T(8,128)(2,1)S(1)}, bf16[64,3840]{1,0:T(8,128)(2,1)S(1)}, u32[]{:S(2)}, u32[]{:S(2)}) collective-permute-start(bf16[64,3840]{1,0:T(8,128)(2,1)S(1)} %get-tuple-element.66), channel_id=1, source_target_pairs={{0,1},{1,0},{2,3},{3,2},{4,5},{5,4},{6,7},{7,6},{8,9},{9,8},{10,11... | collective-permute-start | bytes 1474568 | tf_op jit(solution)/shard_map/ppermute | solution.py:22
  15.4 1.5 %collective-permute-start.15 = (bf16[64,1536]{1,0:T(8,128)(2,1)S(1)}, bf16[64,1536]{1,0:T(8,128)(2,1)S(1)}, u32[]{:S(2)}, u32[]{:S(2)}) collective-permute-start(bf16[64,1536]{1,0:T(8,128)(2,1)S(1)} %add_up.2), channel_id=1, source_target_pairs={{0,2},{1,3},{2,0},{3,1},{4,6},{5,7},{6,4},{7,5},{8,10},{9,11},{10,... | collective-permute-start | bytes 589832 | tf_op jit(solution)/shard_map/ppermute | solution.py:22
  16.9 0.1 add_up.3
  17.0 1.6 %collective-permute-start.12 = (bf16[64,3200]{1,0:T(8,128)(2,1)S(1)}, bf16[64,3200]{1,0:T(8,128)(2,1)S(1)}, u32[]{:S(2)}, u32[]{:S(2)}) collective-permute-start(bf16[64,3200]{1,0:T(8,128)(2,1)S(1)} %get-tuple-element.67), channel_id=1, source_target_pairs={{0,2},{1,3},{2,0},{3,1},{4,6},{5,7},{6,4},{7,5},{8,10},{9,11},{10,... | collective-permute-start | bytes 1228808 | tf_op jit(solution)/shard_map/ppermute | solution.py:22
  18.6 0.9 %project.3 = (f32[64,5376]{1,0:T(8,128)S(1)}, bf16[64,2688]{1,0:T(8,128)(2,1)S(1)}, bf16[64,2688]{1,0:T(8,128)(2,1)S(1)}) custom-call(bf16[128,512]{1,0:T(8,128)(2,1)S(1)} %get-tuple-element.68.rows, bf16[512,5376]{1,0:T(8,128)(2,1)S(1)} %get-tuple-element.48.weight), custom_call_target="tpu_custom_call" | custom-call | flops 704643072 | tf_op jit(solution)/shard_map/project/pallas_call | solution.py:329
  19.5 0.1 collective-permute-start.18
  19.6 0.4 %collective-permute-start.19 = (bf16[64,2688]{1,0:T(8,128)(2,1)S(1)}, bf16[64,2688]{1,0:T(8,128)(2,1)S(1)}, u32[]{:S(2)}, u32[]{:S(2)}) collective-permute-start(bf16[64,2688]{1,0:T(8,128)(2,1)S(1)} %get-tuple-element.74), channel_id=1, source_target_pairs={{0,1},{1,0},{2,3},{3,2},{4,5},{5,4},{6,7},{7,6},{8,9},{9,8},{10,11... | collective-permute-start | bytes 1032200 | tf_op jit(solution)/shard_map/ppermute | solution.py:22
  20.1 8.5 %collective-permute-start.14 = (bf16[64,640]{1,0:T(8,128)(2,1)S(1)}, bf16[64,640]{1,0:T(8,128)(2,1)S(1)}, u32[]{:S(2)}, u32[]{:S(2)}) collective-permute-start(bf16[64,640]{1,0:T(8,128)(2,1)S(1)} %get-tuple-element.71), channel_id=1, source_target_pairs={{0,1},{1,0},{2,3},{3,2},{4,5},{5,4},{6,7},{7,6},{8,9},{9,8},{10,11... | collective-permute-start | bytes 245768 | tf_op jit(solution)/shard_map/ppermute | solution.py:46
  28.6 2.7 %collective-permute-done.14 = bf16[64,640]{1,0:T(8,128)(2,1)S(1)} collective-permute-done((bf16[64,640]{1,0:T(8,128)(2,1)S(1)}, bf16[64,640]{1,0:T(8,128)(2,1)S(1)}, u32[]{:S(2)}, u32[]{:S(2)}) %collective-permute-start.14) | collective-permute-done | bytes 81952 | tf_op jit(solution)/shard_map/ppermute | solution.py:46
  31.2 0.6 %collective-permute-start.16 = (bf16[64,640]{1,0:T(8,128)(2,1)S(1)}, bf16[64,640]{1,0:T(8,128)(2,1)S(1)}, u32[]{:S(2)}, u32[]{:S(2)}) collective-permute-start(bf16[64,640]{1,0:T(8,128)(2,1)S(1)} %collective-permute-done.14), channel_id=1, source_target_pairs={{0,1},{1,0},{2,3},{3,2},{4,5},{5,4},{6,7},{7,6},{8,9},{9,8},{10,11... | collective-permute-start | bytes 245768 | tf_op jit(solution)/shard_map/ppermute | solution.py:46
  31.8 1.4 %collective-permute-start.13 = (bf16[64,640]{1,0:T(8,128)(2,1)S(1)}, bf16[64,640]{1,0:T(8,128)(2,1)S(1)}, u32[]{:S(2)}, u32[]{:S(2)}) collective-permute-start(bf16[64,640]{1,0:T(8,128)(2,1)S(1)} %get-tuple-element.71), channel_id=1, source_target_pairs={{0,2},{1,3},{2,0},{3,1},{4,6},{5,7},{6,4},{7,5},{8,10},{9,11},{10,... | collective-permute-start | bytes 245768 | tf_op jit(solution)/shard_map/ppermute | solution.py:46
  33.3 2.8 %collective-permute-done.16 = bf16[64,640]{1,0:T(8,128)(2,1)S(1)} collective-permute-done((bf16[64,640]{1,0:T(8,128)(2,1)S(1)}, bf16[64,640]{1,0:T(8,128)(2,1)S(1)}, u32[]{:S(2)}, u32[]{:S(2)}) %collective-permute-start.16) | collective-permute-done | bytes 81952 | tf_op jit(solution)/shard_map/ppermute | solution.py:46
  36.0 0.7 %combine.2.refs_6_ = bf16[64,5376]{1,0:T(8,128)(2,1)} custom-call(f32[64,5376]{1,0:T(8,128)S(1)} %get-tuple-element.69.refs_0_, bf16[64,1536]{1,0:T(8,128)(2,1)S(1)} %collective-permute-done.15.refs_1_, bf16[64,2688]{1,0:T(8,128)(2,1)S(1)} %collective-permute-done.18.refs_2_.refs_4_, bf16[64,2688]{1,0:T(8,128)(2,1)S(1)} %collective-permute-done.19.refs_3_.refs_5_), custom_call_target="tpu_custom_call" | custom-call | tf_op jit(solution)/shard_map/combine/pallas_call | solution.py:398
  36.8 0.1 collective-permute-done.13.refs_2_
  36.9 3.6 %collective-permute-done.17.refs_3_ = bf16[64,640]{1,0:T(8,128)(2,1)S(1)} collective-permute-done((bf16[64,640]{1,0:T(8,128)(2,1)S(1)}, bf16[64,640]{1,0:T(8,128)(2,1)S(1)}, u32[]{:S(2)}, u32[]{:S(2)}) %collective-permute-start.17) | collective-permute-done | bytes 81952 | tf_op jit(solution)/shard_map/ppermute | solution.py:46
  40.5 0.9 %combine.3 = bf16[64,5376]{1,0:T(8,128)(2,1)} custom-call(f32[64,5376]{1,0:T(8,128)S(1)} %get-tuple-element.69.refs_0_, bf16[64,3200]{1,0:T(8,128)(2,1)S(1)} %collective-permute-done.12.refs_1_, bf16[64,640]{1,0:T(8,128)(2,1)S(1)} %collective-permute-done.13.refs_2_, ...), custom_call_target="tpu_custom_call", output_to_operand_aliasing={{}: (6, {})} | custom-call | tf_op jit(solution)/shard_map/combine/pallas_call | solution.py:398
  (18 shorter events, 0.1 us)
Async XLA Ops:
  0.0 4.0 %collective-permute-start.2 = (bf16[256,256]{1,0:T(8,128)(2,1)}, bf16[256,256]{1,0:T(8,128)(2,1)S(1)}, u32[]{:S(2)}, u32[]{:S(2)}) collective-permute-start(bf16[256,256]{1,0:T(8,128)(2,1)} %keys_in.1), channel_id=1, source_target_pairs={{0,8},{1,9},{2,10},{3,11},{4,12},{5,13},{6,14},{7,15},{8,16},{9,17... | collective-permute-start | bytes 393224 | tf_op jit(solution)/shard_map/ppermute | solution.py:46
  0.0 6.5 %collective-permute-start = (bf16[256,256]{1,0:T(8,128)(2,1)}, bf16[256,256]{1,0:T(8,128)(2,1)S(1)}, u32[]{:S(2)}, u32[]{:S(2)}) collective-permute-start(bf16[256,256]{1,0:T(8,128)(2,1)} %keys_in.1), channel_id=1, source_target_pairs={{0,4},{1,5},{2,6},{3,7},{4,0},{5,1},{6,2},{7,3},{8,12},{9,13},{10,... | collective-permute-start | bytes 393224 | tf_op jit(solution)/shard_map/ppermute | solution.py:46
  1.5 5.0 %collective-permute-start.3 = (bf16[256,256]{1,0:T(8,128)(2,1)}, bf16[256,256]{1,0:T(8,128)(2,1)S(1)}, u32[]{:S(2)}, u32[]{:S(2)}) collective-permute-start(bf16[256,256]{1,0:T(8,128)(2,1)} %values_in.1), channel_id=1, source_target_pairs={{0,8},{1,9},{2,10},{3,11},{4,12},{5,13},{6,14},{7,15},{8,16},{9,17... | collective-permute-start | bytes 393224 | tf_op jit(solution)/shard_map/ppermute | solution.py:46
  1.8 7.2 %collective-permute-start.1 = (bf16[256,256]{1,0:T(8,128)(2,1)}, bf16[256,256]{1,0:T(8,128)(2,1)S(1)}, u32[]{:S(2)}, u32[]{:S(2)}) collective-permute-start(bf16[256,256]{1,0:T(8,128)(2,1)} %values_in.1), channel_id=1, source_target_pairs={{0,4},{1,5},{2,6},{3,7},{4,0},{5,1},{6,2},{7,3},{8,12},{9,13},{10,... | collective-permute-start | bytes 393224 | tf_op jit(solution)/shard_map/ppermute | solution.py:46
  4.0 4.9 %collective-permute-start.4 = (bf16[256,256]{1,0:T(8,128)(2,1)S(1)}, bf16[256,256]{1,0:T(8,128)(2,1)S(1)}, u32[]{:S(2)}, u32[]{:S(2)}) collective-permute-start(bf16[256,256]{1,0:T(8,128)(2,1)S(1)} %collective-permute-done.2.refs_5_), channel_id=1, source_target_pairs={{0,1},{1,0},{2,3},{3,2},{4,5},{5,4},{6,7},{7,6},{8,16},{9,17},{10,... | collective-permute-start | bytes 393224 | tf_op jit(solution)/shard_map/ppermute | solution.py:46
  6.5 2.4 %collective-permute-start.6 = (bf16[256,256]{1,0:T(8,128)(2,1)S(1)}, bf16[256,256]{1,0:T(8,128)(2,1)S(1)}, u32[]{:S(2)}, u32[]{:S(2)}) collective-permute-start(bf16[256,256]{1,0:T(8,128)(2,1)S(1)} %collective-permute-done.2.refs_5_), channel_id=1, source_target_pairs={{0,1},{1,0},{2,3},{3,2},{4,5},{5,4},{6,7},{7,6},{8,12},{9,13},{10,... | collective-permute-start | bytes 393224 | tf_op jit(solution)/shard_map/ppermute | solution.py:46
  6.5 2.9 %collective-permute-start.5 = (bf16[256,256]{1,0:T(8,128)(2,1)S(1)}, bf16[256,256]{1,0:T(8,128)(2,1)S(1)}, u32[]{:S(2)}, u32[]{:S(2)}) collective-permute-start(bf16[256,256]{1,0:T(8,128)(2,1)S(1)} %collective-permute-done.3.refs_6_), channel_id=1, source_target_pairs={{0,1},{1,0},{2,3},{3,2},{4,5},{5,4},{6,7},{7,6},{8,16},{9,17},{10,... | collective-permute-start | bytes 393224 | tf_op jit(solution)/shard_map/ppermute | solution.py:46
  8.9 2.7 %collective-permute-start.7 = (bf16[256,256]{1,0:T(8,128)(2,1)S(1)}, bf16[256,256]{1,0:T(8,128)(2,1)S(1)}, u32[]{:S(2)}, u32[]{:S(2)}) collective-permute-start(bf16[256,256]{1,0:T(8,128)(2,1)S(1)} %collective-permute-done.3.refs_6_), channel_id=1, source_target_pairs={{0,1},{1,0},{2,3},{3,2},{4,5},{5,4},{6,7},{7,6},{8,12},{9,13},{10,... | collective-permute-start | bytes 393224 | tf_op jit(solution)/shard_map/ppermute | solution.py:46
  8.9 3.3 %collective-permute-start.8 = (bf16[256,256]{1,0:T(8,128)(2,1)S(1)}, bf16[256,256]{1,0:T(8,128)(2,1)S(1)}, u32[]{:S(2)}, u32[]{:S(2)}) collective-permute-start(bf16[256,256]{1,0:T(8,128)(2,1)S(1)} %collective-permute-done.6.refs_3_), channel_id=1, source_target_pairs={{0,1},{1,0},{2,3},{3,2},{4,5},{5,4},{6,7},{7,6},{8,16},{9,17},{10,... | collective-permute-start | bytes 393224 | tf_op jit(solution)/shard_map/ppermute | solution.py:46
  9.5 2.8 %collective-permute-start.9 = (bf16[256,256]{1,0:T(8,128)(2,1)S(1)}, bf16[256,256]{1,0:T(8,128)(2,1)S(1)}, u32[]{:S(2)}, u32[]{:S(2)}) collective-permute-start(bf16[256,256]{1,0:T(8,128)(2,1)S(1)} %collective-permute-done.5.refs_8_), channel_id=1, source_target_pairs={{0,1},{1,0},{2,3},{3,2},{4,5},{5,4},{6,7},{7,6},{8,9},{9,8},{10,11... | collective-permute-start | bytes 393224 | tf_op jit(solution)/shard_map/ppermute | solution.py:46
  13.3 1.6 %collective-permute-start.10 = (bf16[64,1536]{1,0:T(8,128)(2,1)S(1)}, bf16[64,1536]{1,0:T(8,128)(2,1)S(1)}, u32[]{:S(2)}, u32[]{:S(2)}) collective-permute-start(bf16[64,1536]{1,0:T(8,128)(2,1)S(1)} %get-tuple-element.63), channel_id=1, source_target_pairs={{0,1},{1,0},{2,3},{3,2},{4,5},{5,4},{6,7},{7,6},{8,9},{9,8},{10,11... | collective-permute-start | bytes 589832 | tf_op jit(solution)/shard_map/ppermute | solution.py:22
  15.0 1.9 %collective-permute-start.11 = (bf16[64,3840]{1,0:T(8,128)(2,1)S(1)}, bf16[64,3840]{1,0:T(8,128)(2,1)S(1)}, u32[]{:S(2)}, u32[]{:S(2)}) collective-permute-start(bf16[64,3840]{1,0:T(8,128)(2,1)S(1)} %get-tuple-element.66), channel_id=1, source_target_pairs={{0,1},{1,0},{2,3},{3,2},{4,5},{5,4},{6,7},{7,6},{8,9},{9,8},{10,11... | collective-permute-start | bytes 1474568 | tf_op jit(solution)/shard_map/ppermute | solution.py:22
  15.4 13.2 %collective-permute-start.15 = (bf16[64,1536]{1,0:T(8,128)(2,1)S(1)}, bf16[64,1536]{1,0:T(8,128)(2,1)S(1)}, u32[]{:S(2)}, u32[]{:S(2)}) collective-permute-start(bf16[64,1536]{1,0:T(8,128)(2,1)S(1)} %add_up.2), channel_id=1, source_target_pairs={{0,2},{1,3},{2,0},{3,1},{4,6},{5,7},{6,4},{7,5},{8,10},{9,11},{10,... | collective-permute-start | bytes 589832 | tf_op jit(solution)/shard_map/ppermute | solution.py:22
  17.0 23.5 %collective-permute-start.12 = (bf16[64,3200]{1,0:T(8,128)(2,1)S(1)}, bf16[64,3200]{1,0:T(8,128)(2,1)S(1)}, u32[]{:S(2)}, u32[]{:S(2)}) collective-permute-start(bf16[64,3200]{1,0:T(8,128)(2,1)S(1)} %get-tuple-element.67), channel_id=1, source_target_pairs={{0,2},{1,3},{2,0},{3,1},{4,6},{5,7},{6,4},{7,5},{8,10},{9,11},{10,... | collective-permute-start | bytes 1228808 | tf_op jit(solution)/shard_map/ppermute | solution.py:22
  19.5 16.6 %collective-permute-start.18 = (bf16[64,2688]{1,0:T(8,128)(2,1)S(1)}, bf16[64,2688]{1,0:T(8,128)(2,1)S(1)}, u32[]{:S(2)}, u32[]{:S(2)}) collective-permute-start(bf16[64,2688]{1,0:T(8,128)(2,1)S(1)} %get-tuple-element.73), channel_id=1, source_target_pairs={{0,1},{1,0},{2,3},{3,2},{4,5},{5,4},{6,7},{7,6},{8,9},{9,8},{10,11... | collective-permute-start | bytes 1032200 | tf_op jit(solution)/shard_map/ppermute | solution.py:22
  19.6 16.4 %collective-permute-start.19 = (bf16[64,2688]{1,0:T(8,128)(2,1)S(1)}, bf16[64,2688]{1,0:T(8,128)(2,1)S(1)}, u32[]{:S(2)}, u32[]{:S(2)}) collective-permute-start(bf16[64,2688]{1,0:T(8,128)(2,1)S(1)} %get-tuple-element.74), channel_id=1, source_target_pairs={{0,1},{1,0},{2,3},{3,2},{4,5},{5,4},{6,7},{7,6},{8,9},{9,8},{10,11... | collective-permute-start | bytes 1032200 | tf_op jit(solution)/shard_map/ppermute | solution.py:22
  20.1 11.2 %collective-permute-start.14 = (bf16[64,640]{1,0:T(8,128)(2,1)S(1)}, bf16[64,640]{1,0:T(8,128)(2,1)S(1)}, u32[]{:S(2)}, u32[]{:S(2)}) collective-permute-start(bf16[64,640]{1,0:T(8,128)(2,1)S(1)} %get-tuple-element.71), channel_id=1, source_target_pairs={{0,1},{1,0},{2,3},{3,2},{4,5},{5,4},{6,7},{7,6},{8,9},{9,8},{10,11... | collective-permute-start | bytes 245768 | tf_op jit(solution)/shard_map/ppermute | solution.py:46
  31.2 4.8 %collective-permute-start.16 = (bf16[64,640]{1,0:T(8,128)(2,1)S(1)}, bf16[64,640]{1,0:T(8,128)(2,1)S(1)}, u32[]{:S(2)}, u32[]{:S(2)}) collective-permute-start(bf16[64,640]{1,0:T(8,128)(2,1)S(1)} %collective-permute-done.14), channel_id=1, source_target_pairs={{0,1},{1,0},{2,3},{3,2},{4,5},{5,4},{6,7},{7,6},{8,9},{9,8},{10,11... | collective-permute-start | bytes 245768 | tf_op jit(solution)/shard_map/ppermute | solution.py:46
  31.8 5.1 %collective-permute-start.13 = (bf16[64,640]{1,0:T(8,128)(2,1)S(1)}, bf16[64,640]{1,0:T(8,128)(2,1)S(1)}, u32[]{:S(2)}, u32[]{:S(2)}) collective-permute-start(bf16[64,640]{1,0:T(8,128)(2,1)S(1)} %get-tuple-element.71), channel_id=1, source_target_pairs={{0,2},{1,3},{2,0},{3,1},{4,6},{5,7},{6,4},{7,5},{8,10},{9,11},{10,... | collective-permute-start | bytes 245768 | tf_op jit(solution)/shard_map/ppermute | solution.py:46
  36.0 4.4 %collective-permute-start.17 = (bf16[64,640]{1,0:T(8,128)(2,1)S(1)}, bf16[64,640]{1,0:T(8,128)(2,1)S(1)}, u32[]{:S(2)}, u32[]{:S(2)}) collective-permute-start(bf16[64,640]{1,0:T(8,128)(2,1)S(1)} %collective-permute-done.16), channel_id=1, source_target_pairs={{0,1},{1,0},{2,3},{3,2},{4,5},{5,4},{6,7},{7,6},{8,9},{9,8},{10,11... | collective-permute-start | bytes 245768 | tf_op jit(solution)/shard_map/ppermute | solution.py:46
